TPU v7x, 32 devices: a whole 2x2x4 slice. The times are simulated.
32 devices in a mesh: section: 2 (over x), seq: 2 (over y), fsdp: 8 (over z, core).
Axes of the slice: x: 2, y: 2, z: 4, core: 2. Of those that a mesh axis runs over, the one named last changes fastest.
Arguments:
- tokens: bfloat16 [8, 2, 512, 1024], P('fsdp', None, 'seq'), may hold values from -6 to 6
- cotangent: bfloat16 [8, 2, 512, 1024], P('fsdp', None, 'seq'), may hold values from -6 to 6
- norm_gains: float32 [2, 2, 1024], P('section'), may hold values from 0.5 to 1.5
- head_gains: float32 [2, 64], replicated, may hold values from 0.5 to 1.5
- conv_kernel: float32 [3, 1024], replicated, may hold values from -0.1 to 0.1
- mix_in: bfloat16 [2, 1024, 2048], P('section', 'fsdp'), may hold values from -0.1875 to 0.1875
- mix_out: bfloat16 [2, 1024, 1024], P('section', 'fsdp'), may hold values from -2 to 2
- w_gate: bfloat16 [2, 1024, 4608], P('section', 'fsdp'), may hold values from -0.1875 to 0.1875
- w_up: bfloat16 [2, 1024, 4608], P('section', 'fsdp'), may hold values from -0.1875 to 0.1875
- w_down: bfloat16 [2, 4608, 1024], P('section', 'fsdp'), may hold values from -0.09375 to 0.09375
- conv_c: bfloat16 [1024, 1024], P(('section', 'fsdp')), may hold values from -0.1875 to 0.1875
Outputs:
- ends: float32 [2, 8, 2, 512, 1024], P('section', 'fsdp', None, 'seq')
- grad_norm_gains: float32 [2, 2, 1024], replicated
- grad_head_gains: float32 [2, 64], replicated
- grad_conv_kernel: float32 [3, 1024], replicated
- grad_mix_in: float32 [2, 1024, 2048], P('section', ('seq', 'fsdp'))
- grad_mix_out: float32 [2, 1024, 1024], P('section', ('seq', 'fsdp'))
- grad_w_gate: float32 [2, 1024, 4608], P('section', ('seq', 'fsdp'))
- grad_w_up: float32 [2, 1024, 4608], P('section', ('seq', 'fsdp'))
- grad_w_down: float32 [2, 4608, 1024], P('section', ('seq', 'fsdp'))
- grad_conv_c: float32 [1024, 1024], P(('section', 'seq', 'fsdp'))
All inputs are finite; a program needn't handle non-finite values.
Results may differ from a plain program's by a relative error of at most 0.025.
Values may be sent and summed in bfloat16 or wider, within the bound.
No kernel may reach another device: no remote copies, remote signals or barrier semaphores. Data moves between devices by JAX's collectives and lax.ppermute only.
A program may use at most 448 MiB of HBM per device.

v0:
```python
import jax
import jax.numpy as jnp
from jax import lax
from jax.sharding import PartitionSpec as P

HEADS = 16
KV_HEADS = 8
HEAD = 64


EPSILON = 1e-05
THETA = 1000000.0
NEGATIVE = -1e30


def shifted(value, axis, steps):
    count = lax.axis_size(axis)
    leading, last = (max(0, -steps), min(count, count - steps))
    return lax.ppermute(value, axis, [(source, source + steps) for source in range(leading, last)])


def rms_scale(value):
    return lax.rsqrt(jnp.mean(value * value, axis=-1, keepdims=True) + EPSILON)


def norm_back(grad_out, value, scale, gain):
    inner = grad_out * gain
    return scale * (inner - value * scale * scale * jnp.mean(inner * value, axis=-1, keepdims=True))


def matmul(left, right):
    return jnp.dot(left, right, preferred_element_type=jnp.float32)


def matmul_t(left, right):
    return lax.dot_general(
        left, right, (((1,), (1,)), ((), ())), preferred_element_type=jnp.float32
    )


def outer_sum(left, right):
    return lax.dot_general(
        left, right, (((0,), (0,)), ((), ())), preferred_element_type=jnp.float32
    )


def rope_tables(positions, width):
    half = width // 2
    frequency = THETA ** (-jnp.arange(half, dtype=jnp.float32) * 2.0 / width)
    angle = positions.astype(jnp.float32)[:, None] * frequency[None, :]
    return (jnp.cos(angle), jnp.sin(angle))


def rotate(value, cosine, sine):
    half = value.shape[-1] // 2
    first, second = (value[..., :half], value[..., half:])
    return jnp.concatenate(
        [first * cosine - second * sine, second * cosine + first * sine], axis=-1
    )


def rotate_back(grad, cosine, sine):
    half = grad.shape[-1] // 2
    first, second = (grad[..., :half], grad[..., half:])
    return jnp.concatenate(
        [first * cosine + second * sine, second * cosine - first * sine], axis=-1
    )


def write_rows(buffer, values, start, valid):
    old = lax.dynamic_slice_in_dim(buffer, start, values.shape[0], 0)
    return lax.dynamic_update_slice_in_dim(buffer, jnp.where(valid, values, old), start, 0)


def write_stretch(buffer, value, stretch, valid):
    return write_rows(buffer, value[None], stretch, valid)


def read_stretch(buffer, stretch):
    return lax.dynamic_index_in_dim(buffer, stretch, 0, keepdims=False)


def local(
    tokens,
    cotangent,
    norm_gains,
    head_gains,
    conv_kernel,
    mix_in,
    mix_out,
    w_gate,
    w_up,
    w_down,
    conv_c,
):
    section_index = lax.axis_index("section")
    first = section_index == 0
    sections = lax.axis_size("section")
    seq_count = lax.axis_size("seq")
    stretches = tokens.shape[1]
    rows = tokens.shape[2]
    width = tokens.shape[3]
    hidden_width = w_gate.shape[2]
    block = rows * seq_count
    length = block * stretches
    heads_per = HEADS // KV_HEADS
    group_width = (heads_per + 2) * HEAD
    channels = group_width // 2
    lanes = width // seq_count
    gains = norm_gains[0]
    lane_start = lax.axis_index("seq") * lanes
    kernel_part = lax.dynamic_slice_in_dim(conv_kernel, lane_start, lanes, 1)
    full_c = lax.all_gather(conv_c, ("section", "fsdp"), axis=0, tiled=True)
    gathered = (
        lax.all_gather(mix_in, "fsdp", axis=1, tiled=True),
        lax.all_gather(mix_out, "fsdp", axis=1, tiled=True),
        lax.all_gather(w_gate, "fsdp", axis=1, tiled=True),
        lax.all_gather(w_up, "fsdp", axis=1, tiled=True),
        lax.all_gather(w_down, "fsdp", axis=1, tiled=True),
    )
    proj_in, proj_out, gate_full, up_full, down_full = [piece[0] for piece in gathered]

    def split_heads(pack):
        count = pack.shape[0]
        grouped = pack.reshape(count, -1, group_width)
        query = grouped[:, :, : heads_per * HEAD].reshape(count, -1, heads_per, HEAD)
        keys = grouped[:, :, heads_per * HEAD : (heads_per + 1) * HEAD]
        values = grouped[:, :, (heads_per + 1) * HEAD :]
        return (query, keys, values)

    def keys_of(packbuf, small_gains):
        unused, keys, values = split_heads(packbuf)
        keys = keys.astype(jnp.float32)
        cosine, sine = rope_tables(jnp.arange(length), HEAD)
        rotated = rotate(keys * rms_scale(keys) * small_gains[1], cosine[:, None], sine[:, None])
        return (rotated.astype(jnp.bfloat16), values)

    def queries_of(packbuf, start, small_gains):
        part = lax.dynamic_slice_in_dim(packbuf, start, block, 0)
        query, keys, unused = split_heads(part)
        query = query.astype(jnp.float32)
        keys = keys.astype(jnp.float32)
        cosine, sine = rope_tables(start + jnp.arange(block), HEAD)
        query_scale = rms_scale(query)
        rotated = rotate(
            query * query_scale * small_gains[0], cosine[:, None, None], sine[:, None, None]
        )
        return (
            rotated.astype(jnp.bfloat16),
            query,
            query_scale,
            keys,
            rms_scale(keys),
            cosine,
            sine,
        )

    def scores_of(query_rot, key_rot, start):
        scores = jnp.einsum(
            "tgjd,sgd->gjts", query_rot, key_rot, preferred_element_type=jnp.float32
        ) * HEAD ** (-0.5)
        allowed = (start + jnp.arange(block))[:, None] >= jnp.arange(length)[None, :]
        return jnp.where(allowed, scores, NEGATIVE)

    def conv_parts(packbuf):
        grouped = packbuf.reshape(length, -1, 2, channels)
        product = grouped[:, :, 0].reshape(length, lanes).astype(jnp.float32)
        gate = grouped[:, :, 1].reshape(length, lanes).astype(jnp.float32)
        return (product, gate)

    def conv_state(product, taps):
        once = jnp.concatenate([jnp.zeros_like(product[:1]), product[:-1]], axis=0)
        twice = jnp.concatenate([jnp.zeros_like(product[:2]), product[:-2]], axis=0)
        return (taps[0] * twice + taps[1] * once + taps[2] * product, once, twice)

    def attend_forward(packbuf, log_totals, start, valid, small_gains, taps):
        key_rot, values = keys_of(packbuf, small_gains)
        query_rot = queries_of(packbuf, start, small_gains)[0]
        scores = scores_of(query_rot, key_rot, start)
        top = jnp.max(scores, axis=-1, keepdims=True)
        exponent = jnp.exp(scores - top)
        total = jnp.sum(exponent, axis=-1, keepdims=True)
        probs = (exponent / total).astype(jnp.bfloat16)
        heads = jnp.einsum("gjts,sgd->tgjd", probs, values, preferred_element_type=jnp.float32)
        log_total = jnp.transpose((top + jnp.log(total))[..., 0], (2, 0, 1))
        return (heads.reshape(block, lanes), write_rows(log_totals, log_total, start, valid))

    def conv_forward(packbuf, log_totals, start, valid, small_gains, taps):
        product, gate = conv_parts(packbuf)
        state = conv_state(product, taps)[0]
        rows_state = lax.dynamic_slice_in_dim(state, start, block, 0)
        rows_gate = lax.dynamic_slice_in_dim(gate, start, block, 0)
        return (rows_gate * rows_state, log_totals)

    def attend_backward(
        packbuf,
        log_totals,
        back_sums,
        head_grad,
        kernel_grad,
        start,
        valid,
        grad_groups,
        small_gains,
        taps,
    ):
        key_rot, values = keys_of(packbuf, small_gains)
        query_rot, query, query_scale, keys, key_scale, cosine, sine = queries_of(
            packbuf, start, small_gains
        )
        scores = scores_of(query_rot, key_rot, start)
        log_total = lax.dynamic_slice_in_dim(log_totals, start, block, 0)
        probs = jnp.exp(scores - jnp.transpose(log_total, (1, 2, 0))[..., None])
        rounded = probs.astype(jnp.bfloat16)
        grad_heads = grad_groups.reshape(block, -1, heads_per, HEAD)
        grad_probs = jnp.einsum(
            "tgjd,sgd->gjts", grad_heads, values, preferred_element_type=jnp.float32
        )
        grad_scores = probs * (grad_probs - jnp.sum(probs * grad_probs, axis=-1, keepdims=True))
        grad_scores = grad_scores.astype(jnp.bfloat16)
        grad_values = jnp.einsum(
            "gjts,tgjd->sgd", rounded, grad_heads, preferred_element_type=jnp.float32
        )
        grad_keys = jnp.einsum(
            "gjts,tgjd->sgd", grad_scores, query_rot, preferred_element_type=jnp.float32
        ) * HEAD ** (-0.5)
        grad_query = jnp.einsum(
            "gjts,sgd->tgjd", grad_scores, key_rot, preferred_element_type=jnp.float32
        ) * HEAD ** (-0.5)
        contribution = jnp.concatenate([grad_keys, grad_values], axis=-1).reshape(length, lanes)
        back_sums = back_sums + jnp.where(valid, contribution, 0.0)
        own = lax.dynamic_slice_in_dim(back_sums, start, block, 0).reshape(block, -1, 2 * HEAD)
        query_normed = rotate_back(grad_query, cosine[:, None, None], sine[:, None, None])
        key_normed = rotate_back(own[..., :HEAD], cosine[:, None], sine[:, None])
        query_gain = jnp.sum(query_normed * query * query_scale, axis=(0, 1, 2))
        key_gain = jnp.sum(key_normed * keys * key_scale, axis=(0, 1))
        head_grad = head_grad + jnp.where(valid, jnp.stack([query_gain, key_gain]), 0.0)
        query_raw = norm_back(query_normed, query, query_scale, small_gains[0])
        key_raw = norm_back(key_normed, keys, key_scale, small_gains[1])
        grad_pack = jnp.concatenate(
            [query_raw.reshape(block, -1, heads_per * HEAD), key_raw, own[..., HEAD:]], axis=-1
        )
        return (grad_pack.reshape(block, -1), back_sums, head_grad, kernel_grad)

    def conv_backward(
        packbuf,
        log_totals,
        back_sums,
        head_grad,
        kernel_grad,
        start,
        valid,
        grad_groups,
        small_gains,
        taps,
    ):
        product, gate = conv_parts(packbuf)
        state, once, twice = conv_state(product, taps)
        rows_state = lax.dynamic_slice_in_dim(state, start, block, 0)
        rows_gate = lax.dynamic_slice_in_dim(gate, start, block, 0)
        grad_out = grad_groups.astype(jnp.float32)
        grad_gate = grad_out * rows_state
        grad_rows = jnp.where(valid, grad_out * rows_gate, 0.0)
        grad_state = lax.dynamic_update_slice_in_dim(jnp.zeros_like(product), grad_rows, start, 0)
        ahead = jnp.concatenate([grad_state[1:], jnp.zeros_like(grad_state[:1])], axis=0)
        further = jnp.concatenate([grad_state[2:], jnp.zeros_like(grad_state[:2])], axis=0)
        back_sums = back_sums + taps[2] * grad_state + taps[1] * ahead + taps[0] * further
        kernel_grad = kernel_grad + jnp.stack(
            [
                jnp.sum(grad_state * twice, axis=0),
                jnp.sum(grad_state * once, axis=0),
                jnp.sum(grad_state * product, axis=0),
            ]
        )
        own = lax.dynamic_slice_in_dim(back_sums, start, block, 0)
        grad_pack = jnp.stack(
            [own.reshape(block, -1, channels), grad_gate.reshape(block, -1, channels)], axis=2
        )
        return (grad_pack.reshape(block, -1), back_sums, head_grad, kernel_grad)

    def attention_pack(projected, normed, c_full):
        return projected.astype(jnp.bfloat16)

    def conv_pack(projected, normed, c_full):
        gate = matmul(normed, c_full)
        product = projected[:, :width] * projected[:, width:]
        stacked = jnp.stack(
            [product.reshape(rows, -1, channels), gate.reshape(rows, -1, channels)], axis=2
        )
        return stacked.reshape(rows, 2 * width).astype(jnp.bfloat16)

    def attention_unpack(grad_pack, projected, c_full):
        return (
            grad_pack,
            jnp.zeros((rows, width), jnp.bfloat16),
            jnp.zeros((rows, width), jnp.float32),
        )

    def conv_unpack(grad_pack, projected, c_full):
        grouped = grad_pack.reshape(rows, -1, 2, channels)
        grad_product = grouped[:, :, 0].reshape(rows, width).astype(jnp.float32)
        grad_gate = grouped[:, :, 1].reshape(rows, width)
        grad_proj = jnp.concatenate(
            [grad_product * projected[:, width:], grad_product * projected[:, :width]], axis=-1
        )
        return (grad_proj.astype(jnp.bfloat16), grad_gate, matmul_t(grad_gate, c_full))

    packbuf = jnp.zeros((length, 2 * lanes), jnp.bfloat16)
    log_totals = jnp.zeros((length, KV_HEADS // seq_count, heads_per), jnp.float32)
    received = jnp.zeros((rows, width), jnp.bfloat16)
    kept_inputs = jnp.zeros((stretches, rows, width), jnp.bfloat16)
    kept_projected = jnp.zeros((stretches, rows, 2 * width), jnp.float32)
    kept_returned = jnp.zeros((stretches, rows, width), jnp.bfloat16)
    kept_resid = jnp.zeros((stretches, rows, width), jnp.float32)
    kept_gate = jnp.zeros((stretches, rows, hidden_width), jnp.float32)
    kept_upward = jnp.zeros((stretches, rows, hidden_width), jnp.float32)
    outputs = jnp.zeros((stretches, rows, width), jnp.float32)
    for slot in range(stretches + sections - 1):
        raw = slot - section_index
        valid = jnp.logical_and(raw >= 0, raw < stretches)
        stretch = jnp.clip(raw, 0, stretches - 1)
        start = stretch * block
        source = jnp.where(first, read_stretch(tokens[0], stretch), received).astype(jnp.float32)
        normed = (source * rms_scale(source) * gains[0]).astype(jnp.bfloat16)
        projected = matmul(normed, proj_in)
        pack = lax.cond(first, attention_pack, conv_pack, projected, normed, full_c)
        arrived = lax.all_to_all(pack, "seq", split_axis=1, concat_axis=0, tiled=True)
        packbuf = write_rows(packbuf, arrived, start, valid)
        mixed, log_totals = lax.cond(
            first,
            attend_forward,
            conv_forward,
            packbuf,
            log_totals,
            start,
            valid,
            head_gains,
            kernel_part,
        )
        returned = lax.all_to_all(
            mixed.astype(jnp.bfloat16), "seq", split_axis=0, concat_axis=1, tiled=True
        )
        resid = source + matmul(returned, proj_out)
        normed_two = (resid * rms_scale(resid) * gains[1]).astype(jnp.bfloat16)
        gate = matmul(normed_two, gate_full)
        upward = matmul(normed_two, up_full)
        active = (jax.nn.silu(gate) * upward).astype(jnp.bfloat16)
        result = resid + matmul(active, down_full)
        kept_inputs = write_stretch(kept_inputs, source.astype(jnp.bfloat16), stretch, valid)
        kept_projected = write_stretch(kept_projected, projected, stretch, valid)
        kept_returned = write_stretch(kept_returned, returned, stretch, valid)
        kept_resid = write_stretch(kept_resid, resid, stretch, valid)
        kept_gate = write_stretch(kept_gate, gate, stretch, valid)
        kept_upward = write_stretch(kept_upward, upward, stretch, valid)
        outputs = write_stretch(outputs, result, stretch, valid)
        if slot < stretches:
            received = shifted(result.astype(jnp.bfloat16), "section", 1)
    back_weights = (proj_in, proj_out, gate_full, up_full, down_full)
    proj_in, proj_out, gate_full, up_full, down_full = back_weights
    back_sums = jnp.zeros((length, lanes), jnp.float32)
    head_grad = jnp.zeros((2, HEAD), jnp.float32)
    kernel_grad = jnp.zeros((3, lanes), jnp.float32)
    gain_grad = jnp.zeros((2, width), jnp.float32)
    grad_received = jnp.zeros((rows, width), jnp.bfloat16)
    input_grads = jnp.zeros((stretches, rows, width), jnp.float32)
    kept_dproj = jnp.zeros((stretches, rows, 2 * width), jnp.bfloat16)
    kept_dgate_c = jnp.zeros((stretches, rows, width), jnp.bfloat16)
    kept_dmix = jnp.zeros((stretches, rows, width), jnp.bfloat16)
    kept_dgate = jnp.zeros((stretches, rows, hidden_width), jnp.bfloat16)
    kept_dupward = jnp.zeros((stretches, rows, hidden_width), jnp.bfloat16)
    kept_dff = jnp.zeros((stretches, rows, width), jnp.bfloat16)
    for slot in range(stretches + sections - 1):
        raw = stretches - 1 - slot + sections - 1 - section_index
        valid = jnp.logical_and(raw >= 0, raw < stretches)
        stretch = jnp.clip(raw, 0, stretches - 1)
        start = stretch * block
        grad_result = jnp.where(first, grad_received, read_stretch(cotangent[0], stretch)).astype(
            jnp.float32
        )
        source = read_stretch(kept_inputs, stretch).astype(jnp.float32)
        scale_one = rms_scale(source)
        resid = read_stretch(kept_resid, stretch)
        scale_two = rms_scale(resid)
        gate = read_stretch(kept_gate, stretch)
        upward = read_stretch(kept_upward, stretch)
        grad_ff = grad_result.astype(jnp.bfloat16)
        grad_active = matmul_t(grad_ff, down_full)
        sigma = jax.nn.sigmoid(gate)
        grad_gate = (grad_active * upward * sigma * (1.0 + gate * (1.0 - sigma))).astype(
            jnp.bfloat16
        )
        grad_upward = (grad_active * gate * sigma).astype(jnp.bfloat16)
        grad_normed_two = matmul_t(grad_gate, gate_full) + matmul_t(grad_upward, up_full)
        gain_two = jnp.sum(grad_normed_two * resid * scale_two, axis=0)
        grad_resid = grad_result + norm_back(grad_normed_two, resid, scale_two, gains[1])
        grad_mix = grad_resid.astype(jnp.bfloat16)
        grad_returned = matmul_t(grad_mix, proj_out).astype(jnp.bfloat16)
        grad_groups = lax.all_to_all(grad_returned, "seq", split_axis=1, concat_axis=0, tiled=True)
        grad_pack_groups, back_sums, head_grad, kernel_grad = lax.cond(
            first,
            attend_backward,
            conv_backward,
            packbuf,
            log_totals,
            back_sums,
            head_grad,
            kernel_grad,
            start,
            valid,
            grad_groups,
            head_gains,
            kernel_part,
        )
        grad_pack = lax.all_to_all(
            grad_pack_groups.astype(jnp.bfloat16), "seq", split_axis=0, concat_axis=1, tiled=True
        )
        projected = read_stretch(kept_projected, stretch)
        grad_proj, grad_gate_c, extra = lax.cond(
            first, attention_unpack, conv_unpack, grad_pack, projected, full_c
        )
        grad_normed = matmul_t(grad_proj, proj_in) + extra
        gain_one = jnp.sum(grad_normed * source * scale_one, axis=0)
        gain_grad = gain_grad + jnp.where(valid, jnp.stack([gain_one, gain_two]), 0.0)
        grad_source = grad_resid + norm_back(grad_normed, source, scale_one, gains[0])
        input_grads = write_stretch(input_grads, grad_source, stretch, valid)
        kept_dproj = write_stretch(kept_dproj, grad_proj, stretch, valid)
        kept_dgate_c = write_stretch(kept_dgate_c, grad_gate_c, stretch, valid)
        kept_dmix = write_stretch(kept_dmix, grad_mix, stretch, valid)
        kept_dgate = write_stretch(kept_dgate, grad_gate, stretch, valid)
        kept_dupward = write_stretch(kept_dupward, grad_upward, stretch, valid)
        kept_dff = write_stretch(kept_dff, grad_ff, stretch, valid)
        if slot < stretches:
            grad_received = shifted(grad_source.astype(jnp.bfloat16), "section", -1)
    total_rows = stretches * rows
    inputs_all = kept_inputs.reshape(total_rows, width).astype(jnp.float32)
    normed_all = (inputs_all * rms_scale(inputs_all) * gains[0]).astype(jnp.bfloat16)
    resid_all = kept_resid.reshape(total_rows, width)
    normed_two_all = (resid_all * rms_scale(resid_all) * gains[1]).astype(jnp.bfloat16)
    gate_all = kept_gate.reshape(total_rows, hidden_width)
    active_all = (jax.nn.silu(gate_all) * kept_upward.reshape(total_rows, hidden_width)).astype(
        jnp.bfloat16
    )
    grads = (
        outer_sum(normed_all, kept_dproj.reshape(total_rows, 2 * width))[None],
        outer_sum(kept_returned.reshape(total_rows, width), kept_dmix.reshape(total_rows, width))[
            None
        ],
        outer_sum(normed_two_all, kept_dgate.reshape(total_rows, hidden_width))[None],
        outer_sum(normed_two_all, kept_dupward.reshape(total_rows, hidden_width))[None],
        outer_sum(active_all, kept_dff.reshape(total_rows, width))[None],
    )
    shards = (
        lax.psum_scatter(grads[0], ("seq", "fsdp"), scatter_dimension=1, tiled=True),
        lax.psum_scatter(grads[1], ("seq", "fsdp"), scatter_dimension=1, tiled=True),
        lax.psum_scatter(grads[2], ("seq", "fsdp"), scatter_dimension=1, tiled=True),
        lax.psum_scatter(grads[3], ("seq", "fsdp"), scatter_dimension=1, tiled=True),
        lax.psum_scatter(grads[4], ("seq", "fsdp"), scatter_dimension=1, tiled=True),
    )
    grad_c = lax.cond(
        first,
        lambda: jnp.zeros((width, width), jnp.float32),
        lambda: outer_sum(normed_all, kept_dgate_c.reshape(total_rows, width)),
    )
    c_shard = lax.psum_scatter(grad_c, ("section", "seq", "fsdp"), scatter_dimension=0, tiled=True)
    blank = jnp.zeros_like(gain_grad)
    norm_full = jnp.where(first, jnp.stack([gain_grad, blank]), jnp.stack([blank, gain_grad]))
    kernel_full = lax.dynamic_update_slice_in_dim(
        jnp.zeros((3, width), jnp.float32), kernel_grad, lane_start, 1
    )
    small = lax.psum((norm_full, head_grad, kernel_full), ("section", "seq", "fsdp"))
    ends = jnp.where(first, input_grads, outputs)[None, None]
    return (
        ends,
        small[0],
        small[1],
        small[2],
        shards[0],
        shards[1],
        shards[2],
        shards[3],
        shards[4],
        c_shard,
    )


def solution(mesh):
    return jax.shard_map(
        local,
        mesh=mesh,
        in_specs=(
            P("fsdp", None, "seq", None),
            P("fsdp", None, "seq", None),
            P("section", None, None),
            P(),
            P(),
            P("section", "fsdp", None),
            P("section", "fsdp", None),
            P("section", "fsdp", None),
            P("section", "fsdp", None),
            P("section", "fsdp", None),
            P(("section", "fsdp"), None),
        ),
        out_specs=(
            P("section", "fsdp", None, "seq", None),
            P(),
            P(),
            P(),
            P("section", ("seq", "fsdp"), None),
            P("section", ("seq", "fsdp"), None),
            P("section", ("seq", "fsdp"), None),
            P("section", ("seq", "fsdp"), None),
            P("section", ("seq", "fsdp"), None),
            P(("section", "seq", "fsdp"), None),
        ),
        check_vma=False,
    )
```

profile of v0, /device:TPU:0, one launch (start us, length us, event | category | flops | bytes accessed | tf_op | source)
XLA Modules:
  0.0 2028.7 jit_solution(9116756202644329447)
XLA Ops:
  11.6 47.9 %all-gather.7.cloned.1.call-done = bf16[1,1024,2048]{2,1,0:T(8,128)(2,1)} async-done(((bf16[1,128,2048]{2,1,0:T(8,128)(2,1)}), bf16[1,1024,2048]{2,1,0:T(8,128)(2,1)}) %all-gather.7.cloned.1.call-update) | async-done | bytes 4194320 | tf_op jit(solution)/shard_map/all_gather | solution.py:115
  66.6 35.3 %all-gather.9.cloned.1.call-done = bf16[1024,1024]{1,0:T(8,128)(2,1)} async-done(((bf16[64,1024]{1,0:T(8,128)(2,1)}), bf16[1024,1024]{1,0:T(8,128)(2,1)}) %all-gather.9.cloned.1.call-update) | async-done | bytes 2097168 | tf_op jit(solution)/shard_map/all_gather | solution.py:113
  108.5 14.2 all-to-all-done
  124.1 36.6 %conditional.14 = (bf16[512,512]{0,1:T(8,128)(2,1)S(1)}, f32[1024,4,2]{0,2,1:T(2,128)}) conditional(s32[]{:T(128)} %convert_element_type.562, (bf16[1024,1024]{1,0:T(8,128)(2,1)S(1)}, s32[]{:T(128)}, f32[3,512]{1,0:T(4,128)S(1)}) %tuple.138, (s32[]{:T(128)}, bf16[1024,1024]{1,0:T(8,128)(2,1)S(1)}, f32[2,64]{1,0:T(2,128)S(1)}, pred[]{:T(512)}) %tuple.391), branch_computations={%region_3.4_spmd, %region_4.9_spmd} | conditional | flops 1131997184 | bytes 77679600 | solution.py:329
  175.4 47.7 %all-gather.15.cloned.1.call-done = bf16[1,1024,4608]{2,1,0:T(8,128)(2,1)} async-done(((bf16[1,128,4608]{2,1,0:T(8,128)(2,1)}), bf16[1,1024,4608]{2,1,0:T(8,128)(2,1)}) %all-gather.15.cloned.1.call-update) | async-done | bytes 9437200 | tf_op jit(solution)/shard_map/all_gather | solution.py:118
  235.5 78.4 %all-gather.13.cloned.1.call-done = bf16[1,1024,4608]{2,1,0:T(8,128)(2,1)} async-done(((bf16[1,128,4608]{2,1,0:T(8,128)(2,1)}), bf16[1,1024,4608]{2,1,0:T(8,128)(2,1)}) %all-gather.13.cloned.1.call-update) | async-done | bytes 9437200 | tf_op jit(solution)/shard_map/all_gather | solution.py:117
  326.2 78.4 %all-gather.17.cloned.1.call-done = bf16[1,4608,1024]{2,1,0:T(8,128)(2,1)} async-done(((bf16[1,576,1024]{2,1,0:T(8,128)(2,1)}), bf16[1,4608,1024]{2,1,0:T(8,128)(2,1)}) %all-gather.17.cloned.1.call-update) | async-done | bytes 9437200 | tf_op jit(solution)/shard_map/all_gather | solution.py:119
  464.8 37.4 %conditional.16 = (bf16[512,512]{0,1:T(8,128)(2,1)}, f32[1024,4,2]{0,2,1:T(2,128)}) conditional(s32[]{:T(128)} %convert_element_type.562, (bf16[1024,1024]{1,0:T(8,128)(2,1)S(1)}, s32[]{:T(128)}, f32[3,512]{1,0:T(4,128)S(1)}, f32[1024,4,2]{0,2,1:T(2,128)}) %tuple.141, (s32[]{:T(128)}, bf16[1024,1024]{1,0:T(8,128)(2,1)S(1)}, ...), branch_computations={%region_13.14_spmd, %region_14.19_spmd} | conditional | flops 1131997184 | bytes 79760416 | solution.py:329
  586.6 37.2 %conditional.18 = (bf16[512,512]{0,1:T(8,128)(2,1)}, f32[1024,4,2]{0,2,1:T(2,128)}) conditional(s32[]{:T(128)} %convert_element_type.562, (bf16[1024,1024]{1,0:T(8,128)(2,1)S(1)}, s32[]{:T(128)}, f32[3,512]{1,0:T(4,128)S(1)}, f32[1024,4,2]{0,2,1:T(2,128)}) %tuple.144, (s32[]{:T(128)}, bf16[1024,1024]{1,0:T(8,128)(2,1)S(1)}, ...), branch_computations={%region_23.24_spmd, %region_24.29_spmd} | conditional | flops 1131997184 | bytes 79760416 | solution.py:329
  711.5 78.6 %conditional.19 = (bf16[512,1024]{0,1:T(8,128)(2,1)}, f32[1024,512]{0,1:T(8,128)}, f32[2,64]{1,0:T(2,128)}, f32[3,512]{1,0:T(4,128)}) conditional(s32[]{:T(128)} %convert_element_type.562, (f32[3,512]{1,0:T(4,128)S(1)}, pred[]{:T(512)}, bf16[512,512]{1,0:T(8,128)(2,1)}, bf16[1024,1024]{1,0:T(8,128)(2,1)S(1)}, s32[]{:T(128)}) %tuple.389, ...), branch_computations={%region_33.37_spmd, %region_37.47_spmd} | conditional | flops 2745098496 | bytes 237598816 | solution.py:399
  747.4 15.1 fusion.73
  830.1 16.4 fusion.269
  874.9 88.2 %conditional.21 = (bf16[512,1024]{0,1:T(8,128)(2,1)}, f32[1024,512]{0,1:T(8,128)}, f32[2,64]{1,0:T(2,128)}, f32[3,512]{1,0:T(4,128)}) conditional(s32[]{:T(128)} %convert_element_type.562, (f32[3,512]{1,0:T(4,128)S(1)}, pred[]{:T(512)}, bf16[512,512]{1,0:T(8,128)(2,1)}, bf16[1024,1024]{1,0:T(8,128)(2,1)S(1)}, s32[]{:T(128)}, ...), branch_computations={%region_53.57_spmd, %region_57.67_spmd} | conditional | flops 2745623040 | bytes 243883584 | solution.py:399
  918.1 15.1 fusion.111
  1009.8 15.9 fusion.268
  1060.0 84.7 %conditional.23 = (bf16[512,1024]{0,1:T(8,128)(2,1)S(1)}, f32[2,64]{1,0:T(2,128)}, f32[3,512]{1,0:T(4,128)}) conditional(s32[]{:T(128)} %convert_element_type.562, (f32[3,512]{1,0:T(4,128)S(1)}, pred[]{:T(512)}, bf16[512,512]{1,0:T(8,128)(2,1)}, bf16[1024,1024]{1,0:T(8,128)(2,1)S(1)}, s32[]{:T(128)}, /*index=5*/f32[1024,512]{0,1:T(8,128)}, ...), branch_computations={%region_73.77_spmd, %region_77.87_spmd} | conditional | flops 2745360896 | bytes 220814688 | solution.py:399
  1101.3 15.6 fusion.154
  1185.7 16.3 convolution_bitcast_fusion.7
  1250.0 39.9 %all-reduce.20 = (f32[2,2,1024]{2,1,0:T(2,128)}, f32[2,64]{1,0:T(2,128)}, f32[3,1024]{1,0:T(4,128)}) all-reduce(f32[2,2,1024]{2,1,0:T(2,128)S(1)} %pad_select_fusion, f32[2,64]{1,0:T(2,128)} %get-tuple-element.538, ...), channel_id=1, replica_groups=mesh['section'=2,'seq'=2,'fsdp'=8] {'section','seq','fsdp'}, use_global_device_ids=true, to_apply=%region_96.97 | all-reduce | flops 7296 | bytes 58368 | tf_op jit(solution)/shard_map/psum | solution.py:470
  1296.6 19.9 reduce-scatter.17.cloned.1.call-done
  1316.6 106.8 %reduce-scatter.7.cloned.1.call-done = f32[1,64,2048]{2,1,0:T(8,128)} async-done(((f32[1,1024,2048]{2,1,0:T(8,128)}), f32[1,64,2048]{2,1,0:T(8,128)}) %reduce-scatter.7.cloned.1.call-update) | async-done | bytes 524304 | tf_op jit(solution)/shard_map/reduce_scatter | solution.py:453
  1423.4 199.7 %reduce-scatter.15.cloned.1.call-done = f32[1,288,1024]{2,1,0:T(8,128)} async-done(((f32[1,4608,1024]{2,1,0:T(8,128)}), f32[1,288,1024]{2,1,0:T(8,128)}) %reduce-scatter.15.cloned.1.call-update) | async-done | bytes 1179664 | tf_op jit(solution)/shard_map/reduce_scatter | solution.py:457
  1623.1 199.3 %reduce-scatter.11.cloned.1.call-done = f32[1,64,4608]{2,1,0:T(8,128)} async-done(((f32[1,1024,4608]{2,1,0:T(8,128)}), f32[1,64,4608]{2,1,0:T(8,128)}) %reduce-scatter.11.cloned.1.call-update) | async-done | bytes 1179664 | tf_op jit(solution)/shard_map/reduce_scatter | solution.py:455
  1822.4 199.2 %reduce-scatter.13.cloned.1.call-done = f32[1,64,4608]{2,1,0:T(8,128)} async-done(((f32[1,1024,4608]{2,1,0:T(8,128)}), f32[1,64,4608]{2,1,0:T(8,128)}) %reduce-scatter.13.cloned.1.call-update) | async-done | bytes 1179664 | tf_op jit(solution)/shard_map/reduce_scatter | solution.py:456
  (734 shorter events, 852.1 us)
Async XLA Ops:
  7.2 52.3 %all-gather.7.cloned.1.call-start = ((), (), s32[]{:S(2)}) async-start(), calls=%async_computation.18 | async-start | bytes 4718592 | tf_op jit(solution)/shard_map/all_gather | solution.py:115
  7.9 93.9 %all-gather.9.cloned.1.call-start = ((), (), s32[]{:S(2)}) async-start(), calls=%async_computation.19 | async-start | bytes 2228224 | tf_op jit(solution)/shard_map/all_gather | solution.py:113
  8.7 164.0 %all-gather.11.cloned.1.call-start = ((), (), s32[]{:S(2)}) async-start(), calls=%async_computation.20 | async-start | bytes 2359296 | tf_op jit(solution)/shard_map/all_gather | solution.py:116
  9.4 213.7 %all-gather.15.cloned.1.call-start = ((), (), s32[]{:S(2)}) async-start(), calls=%async_computation.22 | async-start | bytes 10616832 | tf_op jit(solution)/shard_map/all_gather | solution.py:118
  10.0 303.8 %all-gather.13.cloned.1.call-start = ((), (), s32[]{:S(2)}) async-start(), calls=%async_computation.21 | async-start | bytes 10616832 | tf_op jit(solution)/shard_map/all_gather | solution.py:117
  10.6 394.0 %all-gather.17.cloned.1.call-start = ((), (), s32[]{:S(2)}) async-start(), calls=%async_computation.23 | async-start | bytes 10616832 | tf_op jit(solution)/shard_map/all_gather | solution.py:119
  104.9 17.9 all-to-all-start
  414.9 15.3 collective-permute-start
  442.9 18.0 all-to-all-start.2
  544.0 10.8 collective-permute-start.1
  567.0 15.6 all-to-all-start.4
  625.8 11.1 all-to-all-start.5
  792.4 13.9 all-to-all-start.7
  818.5 11.2 collective-permute-start.2
  965.4 15.0 all-to-all-start.9
  969.8 326.8 %reduce-scatter.9.cloned.1.call-start = ((), (), s32[]{:S(2)}) async-start(), calls=%async_computation.25 | async-start | bytes 4456448 | tf_op jit(solution)/shard_map/reduce_scatter | solution.py:454
  995.8 11.5 collective-permute-start.3
  1049.1 10.9 all-to-all-start.10
  1146.0 13.9 all-to-all-start.11
  1150.5 166.1 %reduce-scatter.17.cloned.1.call-start = ((), (), s32[]{:S(2)}) async-start(), calls=%async_computation.29 | async-start | bytes 4325376 | tf_op jit(solution)/shard_map/reduce_scatter | solution.py:464
  1176.5 246.9 %reduce-scatter.7.cloned.1.call-start = ((), (), s32[]{:S(2)}) async-start(), calls=%async_computation.24 | async-start | bytes 8912896 | tf_op jit(solution)/shard_map/reduce_scatter | solution.py:453
  1184.5 438.6 %reduce-scatter.15.cloned.1.call-start = ((), (), s32[]{:S(2)}) async-start(), calls=%async_computation.28 | async-start | bytes 20054016 | tf_op jit(solution)/shard_map/reduce_scatter | solution.py:457
  1202.0 620.5 %reduce-scatter.11.cloned.1.call-start = ((), (), s32[]{:S(2)}) async-start(), calls=%async_computation.26 | async-start | bytes 20054016 | tf_op jit(solution)/shard_map/reduce_scatter | solution.py:455
  1215.5 806.1 %reduce-scatter.13.cloned.1.call-start = ((), (), s32[]{:S(2)}) async-start(), calls=%async_computation.27 | async-start | bytes 20054016 | tf_op jit(solution)/shard_map/reduce_scatter | solution.py:456
  (156 other events, 2521.2 us)
Sparse Core Ops, SparseCore 0:
  9.6 49.8 all-gather.6
  61.7 40.1 all-gather.8
  103.5 27.8 all-gather.10
  132.9 90.2 all-gather.14
  224.6 89.1 all-gather.12
  315.3 89.1 all-gather.16
  1045.7 72.1 reduce-scatter.8
  1176.7 139.8 reduce-scatter.16
  1321.8 101.6 reduce-scatter.6
  1428.5 194.5 reduce-scatter.14
  1628.3 194.0 reduce-scatter.10
  1827.5 194.0 reduce-scatter.12
where the time goes:
time: 2040 us; the launch traced here: 2030 us
  waiting for transfers between devices  1110 us (54%)
  matrix products  403 us (20%)
  other arithmetic  199 us (10%)
  local copies, waits for them, and re-layouts  157 us (8%)
  blocking collectives  81.7 us (4%)
  starting transfers between devices  45.2 us (2%)
    reduce_scatter x1, waiting for transfers between devices, local(): lax.psum_scatter(grads[4], ('seq', 'fsdp'), scatter_dimension=1, tiled=True)  200 us
    reduce_scatter x1, waiting for transfers between devices, local(): lax.psum_scatter(grads[2], ('seq', 'fsdp'), scatter_dimension=1, tiled=True)  199 us
    reduce_scatter x1, waiting for transfers between devices, local(): lax.psum_scatter(grads[3], ('seq', 'fsdp'), scatter_dimension=1, tiled=True)  199 us
    reduce_scatter x1, waiting for transfers between devices, local(): lax.psum_scatter(grads[0], ('seq', 'fsdp'), scatter_dimension=1, tiled=True)  107 us
    dot_general x15, matrix products, matmul_t(): lax.dot_general(left, right, (((1,), (1,)), ((), ())), preferred_element_...  101 us
    dot_general x15, matrix products, matmul(): return jnp.dot(left, right, preferred_element_type=jnp.float32)  91.8 us
    all_gather x1, waiting for transfers between devices, local(): lax.all_gather(w_gate, 'fsdp', axis=1, tiled=True)  78.4 us
    all_gather x1, waiting for transfers between devices, local(): lax.all_gather(w_down, 'fsdp', axis=1, tiled=True)  78.4 us
  transfers between devices with their start and end apart: 24, of which 21 were waited for; matrix products, arithmetic and copies ran while one was open for 13% of the time, Pallas kernels for 0%

commit v1 on v0

v1 whole, which is shorter than its diff:
```python
import functools

import jax
import jax.numpy as jnp
from jax import lax
from jax.experimental import pallas as pl
from jax.experimental.pallas import tpu as pltpu
from jax.sharding import PartitionSpec as P

HEADS = 16
KV_HEADS = 8
HEAD = 64
PAIR = 2 * HEAD
GROUP = 2 * PAIR

EPSILON = 1e-05
THETA = 1000000.0
NEGATIVE = -1e30
BF16 = jnp.bfloat16
F32 = jnp.float32
VMEM_LIMIT = 56 * 1024 * 1024


def rms_scale(value):
    return lax.rsqrt(jnp.mean(value * value, axis=-1, keepdims=True) + EPSILON)


def norm_back(grad_out, value, scale, gain):
    inner = grad_out * gain
    return scale * (inner - value * scale * scale * jnp.mean(inner * value, axis=-1, keepdims=True))


def matmul(left, right):
    return jnp.dot(left, right, preferred_element_type=F32)


def matmul_t(left, right):
    return lax.dot_general(left, right, (((1,), (1,)), ((), ())), preferred_element_type=F32)


def outer_sum(left, right):
    return lax.dot_general(left, right, (((0,), (0,)), ((), ())), preferred_element_type=F32)


def params():
    return pltpu.CompilerParams(vmem_limit_bytes=VMEM_LIMIT)


def group_mean(value):
    row = lax.broadcasted_iota(jnp.int32, (PAIR, PAIR), 0) // HEAD
    col = lax.broadcasted_iota(jnp.int32, (PAIR, PAIR), 1) // HEAD
    ones = jnp.where(row == col, 1.0 / HEAD, 0.0).astype(F32)
    return jnp.dot(value, ones, precision=lax.Precision.HIGHEST, preferred_element_type=F32)


def lane_swap(value):
    lane = lax.broadcasted_iota(jnp.int32, value.shape, 1) % HEAD
    return jnp.where(
        lane < HEAD // 2, pltpu.roll(value, PAIR - HEAD // 2, 1), pltpu.roll(value, HEAD // 2, 1)
    )


def project_kernel(x_ref, w_ref, cos_ref, sin_ref, gain_ref, raw_ref, q_ref, kv_ref):
    raw = jnp.dot(x_ref[...], w_ref[...], preferred_element_type=F32).astype(BF16)
    raw_ref[...] = raw
    for part, out in ((0, q_ref), (1, kv_ref)):
        vec = raw[:, part * PAIR : (part + 1) * PAIR].astype(F32)
        normed = vec * lax.rsqrt(group_mean(vec * vec) + EPSILON) * gain_ref[part : part + 1, :]
        turned = normed * cos_ref[...] + lane_swap(normed) * sin_ref[...]
        if part == 1:
            lane = lax.broadcasted_iota(jnp.int32, vec.shape, 1)
            turned = jnp.where(lane < HEAD, turned, vec)
        out[...] = turned.astype(BF16)


def project(normed, weight, cosine, sine, gain_rows):
    tokens, width = normed.shape
    whole = lambda g: (0, 0)
    column = lambda g: (0, g)
    return pl.pallas_call(
        project_kernel,
        grid=(KV_HEADS,),
        in_specs=[
            pl.BlockSpec((tokens, width), whole),
            pl.BlockSpec((width, GROUP), column),
            pl.BlockSpec((tokens, PAIR), whole),
            pl.BlockSpec((tokens, PAIR), whole),
            pl.BlockSpec((8, PAIR), whole),
        ],
        out_specs=[
            pl.BlockSpec((tokens, GROUP), column),
            pl.BlockSpec((tokens, PAIR), column),
            pl.BlockSpec((tokens, PAIR), column),
        ],
        out_shape=[
            jax.ShapeDtypeStruct((tokens, KV_HEADS * GROUP), BF16),
            jax.ShapeDtypeStruct((tokens, KV_HEADS * PAIR), BF16),
            jax.ShapeDtypeStruct((tokens, KV_HEADS * PAIR), BF16),
        ],
        compiler_params=params(),
        cost_estimate=pl.CostEstimate(
            flops=2 * tokens * width * KV_HEADS * GROUP, bytes_accessed=12 << 20, transcendentals=0
        ),
    )(normed, weight, cosine, sine, gain_rows)


def attend_kernel(rows, stretches, part_ref, q_ref, own_ref, peer_ref, out_ref):
    second = part_ref[0] == 1
    for stretch in range(stretches):
        blocks = []
        for s in range(stretch + 1):
            blocks += [own_ref[s * rows : (s + 1) * rows, :], peer_ref[s * rows : (s + 1) * rows, :]]
        pack = jnp.concatenate(blocks, axis=0)
        keys, values = (pack[:, :HEAD], pack[:, HEAD:])
        count = pack.shape[0]
        row = lax.broadcasted_iota(jnp.int32, (rows, count), 0)
        col = lax.broadcasted_iota(jnp.int32, (rows, count), 1) - stretch * 2 * rows
        allowed = (col <= row) | ((col >= rows) & second)
        for j in range(2):
            query = q_ref[stretch * rows : (stretch + 1) * rows, j * HEAD : (j + 1) * HEAD]
            scores = matmul_t(query, keys) * HEAD ** (-0.5)
            scores = jnp.where(allowed, scores, NEGATIVE)
            exponent = jnp.exp(scores - jnp.max(scores, axis=1, keepdims=True))
            total = jnp.sum(exponent, axis=1, keepdims=True)
            probs = (exponent * (1.0 / total)).astype(BF16)
            out_ref[stretch * rows : (stretch + 1) * rows, j * HEAD : (j + 1) * HEAD] = jnp.dot(
                probs, values, preferred_element_type=F32
            ).astype(BF16)


def attend(part, query, own, peer, rows, stretches):
    tokens = query.shape[0]
    column = lambda g: (0, g)
    return pl.pallas_call(
        functools.partial(attend_kernel, rows, stretches),
        grid=(KV_HEADS,),
        in_specs=[pl.BlockSpec(memory_space=pltpu.SMEM)]
        + [pl.BlockSpec((tokens, PAIR), column)] * 3,
        out_specs=pl.BlockSpec((tokens, PAIR), column),
        out_shape=jax.ShapeDtypeStruct((tokens, KV_HEADS * PAIR), BF16),
        compiler_params=params(),
        cost_estimate=pl.CostEstimate(
            flops=10_000_000_000, bytes_accessed=4 << 20, transcendentals=7_000_000
        ),
    )(part, query, own, peer)


def attend_back_kernel(
    rows, stretches, part_ref, q_ref, own_ref, peer_ref, grad_ref, dq_ref, down_ref, dpeer_ref
):
    second = part_ref[0] == 1
    for stretch in reversed(range(stretches)):
        blocks = []
        for s in range(stretch + 1):
            blocks += [own_ref[s * rows : (s + 1) * rows, :], peer_ref[s * rows : (s + 1) * rows, :]]
        pack = jnp.concatenate(blocks, axis=0)
        keys, values = (pack[:, :HEAD], pack[:, HEAD:])
        count = pack.shape[0]
        col = lax.broadcasted_iota(jnp.int32, (count, rows), 0) - stretch * 2 * rows
        row = lax.broadcasted_iota(jnp.int32, (count, rows), 1)
        allowed = (col <= row) | ((col >= rows) & second)
        span = slice(stretch * rows, (stretch + 1) * rows)
        dkeys, dvalues, dquery = (0.0, 0.0, [])
        for j in range(2):
            query = q_ref[span, j * HEAD : (j + 1) * HEAD]
            grad = grad_ref[span, j * HEAD : (j + 1) * HEAD]
            scores = matmul_t(keys, query) * HEAD ** (-0.5)
            scores = jnp.where(allowed, scores, NEGATIVE)
            exponent = jnp.exp(scores - jnp.max(scores, axis=0, keepdims=True))
            probs = exponent * (1.0 / jnp.sum(exponent, axis=0, keepdims=True))
            dprobs = matmul_t(values, grad)
            dscores = probs * (dprobs - jnp.sum(probs * dprobs, axis=0, keepdims=True))
            dscores = dscores.astype(BF16)
            dvalues += jnp.dot(probs.astype(BF16), grad, preferred_element_type=F32)
            dkeys += jnp.dot(dscores, query, preferred_element_type=F32) * HEAD ** (-0.5)
            dquery.append(outer_sum(dscores, keys) * HEAD ** (-0.5))
        dq_ref[span, :] = jnp.concatenate(dquery, axis=1)
        both = jnp.concatenate([dkeys, dvalues], axis=1)
        for s in range(stretch + 1):
            for place, out in ((2 * s, down_ref), (2 * s + 1, dpeer_ref)):
                piece = both[place * rows : (place + 1) * rows]
                span_s = slice(s * rows, (s + 1) * rows)
                if stretch == stretches - 1:
                    out[span_s, :] = piece
                else:
                    out[span_s, :] += piece


def attend_back(part, query, own, peer, grad, rows, stretches):
    tokens = query.shape[0]
    column = lambda g: (0, g)
    shape = jax.ShapeDtypeStruct((tokens, KV_HEADS * PAIR), F32)
    return pl.pallas_call(
        functools.partial(attend_back_kernel, rows, stretches),
        grid=(KV_HEADS,),
        in_specs=[pl.BlockSpec(memory_space=pltpu.SMEM)]
        + [pl.BlockSpec((tokens, PAIR), column)] * 4,
        out_specs=[pl.BlockSpec((tokens, PAIR), column)] * 3,
        out_shape=[shape] * 3,
        compiler_params=params(),
        cost_estimate=pl.CostEstimate(
            flops=25_000_000_000, bytes_accessed=12 << 20, transcendentals=7_000_000
        ),
    )(part, query, own, peer, grad)


def project_back_kernel(
    raw_ref, dq_ref, own_ref, recv_ref, cos_ref, sin_ref, gain_ref, w_ref, pack_ref, normed_ref, head_ref
):
    first = pl.program_id(0) == 0
    grads = []
    for part in range(2):
        vec = raw_ref[:, part * PAIR : (part + 1) * PAIR].astype(F32)
        if part == 0:
            grad = dq_ref[...]
        else:
            grad = own_ref[...] + recv_ref[...].astype(F32)
        gain = gain_ref[part : part + 1, :]
        scale = lax.rsqrt(group_mean(vec * vec) + EPSILON)
        turned = grad * cos_ref[...] - lane_swap(grad) * sin_ref[...]
        gain_sum = jnp.sum(turned * vec * scale, axis=0, keepdims=True)
        inner = turned * gain
        back = scale * (inner - vec * scale * scale * group_mean(inner * vec))
        if part == 1:
            lane = lax.broadcasted_iota(jnp.int32, vec.shape, 1)
            back = jnp.where(lane < HEAD, back, grad)
        back = back.astype(BF16)
        pack_ref[:, part * PAIR : (part + 1) * PAIR] = back
        grads.append((back, gain_sum))
    total = matmul_t(grads[0][0], w_ref[:, :PAIR]) + matmul_t(grads[1][0], w_ref[:, PAIR:])

    @pl.when(first)
    def _():
        normed_ref[...] = total
        head_ref[...] = jnp.zeros_like(head_ref)

    @pl.when(jnp.logical_not(first))
    def _():
        normed_ref[...] += total

    for part in range(2):
        head_ref[part : part + 1, :] += grads[part][1]


def project_back(raw, dquery, own, recv, cosine, sine, gain_rows, weight):
    tokens = raw.shape[0]
    width = weight.shape[0]
    whole = lambda g: (0, 0)
    column = lambda g: (0, g)
    return pl.pallas_call(
        project_back_kernel,
        grid=(KV_HEADS,),
        in_specs=[
            pl.BlockSpec((tokens, GROUP), column),
            pl.BlockSpec((tokens, PAIR), column),
            pl.BlockSpec((tokens, PAIR), column),
            pl.BlockSpec((tokens, PAIR), column),
            pl.BlockSpec((tokens, PAIR), whole),
            pl.BlockSpec((tokens, PAIR), whole),
            pl.BlockSpec((8, PAIR), whole),
            pl.BlockSpec((width, GROUP), column),
        ],
        out_specs=[
            pl.BlockSpec((tokens, GROUP), column),
            pl.BlockSpec((tokens, width), whole),
            pl.BlockSpec((8, PAIR), whole),
        ],
        out_shape=[
            jax.ShapeDtypeStruct((tokens, KV_HEADS * GROUP), BF16),
            jax.ShapeDtypeStruct((tokens, width), F32),
            jax.ShapeDtypeStruct((8, PAIR), F32),
        ],
        compiler_params=params(),
        cost_estimate=pl.CostEstimate(
            flops=2 * tokens * width * KV_HEADS * GROUP, bytes_accessed=16 << 20, transcendentals=0
        ),
    )(raw, dquery, own, recv, cosine, sine, gain_rows, weight)


def forward_kernel(x_ref, base_ref, g_ref, u_ref, d_ref, out_ref, act_ref, one_ref, two_ref):
    gate = jnp.dot(x_ref[...], g_ref[...], preferred_element_type=F32)
    upward = jnp.dot(x_ref[...], u_ref[...], preferred_element_type=F32)
    sigma = jax.nn.sigmoid(gate)
    silu = gate * sigma
    active = (silu * upward).astype(BF16)
    act_ref[...] = active
    one_ref[...] = (upward * sigma * (1.0 + gate * (1.0 - sigma))).astype(BF16)
    two_ref[...] = silu.astype(BF16)
    down = jnp.dot(active, d_ref[...], preferred_element_type=F32)

    @pl.when(pl.program_id(0) == 0)
    def _():
        out_ref[...] = base_ref[...] + down

    @pl.when(pl.program_id(0) > 0)
    def _():
        out_ref[...] += down


def backward_kernel(grad_ref, one_ref, two_ref, g_ref, u_ref, d_ref, out_ref, dg_ref, du_ref):
    active = matmul_t(grad_ref[...], d_ref[...])
    dgate = (active * one_ref[...].astype(F32)).astype(BF16)
    dup = (active * two_ref[...].astype(F32)).astype(BF16)
    dg_ref[...] = dgate
    du_ref[...] = dup
    total = matmul_t(dgate, g_ref[...]) + matmul_t(dup, u_ref[...])

    @pl.when(pl.program_id(0) == 0)
    def _():
        out_ref[...] = total

    @pl.when(pl.program_id(0) > 0)
    def _():
        out_ref[...] += total


def hidden_chunk(hidden):
    return next(size for size in (512, 384, 256, 128, hidden) if hidden % size == 0)


def ff_forward(normed, base, gate, upward, down):
    tokens, width = normed.shape
    hidden = gate.shape[1]
    chunk = hidden_chunk(hidden)
    whole = lambda j: (0, 0)
    column = lambda j: (0, j)
    saved = jax.ShapeDtypeStruct((tokens, hidden), BF16)
    return pl.pallas_call(
        forward_kernel,
        grid=(hidden // chunk,),
        in_specs=[
            pl.BlockSpec((tokens, width), whole),
            pl.BlockSpec((tokens, width), whole),
            pl.BlockSpec((width, chunk), column),
            pl.BlockSpec((width, chunk), column),
            pl.BlockSpec((chunk, width), lambda j: (j, 0)),
        ],
        out_specs=[pl.BlockSpec((tokens, width), whole)]
        + [pl.BlockSpec((tokens, chunk), column)] * 3,
        out_shape=[jax.ShapeDtypeStruct((tokens, width), F32), saved, saved, saved],
        compiler_params=params(),
        cost_estimate=pl.CostEstimate(
            flops=6 * tokens * width * hidden,
            bytes_accessed=6 * hidden * (width + tokens),
            transcendentals=tokens * hidden,
        ),
    )(normed, base, gate, upward, down)


def ff_backward(grad, one, two, gate, upward, down):
    tokens, width = grad.shape
    hidden = gate.shape[1]
    chunk = hidden_chunk(hidden)
    whole = lambda j: (0, 0)
    column = lambda j: (0, j)
    saved = jax.ShapeDtypeStruct((tokens, hidden), BF16)
    return pl.pallas_call(
        backward_kernel,
        grid=(hidden // chunk,),
        in_specs=[
            pl.BlockSpec((tokens, width), whole),
            pl.BlockSpec((tokens, chunk), column),
            pl.BlockSpec((tokens, chunk), column),
            pl.BlockSpec((width, chunk), column),
            pl.BlockSpec((width, chunk), column),
            pl.BlockSpec((chunk, width), lambda j: (j, 0)),
        ],
        out_specs=[pl.BlockSpec((tokens, width), whole)]
        + [pl.BlockSpec((tokens, chunk), column)] * 2,
        out_shape=[jax.ShapeDtypeStruct((tokens, width), F32), saved, saved],
        compiler_params=params(),
        cost_estimate=pl.CostEstimate(
            flops=6 * tokens * width * hidden,
            bytes_accessed=6 * hidden * (width + tokens),
            transcendentals=0,
        ),
    )(grad, one, two, gate, upward, down)


def local(
    tokens,
    cotangent,
    norm_gains,
    head_gains,
    conv_kernel,
    mix_in,
    mix_out,
    w_gate,
    w_up,
    w_down,
    conv_c,
):
    first = lax.axis_index("section") == 0
    part = lax.axis_index("seq")
    place = lax.axis_index("fsdp")
    fsdp = lax.axis_size("fsdp")
    chips = fsdp // 2
    chip, core = (place // 2, place % 2)
    stretches, rows, width = tokens.shape[1:]
    hidden = w_gate.shape[2]
    total = stretches * rows
    block = 2 * rows
    gains = norm_gains[0]

    cores = [(i, i ^ 1) for i in range(fsdp)]
    swap = [(0, 1), (1, 0)]

    def to_core(value):
        return lax.ppermute(value, "fsdp", cores)

    def to_peer(value):
        return lax.ppermute(value, "seq", swap)

    def along(value, steps):
        return lax.ppermute(value, "fsdp", [(i, (i + 2 * steps) % fsdp) for i in range(fsdp)])

    def gather(shards):
        results, sent = ([], [])
        for number, shard in enumerate(shards):
            depth, columns = shard.shape
            half = depth // 2
            mine = lax.dynamic_slice_in_dim(shard, part * half, half, 0)
            if number >= 1:
                tied = sent[0] if number == 1 else sent[number - 2]
                mine, unused = lax.optimization_barrier((mine, tied))
            arrived = [along(mine, step) for step in range(1, chips)]
            sent.append(arrived)
            crossed = [to_peer(piece) for piece in arrived]
            held = jnp.zeros((chips, 2, half, columns), BF16)
            held = lax.dynamic_update_slice(
                held, shard.reshape(1, 2, half, columns), (chip, 0, 0, 0)
            )
            for step, near, far in zip(range(1, chips), arrived, crossed):
                source = (chip - step) % chips
                held = lax.dynamic_update_slice(held, near[None, None], (source, part, 0, 0))
                held = lax.dynamic_update_slice(held, far[None, None], (source, 1 - part, 0, 0))
            other = to_core(held)
            full = jnp.broadcast_to(held[:, None], (chips, 2, 2, half, columns))
            full = lax.dynamic_update_slice(full, other[:, None], (0, 1 - core, 0, 0, 0))
            results.append(full.reshape(fsdp * depth, columns))
        return results

    def core_columns(value, which, cut):
        wide = value.reshape(value.shape[0], 2, chips, 2, cut)
        return lax.dynamic_index_in_dim(wide, which, 3, keepdims=False).reshape(
            value.shape[0], chips * 2 * cut
        )

    def reduce(left, right):
        cut = left.shape[1] // (2 * fsdp)
        columns = right.shape[1]
        leaving = outer_sum(core_columns(left, 1 - core, cut), right).astype(BF16)
        staying = outer_sum(core_columns(left, core, cut), right)
        both = (staying + to_core(leaving).astype(F32)).astype(BF16)
        both = both.reshape(2, chips, cut, columns)
        crossing = lax.dynamic_index_in_dim(both, 1 - part, 0, keepdims=False)
        own = lax.dynamic_index_in_dim(both, part, 0, keepdims=False)
        own = (own.astype(F32) + to_peer(crossing).astype(F32)).astype(BF16)
        result = lax.dynamic_index_in_dim(own, chip, 0, keepdims=False).astype(F32)
        for step in range(1, chips):
            piece = lax.dynamic_index_in_dim(own, (chip + step) % chips, 0, keepdims=False)
            result = result + along(piece, step).astype(F32)
        return result

    def reduce_small(value):
        value = value + to_core(value)
        value = value + to_peer(value)
        step = 2
        while step < fsdp:
            value = value + lax.ppermute(value, "fsdp", [(i, i ^ step) for i in range(fsdp)])
            step *= 2
        return value

    def zeros(*shape, kind=BF16):
        return jnp.zeros(shape, kind)

    c_low = lax.ppermute(conv_c, "section", [(0, 1)])
    shards = (mix_in[0], mix_out[0], w_gate[0], w_up[0], w_down[0])

    positions = (
        jnp.arange(stretches)[:, None] * block + part * rows + jnp.arange(rows)[None, :]
    ).reshape(total)
    part_ref = part.astype(jnp.int32).reshape(1)

    def rope():
        lane = jnp.arange(PAIR)
        frequency = THETA ** (-(lane % (HEAD // 2)).astype(F32) * 2.0 / HEAD)
        angle = positions.astype(F32)[:, None] * frequency[None, :]
        sign = jnp.where(lane % HEAD < HEAD // 2, -1.0, 1.0)
        return (jnp.cos(angle), jnp.sin(angle) * sign[None, :])

    def gain_rows():
        return jnp.zeros((8, PAIR), F32).at[:2].set(jnp.tile(head_gains, (1, 2)))

    def attention_forward():
        w_in, w_out, gate, upward, down = gather(shards)
        source = tokens[0].reshape(total, width).astype(F32)
        normed = (source * rms_scale(source) * gains[0]).astype(BF16)
        cosine, sine = rope()
        raw, query, own = project(normed, w_in, cosine, sine, gain_rows())
        peer = to_peer(own)
        heads = attend(part_ref, query, own, peer, rows, stretches)
        resid = source + matmul(heads, w_out)
        normed_two = (resid * rms_scale(resid) * gains[1]).astype(BF16)
        result, active, one, two = ff_forward(normed_two, resid, gate, upward, down)
        weights = (w_in, w_out, gate, upward, down, zeros(width, width))
        kept = (normed, raw, query, own, peer, heads, resid, normed_two, active, one, two)
        return (weights, kept, cosine, sine, result.astype(BF16))

    def conv_gather():
        both = jnp.concatenate([c_low, conv_c], axis=1)
        w_in, c_wide, w_out, gate, upward, down = gather((shards[0], both, *shards[1:]))
        w_c = jnp.concatenate([c_wide[:, :width], c_wide[:, width:]], axis=0)
        weights = (w_in, w_out, gate, upward, down, w_c)
        flat = lambda: zeros(total, width)
        wide = lambda: zeros(total, hidden)
        kept = (
            flat(), zeros(total, KV_HEADS * GROUP), flat(), flat(), flat(), flat(),
            zeros(total, width, kind=F32), flat(), wide(), wide(), wide(),
        )
        table = lambda: zeros(total, PAIR, kind=F32)
        return (weights, kept, table(), table(), flat())

    weights, kept, cosine, sine, link = lax.cond(first, attention_forward, conv_gather)
    link = lax.ppermute(link, "section", [(0, 1)])

    def tail_of(value, start):
        return to_peer(value.reshape(stretches, rows, width)[:, start : start + 2])

    def conv_both():
        w_in, w_out, gate, upward, down, w_c = weights
        source = link.astype(F32)
        scale_one = rms_scale(source)
        normed = (source * scale_one * gains[0]).astype(BF16)
        pair = matmul(normed, w_in)
        left, right = (pair[:, :width], pair[:, width:])
        product = (left * right).astype(BF16)
        tails = tail_of(product, rows - 2).astype(F32)
        conv_gate = matmul(normed, w_c).astype(BF16).astype(F32)
        early = jnp.concatenate([jnp.zeros_like(tails[:1]), tails[:-1]], axis=0)
        before = jnp.where(part == 0, early, tails)
        inner = product.astype(F32).reshape(stretches, rows, width)
        longer = jnp.concatenate([before, inner], axis=1)
        taps = [longer[:, i : i + rows] for i in range(3)]
        state = sum(conv_kernel[i] * taps[i] for i in range(3)).reshape(total, width)
        heads = (conv_gate * state).astype(BF16)
        resid = source + matmul(heads, w_out)
        scale_two = rms_scale(resid)
        normed_two = (resid * scale_two * gains[1]).astype(BF16)
        result, active, one, two = ff_forward(normed_two, resid, gate, upward, down)

        grad_ff = cotangent[0].reshape(total, width)
        grad_two, dgate, dup = ff_backward(grad_ff, one, two, gate, upward, down)
        gain_two = jnp.sum(grad_two * resid * scale_two, axis=0)
        grad_resid = grad_ff.astype(F32) + norm_back(grad_two, resid, scale_two, gains[1])
        dmix = grad_resid.astype(BF16)
        dheads = matmul_t(dmix, w_out).astype(BF16).astype(F32)
        dgate_c = (dheads * state).astype(BF16)
        dstate = (dheads * conv_gate).reshape(stretches, rows, width)
        fronts = tail_of(dstate, 0)
        late = jnp.concatenate([fronts[1:], jnp.zeros_like(fronts[:1])], axis=0)
        after = jnp.where(part == 0, fronts, late)
        further = jnp.concatenate([dstate, after], axis=1)
        dproduct = sum(conv_kernel[2 - i] * further[:, i : i + rows] for i in range(3))
        dproduct = dproduct.reshape(total, width).astype(BF16).astype(F32)
        kernel_grad = jnp.stack([jnp.sum(dstate * taps[i], axis=(0, 1)) for i in range(3)])
        dproj = jnp.concatenate([dproduct * right, dproduct * left], axis=1).astype(BF16)
        grad_one = matmul_t(dproj, w_in) + matmul_t(dgate_c, w_c)
        gain_one = jnp.sum(grad_one * source * scale_one, axis=0)
        grad_source = grad_resid + norm_back(grad_one, source, scale_one, gains[0])
        small = jnp.concatenate(
            [gain_one[None], gain_two[None], kernel_grad, jnp.zeros((3, width), F32)], axis=0
        )
        moved = (normed, dproj, dgate_c, heads, dmix, normed_two, dgate, dup, active)
        return (result, moved, small, grad_source.astype(BF16))

    def attention_idle():
        flat = lambda: zeros(total, width)
        wide = lambda: zeros(total, hidden)
        moved = (
            flat(), zeros(total, 2 * width), flat(), flat(), flat(), flat(), wide(), wide(), wide(),
        )
        return (zeros(total, width, kind=F32), moved, zeros(8, width, kind=F32), flat())

    outputs, moved, conv_small, grad_link = lax.cond(first, attention_idle, conv_both)
    grad_link = lax.ppermute(grad_link, "section", [(1, 0)])

    def attention_back():
        w_in, w_out, gate, upward, down, unused = weights
        normed, raw, query, own, peer, heads, resid, normed_two, active, one, two = kept
        shard_down = reduce(active, grad_link)
        grad_two, dgate, dup = ff_backward(grad_link, one, two, gate, upward, down)
        shard_gate = reduce(normed_two, dgate)
        shard_up = reduce(normed_two, dup)
        scale_two = rms_scale(resid)
        gain_two = jnp.sum(grad_two * resid * scale_two, axis=0)
        grad_resid = grad_link.astype(F32) + norm_back(grad_two, resid, scale_two, gains[1])
        dmix = grad_resid.astype(BF16)
        shard_out = reduce(heads, dmix)
        dheads = matmul_t(dmix, w_out).astype(BF16)
        dquery, down_kv, peer_kv = attend_back(part_ref, query, own, peer, dheads, rows, stretches)
        recv = to_peer(peer_kv.astype(BF16))
        dproj, grad_one, head_rows = project_back(
            raw, dquery, down_kv, recv, cosine, sine, gain_rows(), w_in
        )
        shard_in = reduce(normed, dproj)
        source = tokens[0].reshape(total, width).astype(F32)
        scale_one = rms_scale(source)
        gain_one = jnp.sum(grad_one * source * scale_one, axis=0)
        grad_source = grad_resid + norm_back(grad_one, source, scale_one, gains[0])
        head_grad = jnp.stack([head_rows[0, :HEAD] + head_rows[0, HEAD:], head_rows[1, :HEAD]])
        head_row = jnp.pad(head_grad.reshape(1, PAIR), ((0, 0), (0, width - PAIR)))
        small = jnp.concatenate(
            [gain_one[None], gain_two[None], jnp.zeros((3, width), F32), head_row,
             jnp.zeros((2, width), F32)], axis=0
        )
        small = reduce_small(small)
        shards = (shard_in, shard_out, shard_gate, shard_up, shard_down)
        return (grad_source, shards, zeros(2 * conv_cut, width, kind=F32), small)

    conv_cut = width // (4 * fsdp)

    def conv_weights():
        normed, dproj, dgate_c, heads, dmix, normed_two, dgate, dup, active = moved
        grad_ff = cotangent[0].reshape(total, width)
        shard_down = reduce(active, grad_ff)
        shard_gate = reduce(normed_two, dgate)
        shard_up = reduce(normed_two, dup)
        shard_out = reduce(heads, dmix)
        shard_in = reduce(normed, dproj)
        turned = normed.reshape(total, 2, 2 * fsdp, conv_cut)
        turned = jnp.transpose(turned, (0, 2, 1, 3)).reshape(total, width)
        shard_c = reduce(turned, dgate_c)
        small = reduce_small(conv_small)
        shards = (shard_in, shard_out, shard_gate, shard_up, shard_down)
        return (outputs, shards, shard_c, small)

    ends, shards_out, shard_c, small = lax.cond(first, attention_back, conv_weights)
    mail = lax.ppermute(
        jnp.concatenate([shard_c, small], axis=0), "section", swap
    )
    c_shard = jnp.where(first, mail[:conv_cut], shard_c[conv_cut:])
    theirs = mail[2 * conv_cut :]
    merged_a, merged_c = (jnp.where(first, small, theirs), jnp.where(first, theirs, small))
    grad_norm = jnp.stack([merged_a[:2], merged_c[:2]])
    grad_head = merged_a[5, :PAIR].reshape(2, HEAD)
    return (
        ends.reshape(1, 1, stretches, rows, width),
        grad_norm,
        grad_head,
        merged_c[2:5],
        *[shard[None] for shard in shards_out],
        c_shard,
    )


def solution(mesh):
    return jax.shard_map(
        local,
        mesh=mesh,
        in_specs=(
            P("fsdp", None, "seq", None),
            P("fsdp", None, "seq", None),
            P("section", None, None),
            P(),
            P(),
            P("section", "fsdp", None),
            P("section", "fsdp", None),
            P("section", "fsdp", None),
            P("section", "fsdp", None),
            P("section", "fsdp", None),
            P(("section", "fsdp"), None),
        ),
        out_specs=(
            P("section", "fsdp", None, "seq", None),
            P(),
            P(),
            P(),
            P("section", ("seq", "fsdp"), None),
            P("section", ("seq", "fsdp"), None),
            P("section", ("seq", "fsdp"), None),
            P("section", ("seq", "fsdp"), None),
            P("section", ("seq", "fsdp"), None),
            P(("section", "seq", "fsdp"), None),
        ),
        check_vma=False,
    )
```

time: 2040 us -> 1030 us (0.50)
  waiting for transfers between devices: 1110 us -> 481 us
  matrix products: 403 us -> 55.8 us
  other arithmetic: 199 us -> 29.6 us
  Pallas kernels: 0 us -> 139 us
  starting transfers between devices: 45.2 us -> 158 us
  blocking collectives: 81.7 us -> 0 us
  local copies, waits for them, and re-layouts: 157 us -> 136 us
    reduce_scatter x6 -> x0, waiting for transfers between devices: 725 us -> none  [the longest x1 200 us: local(): lax.psum_scatter(grads[4], ('seq', 'fsdp'), scatter_dimension=1, tiled=True)]
    ppermute x4 -> x70, waiting for transfers between devices: 28.6 us -> 481 us  [the longest x23 210 us: to_peer(): return lax.ppermute(value, 'seq', swap)]
    all_gather x6 -> x0, waiting for transfers between devices: 288 us -> none  [the longest x1 78.4 us: local(): lax.all_gather(w_gate, 'fsdp', axis=1, tiled=True)]
    dot_general x36 -> x1, matrix products: 253 us -> 3.32 us  [matmul(): return jnp.dot(left, right, preferred_element_type=F32)]
    ppermute x4 -> x70, starting transfers between devices: 9.86 us -> 158 us  [the longest x30 97 us: along(): lax.ppermute(value, 'fsdp', [(i, (i + 2 * steps) % fsdp) for i in range(f...]
    pallas_call x0 -> x6, Pallas kernels: none -> 139 us  [the longest x1 34.3 us: attend_back(): pl.pallas_call(functools.partial(attend_back_kernel, rows, stretches), gr...]
    dot_general x15 -> x1, matrix products: 101 us -> 4.66 us  [matmul_t(): lax.dot_general(left, right, (((1,), (1,)), ((), ())), preferred_element_...]
    all_to_all x8 -> x0, waiting for transfers between devices: 64 us -> none  [the longest x3 36.2 us: local(): lax.all_to_all(pack, 'seq', split_axis=1, concat_axis=0, tiled=True)]
  transfers between devices with their start and end apart: 24 -> 70, of which waited for: 21 -> 29; matrix products, arithmetic and copies ran while one was open for 13% -> 16% of each run, Pallas kernels for 0% -> 11%
where the time goes in v1:
time: 1030 us
  waiting for transfers between devices  481 us (47%)
  starting transfers between devices  158 us (15%)
  Pallas kernels  139 us (13%)
  local copies, waits for them, and re-layouts  136 us (13%)
  matrix products  55.8 us (5%)
  other arithmetic  29.6 us (3%)
  loops' own time  24.9 us (2%)
    ppermute x23, waiting for transfers between devices, to_peer(): return lax.ppermute(value, 'seq', swap)  210 us
    ppermute x30, waiting for transfers between devices, along(): lax.ppermute(value, 'fsdp', [(i, (i + 2 * steps) % fsdp) for i in range(f...  141 us
    ppermute x30, starting transfers between devices, along(): lax.ppermute(value, 'fsdp', [(i, (i + 2 * steps) % fsdp) for i in range(f...  97 us
    ppermute x1, waiting for transfers between devices, local(): grad_link = lax.ppermute(grad_link, 'section', [(1, 0)])  95.4 us
    dot_general x10, matrix products, outer_sum(): lax.dot_general(left, right, (((0,), (0,)), ((), ())), preferred_element_...  47.8 us
    another operation x25, local copies, waits for them, and re-layouts  38.7 us
    pallas_call x1, Pallas kernels, attend_back(): pl.pallas_call(functools.partial(attend_back_kernel, rows, stretches), gr...  34.3 us
    broadcast_in_dim x5, local copies, waits for them, and re-layouts, gather(): full = jnp.broadcast_to(held[:, None], (chips, 2, 2, half, columns))  26.1 us
  transfers between devices with their start and end apart: 70, of which 29 were waited for; matrix products, arithmetic and copies ran while one was open for 16% of the time, Pallas kernels for 11%

profile of v1, /device:TPU:0, one launch (start us, length us, event | category | flops | bytes accessed | tf_op | source)
XLA Modules:
  0.0 1025.1 jit_solution(16046846014052651811)
XLA Ops:
  8.5 372.4 %conditional.3 = (bf16[1024,2048]{1,0:T(8,128)(2,1)}, bf16[1024,1024]{1,0:T(8,128)(2,1)}, bf16[1024,4608]{1,0:T(8,128)(2,1)}, bf16[1024,4608]{1,0:T(8,128)(2,1)}...) conditional(s32[]{:T(128)} %convert_element_type.511, ...), branch_computations={%region_0.1_spmd, %region_1.4_spmd} | conditional | flops 27724738560 | bytes 416488960 | solution.py:524
  58.4 15.1 %collective-permute-start.58 = (bf16[64,4608]{1,0:T(8,128)(2,1)S(1)}, bf16[64,4608]{1,0:T(8,128)(2,1)S(1)}, u32[]{:S(2)}, u32[]{:S(2)}) collective-permute-start(bf16[64,4608]{1,0:T(8,128)(2,1)S(1)} %copy-done.82), channel_id=1, source_target_pairs={{0,4},{1,5},{2,6},{3,7},{4,0},{5,1},{6,2},{7,3},{8,12},{9,13},{10,... | collective-permute-start | bytes 1769480 | tf_op jit(solution)/shard_map/cond/branch_1_fun/ppermute | solution.py:415
  97.1 16.5 %collective-permute-done.58 = bf16[64,4608]{1,0:T(8,128)(2,1)S(1)} collective-permute-done((bf16[64,4608]{1,0:T(8,128)(2,1)S(1)}, bf16[64,4608]{1,0:T(8,128)(2,1)S(1)}, u32[]{:S(2)}, u32[]{:S(2)}) %collective-permute-start.58) | collective-permute-done | bytes 589856 | tf_op jit(solution)/shard_map/cond/branch_1_fun/ppermute | solution.py:415
  113.6 22.4 %collective-permute-start.70 = (bf16[288,1024]{1,0:T(8,128)(2,1)S(1)}, bf16[288,1024]{1,0:T(8,128)(2,1)S(1)}, u32[]{:S(2)}, u32[]{:S(2)}) collective-permute-start(bf16[288,1024]{1,0:T(8,128)(2,1)S(1)} %constant_dynamic-slice_fusion.6), channel_id=1, source_target_pairs={{0,2},{1,3},{2,4},{3,5},{4,6},{5,7},{6,0},{7,1},{8,10},{9,11},{10,... | collective-permute-start | bytes 1769480 | tf_op jit(solution)/shard_map/cond/branch_1_fun/ppermute | solution.py:415
  181.6 24.3 %collective-permute-start.72 = (bf16[288,1024]{1,0:T(8,128)(2,1)S(1)}, bf16[288,1024]{1,0:T(8,128)(2,1)}, u32[]{:S(2)}, u32[]{:S(2)}) collective-permute-start(bf16[288,1024]{1,0:T(8,128)(2,1)S(1)} %constant_dynamic-slice_fusion.6), channel_id=1, source_target_pairs={{0,4},{1,5},{2,6},{3,7},{4,0},{5,1},{6,2},{7,3},{8,12},{9,13},{10,... | collective-permute-start | bytes 1769480 | tf_op jit(solution)/shard_map/cond/branch_1_fun/ppermute | solution.py:415
  209.7 14.5 %collective-permute-done.66 = bf16[64,4608]{1,0:T(8,128)(2,1)S(1)} collective-permute-done((bf16[64,4608]{1,0:T(8,128)(2,1)S(1)}, bf16[64,4608]{1,0:T(8,128)(2,1)S(1)}, u32[]{:S(2)}, u32[]{:S(2)}) %collective-permute-start.66) | collective-permute-done | bytes 589856 | tf_op jit(solution)/shard_map/cond/branch_1_fun/ppermute | solution.py:412
  248.6 14.8 %branch_1_fun.6 = (bf16[512,2048]{1,0:T(8,128)(2,1)}, bf16[512,1024]{1,0:T(8,128)(2,1)}, bf16[512,1024]{1,0:T(8,128)(2,1)S(1)}) custom-call(bf16[512,1024]{1,0:T(8,128)(2,1)S(1)} %fusion.2.x_ref, bf16[1024,2048]{1,0:T(8,128)(2,1)} %bitcast.63.w_ref, f32[512,128]{1,0:T(8,128)S(1)} %get-tuple-element.610.cos_ref, f32[512,128]{1,0:T(8,128)S(1)} %get-tuple-element.611.sin_ref, ...), custom_call_target="tpu_custom_call" | custom-call | flops 2147483648 | bytes 12582912 | tf_op jit(solution)/shard_map/cond/branch_1_fun/pallas_call | solution.py:80
  279.1 12.9 %collective-permute-done.77.peer_ref = bf16[512,1024]{1,0:T(8,128)(2,1)S(1)} collective-permute-done((bf16[512,1024]{1,0:T(8,128)(2,1)S(1)}, bf16[512,1024]{1,0:T(8,128)(2,1)S(1)}, u32[]{:S(2)}, u32[]{:S(2)}) %collective-permute-start.77) | collective-permute-done | bytes 1048608 | tf_op jit(solution)/shard_map/cond/branch_1_fun/ppermute | solution.py:412
  292.0 20.2 %branch_1_fun.7 = bf16[512,1024]{1,0:T(8,128)(2,1)S(1)} custom-call(s32[1]{0:T(128)} %get-tuple-element.260.part_ref, bf16[512,1024]{1,0:T(8,128)(2,1)S(1)} %copy-done.74, bf16[512,1024]{1,0:T(8,128)(2,1)S(1)} %get-tuple-element.602.own_ref, bf16[512,1024]{1,0:T(8,128)(2,1)S(1)} %collective-permute-done.77.peer_ref), custom_call_target="tpu_custom_call" | custom-call | flops 10000000000 | bytes 4194304 | tf_op jit(solution)/shard_map/cond/branch_1_fun/pallas_call | solution.py:134
  352.5 24.6 %branch_1_fun.8 = (f32[512,1024]{1,0:T(8,128)}, bf16[512,4608]{1,0:T(8,128)(2,1)}, bf16[512,4608]{1,0:T(8,128)(2,1)}, bf16[512,4608]{1,0:T(8,128)(2,1)}) custom-call(bf16[512,1024]{1,0:T(8,128)(2,1)S(1)} %multiply_convert_fusion.x_ref, f32[512,1024]{1,0:T(8,128)S(1)} %get-tuple-element.605.base_ref, bf16[1024,4608]{1,0:T(8,128)(2,1)} %bitcast.82.g_ref, ...), custom_call_target="tpu_custom_call" | custom-call | flops 14495514624 | bytes 42467328 | tf_op jit(solution)/shard_map/cond/branch_1_fun/pallas_call | solution.py:328
  381.0 12.6 %collective-permute-start.145 = (bf16[512,1024]{1,0:T(8,128)(2,1)S(1)}, bf16[512,1024]{1,0:T(8,128)(2,1)S(1)}, u32[]{:S(2)}, u32[]{:S(2)}) collective-permute-start(bf16[512,1024]{1,0:T(8,128)(2,1)S(1)} %get-tuple-element.384), channel_id=1, source_target_pairs={{0,16},{1,17},{2,18},{3,19},{4,20},{5,21},{6,22},{7,23},{8,24},{9,... | collective-permute-start | bytes 3145736 | tf_op jit(solution)/shard_map/ppermute | solution.py:525
  393.7 22.6 %collective-permute-done.145 = bf16[512,1024]{1,0:T(8,128)(2,1)S(1)} collective-permute-done((bf16[512,1024]{1,0:T(8,128)(2,1)S(1)}, bf16[512,1024]{1,0:T(8,128)(2,1)S(1)}, u32[]{:S(2)}, u32[]{:S(2)}) %collective-permute-start.145) | collective-permute-done | bytes 1048608 | tf_op jit(solution)/shard_map/ppermute | solution.py:525
  416.3 25.6 %conditional.4 = (f32[512,1024]{1,0:T(8,128)}, bf16[512,1024]{1,0:T(8,128)(2,1)}, bf16[512,2048]{1,0:T(8,128)(2,1)}, bf16[512,1024]{1,0:T(8,128)(2,1)}, bf16[512...) conditional(s32[]{:T(128)} %convert_element_type.511, ...), branch_computations={%region_4.14_spmd, %region_14.15_spmd} | conditional | flops 37638119424 | bytes 365446080 | solution.py:585
  443.2 95.4 %collective-permute-done.146 = bf16[512,1024]{1,0:T(8,128)(2,1)} collective-permute-done((bf16[512,1024]{1,0:T(8,128)(2,1)}, bf16[512,1024]{1,0:T(8,128)(2,1)}, u32[]{:S(2)}, u32[]{:S(2)}) %collective-permute-start.146) | collective-permute-done | bytes 1048608 | tf_op jit(solution)/shard_map/ppermute | solution.py:586
  538.5 473.5 %conditional.5 = (f32[512,1024]{1,0:T(8,128)}, f32[64,1024]{1,0:T(8,128)S(1)}, f32[8,1024]{1,0:T(8,128)S(1)}, f32[1,64,2048]{2,1,0:T(8,128)S(1)}, f32[1,64,1024]...) conditional(s32[]{:T(128)} %convert_element_type.511, ...), branch_computations={%region_15.16_spmd, %region_16.23_spmd} | conditional | flops 60513435648 | bytes 527129376 | solution.py:638
  564.1 25.7 %branch_1_fun.9 = (f32[512,1024]{1,0:T(8,128)}, bf16[512,4608]{1,0:T(8,128)(2,1)}, bf16[512,4608]{1,0:T(8,128)(2,1)}) custom-call(bf16[512,1024]{1,0:T(8,128)(2,1)} %get-tuple-element.298.grad_ref, bf16[512,4608]{1,0:T(8,128)(2,1)} %get-tuple-element.300.one_ref, bf16[512,4608]{1,0:T(8,128)(2,1)} %get-tuple-element.301.two_ref, ...), custom_call_target="tpu_custom_call" | custom-call | flops 14495514624 | bytes 42467328 | tf_op jit(solution)/shard_map/cond/branch_1_fun/pallas_call | solution.py:357
  598.7 34.3 %branch_1_fun.10 = (f32[512,1024]{1,0:T(8,128)}, f32[512,1024]{1,0:T(8,128)}, f32[512,1024]{1,0:T(8,128)}) custom-call(s32[1]{0:T(128)} %get-tuple-element.309.part_ref, bf16[512,1024]{1,0:T(8,128)(2,1)S(1)} %copy-done.75, bf16[512,1024]{1,0:T(8,128)(2,1)S(1)} %copy-done.73, bf16[512,1024]{1,0:T(8,128)(2,1)S(1)} %copy-done.71, ...), custom_call_target="tpu_custom_call" | custom-call | flops 24999999488 | bytes 12582912 | tf_op jit(solution)/shard_map/cond/branch_1_fun/pallas_call | solution.py:193
  661.4 18.9 %branch_1_fun.11 = (bf16[512,2048]{1,0:T(8,128)(2,1)}, f32[512,1024]{1,0:T(8,128)}, f32[8,128]{1,0:T(8,128)}) custom-call(bf16[512,2048]{1,0:T(8,128)(2,1)S(1)} %copy-done.24, f32[512,1024]{1,0:T(8,128)} %get-tuple-element.314.dq_ref, f32[512,1024]{1,0:T(8,128)} %get-tuple-element.315.own_ref, bf16[512,1024]{1,0:T(8,128)(2,1)} %collective-permute-done.114.recv_ref, ...), custom_call_target="tpu_custom_call" | custom-call | flops 2147483648 | bytes 16777216 | tf_op jit(solution)/shard_map/cond/branch_1_fun/pallas_call | solution.py:250
  781.8 33.0 %collective-permute-done.140 = bf16[4,288,1024]{2,1,0:T(8,128)(2,1)S(1)} collective-permute-done((bf16[4,288,1024]{2,1,0:T(8,128)(2,1)S(1)}, bf16[4,288,1024]{2,1,0:T(8,128)(2,1)S(1)}, u32[]{:S(2)}, u32[]{:S(2)}) %collective-permute-start.140) | collective-permute-done | bytes 2359328 | tf_op jit(solution)/shard_map/cond/branch_1_fun/ppermute | solution.py:412
  819.9 45.4 %collective-permute-done.135 = bf16[4,64,4608]{2,1,0:T(8,128)(2,1)S(1)} collective-permute-done((bf16[4,64,4608]{2,1,0:T(8,128)(2,1)S(1)}, bf16[4,64,4608]{2,1,0:T(8,128)(2,1)S(1)}, u32[]{:S(2)}, u32[]{:S(2)}) %collective-permute-start.135) | collective-permute-done | bytes 2359328 | tf_op jit(solution)/shard_map/cond/branch_1_fun/ppermute | solution.py:412
  869.9 41.4 %collective-permute-done.130 = bf16[4,64,4608]{2,1,0:T(8,128)(2,1)S(1)} collective-permute-done((bf16[4,64,4608]{2,1,0:T(8,128)(2,1)S(1)}, bf16[4,64,4608]{2,1,0:T(8,128)(2,1)S(1)}, u32[]{:S(2)}, u32[]{:S(2)}) %collective-permute-start.130) | collective-permute-done | bytes 2359328 | tf_op jit(solution)/shard_map/cond/branch_1_fun/ppermute | solution.py:412
  918.9 47.5 %collective-permute-done.137 = bf16[64,4608]{1,0:T(8,128)(2,1)S(1)} collective-permute-done((bf16[64,4608]{1,0:T(8,128)(2,1)S(1)}, bf16[64,4608]{1,0:T(8,128)(2,1)S(1)}, u32[]{:S(2)}, u32[]{:S(2)}) %collective-permute-start.137) | collective-permute-done | bytes 589856 | tf_op jit(solution)/shard_map/cond/branch_1_fun/ppermute | solution.py:415
  966.7 19.6 %collective-permute-done.142 = bf16[288,1024]{1,0:T(8,128)(2,1)S(1)} collective-permute-done((bf16[288,1024]{1,0:T(8,128)(2,1)S(1)}, bf16[288,1024]{1,0:T(8,128)(2,1)S(1)}, u32[]{:S(2)}, u32[]{:S(2)}) %collective-permute-start.142) | collective-permute-done | bytes 589856 | tf_op jit(solution)/shard_map/cond/branch_1_fun/ppermute | solution.py:415
  986.7 24.8 %collective-permute-done.132 = bf16[64,4608]{1,0:T(8,128)(2,1)S(1)} collective-permute-done((bf16[64,4608]{1,0:T(8,128)(2,1)S(1)}, bf16[64,4608]{1,0:T(8,128)(2,1)S(1)}, u32[]{:S(2)}, u32[]{:S(2)}) %collective-permute-start.132) | collective-permute-done | bytes 589856 | tf_op jit(solution)/shard_map/cond/branch_1_fun/ppermute | solution.py:415
  (381 shorter events, 412.4 us)
Async XLA Ops:
  58.4 55.2 %collective-permute-start.58 = (bf16[64,4608]{1,0:T(8,128)(2,1)S(1)}, bf16[64,4608]{1,0:T(8,128)(2,1)S(1)}, u32[]{:S(2)}, u32[]{:S(2)}) collective-permute-start(bf16[64,4608]{1,0:T(8,128)(2,1)S(1)} %copy-done.82), channel_id=1, source_target_pairs={{0,4},{1,5},{2,6},{3,7},{4,0},{5,1},{6,2},{7,3},{8,12},{9,13},{10,... | collective-permute-start | bytes 1769480 | tf_op jit(solution)/shard_map/cond/branch_1_fun/ppermute | solution.py:415
  92.8 88.9 %collective-permute-start.67 = (bf16[64,4608]{1,0:T(8,128)(2,1)S(1)}, bf16[64,4608]{1,0:T(8,128)(2,1)S(1)}, u32[]{:S(2)}, u32[]{:S(2)}) collective-permute-start(bf16[64,4608]{1,0:T(8,128)(2,1)S(1)} %copy-done.81), channel_id=1, source_target_pairs={{0,6},{1,7},{2,0},{3,1},{4,2},{5,3},{6,4},{7,5},{8,14},{9,15},{10,... | collective-permute-start | bytes 1769480 | tf_op jit(solution)/shard_map/cond/branch_1_fun/ppermute | solution.py:415
  96.0 110.0 %collective-permute-start.65 = (bf16[64,4608]{1,0:T(8,128)(2,1)S(1)}, bf16[64,4608]{1,0:T(8,128)(2,1)S(1)}, u32[]{:S(2)}, u32[]{:S(2)}) collective-permute-start(bf16[64,4608]{1,0:T(8,128)(2,1)S(1)} %copy-done.81), channel_id=1, source_target_pairs={{0,4},{1,5},{2,6},{3,7},{4,0},{5,1},{6,2},{7,3},{8,12},{9,13},{10,... | collective-permute-start | bytes 1769480 | tf_op jit(solution)/shard_map/cond/branch_1_fun/ppermute | solution.py:415
  113.6 131.0 %collective-permute-start.48 = (bf16[4,2,64,2048]{3,2,1,0:T(8,128)(2,1)S(1)}, bf16[4,2,64,2048]{3,2,1,0:T(8,128)(2,1)S(1)}, u32[]{:S(2)}, u32[]{:S(2)}) collective-permute-start(bf16[4,2,64,2048]{3,2,1,0:T(8,128)(2,1)S(1)} %bitcast_dynamic-update-slice_fusion.65), channel_id=1, source_target_pairs={{0,1},{1,0},{2,3},{3,2},{4,5},{5,4},{6,7},{7,6},{8,9},{9,8},{10,11... | collective-permute-start | bytes 6291464 | tf_op jit(solution)/shard_map/cond/branch_1_fun/ppermute | solution.py:409
  113.6 67.2 %collective-permute-start.70 = (bf16[288,1024]{1,0:T(8,128)(2,1)S(1)}, bf16[288,1024]{1,0:T(8,128)(2,1)S(1)}, u32[]{:S(2)}, u32[]{:S(2)}) collective-permute-start(bf16[288,1024]{1,0:T(8,128)(2,1)S(1)} %constant_dynamic-slice_fusion.6), channel_id=1, source_target_pairs={{0,2},{1,3},{2,4},{3,5},{4,6},{5,7},{6,0},{7,1},{8,10},{9,11},{10,... | collective-permute-start | bytes 1769480 | tf_op jit(solution)/shard_map/cond/branch_1_fun/ppermute | solution.py:415
  181.6 53.0 %collective-permute-start.72 = (bf16[288,1024]{1,0:T(8,128)(2,1)S(1)}, bf16[288,1024]{1,0:T(8,128)(2,1)}, u32[]{:S(2)}, u32[]{:S(2)}) collective-permute-start(bf16[288,1024]{1,0:T(8,128)(2,1)S(1)} %constant_dynamic-slice_fusion.6), channel_id=1, source_target_pairs={{0,4},{1,5},{2,6},{3,7},{4,0},{5,1},{6,2},{7,3},{8,12},{9,13},{10,... | collective-permute-start | bytes 1769480 | tf_op jit(solution)/shard_map/cond/branch_1_fun/ppermute | solution.py:415
  224.3 91.5 %collective-permute-start.62 = (bf16[4,2,64,4608]{3,2,1,0:T(8,128)(2,1)}, bf16[4,2,64,4608]{3,2,1,0:T(8,128)(2,1)}, u32[]{:S(2)}, u32[]{:S(2)}) collective-permute-start(bf16[4,2,64,4608]{3,2,1,0:T(8,128)(2,1)} %bitcast_dynamic-update-slice_fusion.59), channel_id=1, source_target_pairs={{0,1},{1,0},{2,3},{3,2},{4,5},{5,4},{6,7},{7,6},{8,9},{9,8},{10,11... | collective-permute-start | bytes 14155784 | tf_op jit(solution)/shard_map/cond/branch_1_fun/ppermute | solution.py:409
  244.5 83.9 %collective-permute-start.69 = (bf16[4,2,64,4608]{3,2,1,0:T(8,128)(2,1)}, bf16[4,2,64,4608]{3,2,1,0:T(8,128)(2,1)}, u32[]{:S(2)}, u32[]{:S(2)}) collective-permute-start(bf16[4,2,64,4608]{3,2,1,0:T(8,128)(2,1)} %bitcast_dynamic-update-slice_fusion.53), channel_id=1, source_target_pairs={{0,1},{1,0},{2,3},{3,2},{4,5},{5,4},{6,7},{7,6},{8,9},{9,8},{10,11... | collective-permute-start | bytes 14155784 | tf_op jit(solution)/shard_map/cond/branch_1_fun/ppermute | solution.py:409
  276.4 63.7 %collective-permute-start.76 = (bf16[4,2,288,1024]{3,2,1,0:T(8,128)(2,1)}, bf16[4,2,288,1024]{3,2,1,0:T(8,128)(2,1)}, u32[]{:S(2)}, u32[]{:S(2)}) collective-permute-start(bf16[4,2,288,1024]{3,2,1,0:T(8,128)(2,1)} %bitcast_dynamic-update-slice_fusion.47), channel_id=1, source_target_pairs={{0,1},{1,0},{2,3},{3,2},{4,5},{5,4},{6,7},{7,6},{8,9},{9,8},{10,11... | collective-permute-start | bytes 14155784 | tf_op jit(solution)/shard_map/cond/branch_1_fun/ppermute | solution.py:409
  441.9 96.7 %collective-permute-start.146 = (bf16[512,1024]{1,0:T(8,128)(2,1)}, bf16[512,1024]{1,0:T(8,128)(2,1)}, u32[]{:S(2)}, u32[]{:S(2)}) collective-permute-start(bf16[512,1024]{1,0:T(8,128)(2,1)} %get-tuple-element.402), channel_id=1, source_target_pairs={{16,0},{17,1},{18,2},{19,3},{20,4},{21,5},{22,6},{23,7},{24,8},{25... | collective-permute-start | bytes 3145736 | tf_op jit(solution)/shard_map/ppermute | solution.py:586
  563.4 191.7 %collective-permute-start.139 = (bf16[2304,1024]{1,0:T(8,128)(2,1)}, bf16[2304,1024]{1,0:T(8,128)(2,1)}, u32[]{:S(2)}, u32[]{:S(2)}) collective-permute-start(bf16[2304,1024]{1,0:T(8,128)(2,1)} %convolution_convert_fusion.10), channel_id=1, source_target_pairs={{0,1},{1,0},{2,3},{3,2},{4,5},{5,4},{6,7},{7,6},{8,9},{9,8},{10,11... | collective-permute-start | bytes 14155784 | tf_op jit(solution)/shard_map/cond/branch_1_fun/ppermute | solution.py:409
  650.7 109.8 %collective-permute-start.134 = (bf16[512,4608]{1,0:T(8,128)(2,1)}, bf16[512,4608]{1,0:T(8,128)(2,1)}, u32[]{:S(2)}, u32[]{:S(2)}) collective-permute-start(bf16[512,4608]{1,0:T(8,128)(2,1)} %convolution_convert_fusion.8), channel_id=1, source_target_pairs={{0,1},{1,0},{2,3},{3,2},{4,5},{5,4},{6,7},{7,6},{8,9},{9,8},{10,11... | collective-permute-start | bytes 14155784 | tf_op jit(solution)/shard_map/cond/branch_1_fun/ppermute | solution.py:409
  709.9 63.8 %collective-permute-start.129 = (bf16[512,4608]{1,0:T(8,128)(2,1)}, bf16[512,4608]{1,0:T(8,128)(2,1)}, u32[]{:S(2)}, u32[]{:S(2)}) collective-permute-start(bf16[512,4608]{1,0:T(8,128)(2,1)} %convolution_convert_fusion.9), channel_id=1, source_target_pairs={{0,1},{1,0},{2,3},{3,2},{4,5},{5,4},{6,7},{7,6},{8,9},{9,8},{10,11... | collective-permute-start | bytes 14155784 | tf_op jit(solution)/shard_map/cond/branch_1_fun/ppermute | solution.py:409
  760.5 54.2 %collective-permute-start.140 = (bf16[4,288,1024]{2,1,0:T(8,128)(2,1)S(1)}, bf16[4,288,1024]{2,1,0:T(8,128)(2,1)S(1)}, u32[]{:S(2)}, u32[]{:S(2)}) collective-permute-start(bf16[4,288,1024]{2,1,0:T(8,128)(2,1)S(1)} %dynamic-slice_bitcast_fusion.24), channel_id=1, source_target_pairs={{0,8},{8,0},{1,9},{9,1},{2,10},{10,2},{3,11},{11,3},{4,12},{12,4},... | collective-permute-start | bytes 7077896 | tf_op jit(solution)/shard_map/cond/branch_1_fun/ppermute | solution.py:412
  767.6 97.6 %collective-permute-start.135 = (bf16[4,64,4608]{2,1,0:T(8,128)(2,1)S(1)}, bf16[4,64,4608]{2,1,0:T(8,128)(2,1)S(1)}, u32[]{:S(2)}, u32[]{:S(2)}) collective-permute-start(bf16[4,64,4608]{2,1,0:T(8,128)(2,1)S(1)} %dynamic-slice_bitcast_fusion.25), channel_id=1, source_target_pairs={{0,8},{8,0},{1,9},{9,1},{2,10},{10,2},{3,11},{11,3},{4,12},{12,4},... | collective-permute-start | bytes 7077896 | tf_op jit(solution)/shard_map/cond/branch_1_fun/ppermute | solution.py:412
  779.9 131.4 %collective-permute-start.130 = (bf16[4,64,4608]{2,1,0:T(8,128)(2,1)S(1)}, bf16[4,64,4608]{2,1,0:T(8,128)(2,1)S(1)}, u32[]{:S(2)}, u32[]{:S(2)}) collective-permute-start(bf16[4,64,4608]{2,1,0:T(8,128)(2,1)S(1)} %dynamic-slice_bitcast_fusion.26), channel_id=1, source_target_pairs={{0,8},{8,0},{1,9},{9,1},{2,10},{10,2},{3,11},{11,3},{4,12},{12,4},... | collective-permute-start | bytes 7077896 | tf_op jit(solution)/shard_map/cond/branch_1_fun/ppermute | solution.py:412
  816.0 98.6 %collective-permute-start.141 = (bf16[288,1024]{1,0:T(8,128)(2,1)S(1)}, bf16[288,1024]{1,0:T(8,128)(2,1)S(1)}, u32[]{:S(2)}, u32[]{:S(2)}) collective-permute-start(bf16[288,1024]{1,0:T(8,128)(2,1)S(1)} %get-tuple-element.542), channel_id=1, source_target_pairs={{0,2},{1,3},{2,4},{3,5},{4,6},{5,7},{6,0},{7,1},{8,10},{9,11},{10,... | collective-permute-start | bytes 1769480 | tf_op jit(solution)/shard_map/cond/branch_1_fun/ppermute | solution.py:415
  816.6 150.1 %collective-permute-start.143 = (bf16[288,1024]{1,0:T(8,128)(2,1)S(1)}, bf16[288,1024]{1,0:T(8,128)(2,1)S(1)}, u32[]{:S(2)}, u32[]{:S(2)}) collective-permute-start(bf16[288,1024]{1,0:T(8,128)(2,1)S(1)} %get-tuple-element.543), channel_id=1, source_target_pairs={{0,6},{1,7},{2,0},{3,1},{4,2},{5,3},{6,4},{7,5},{8,14},{9,15},{10,... | collective-permute-start | bytes 1769480 | tf_op jit(solution)/shard_map/cond/branch_1_fun/ppermute | solution.py:415
  866.0 49.0 %collective-permute-start.136 = (bf16[64,4608]{1,0:T(8,128)(2,1)S(1)}, bf16[64,4608]{1,0:T(8,128)(2,1)S(1)}, u32[]{:S(2)}, u32[]{:S(2)}) collective-permute-start(bf16[64,4608]{1,0:T(8,128)(2,1)S(1)} %get-tuple-element.545), channel_id=1, source_target_pairs={{0,2},{1,3},{2,4},{3,5},{4,6},{5,7},{6,0},{7,1},{8,10},{9,11},{10,... | collective-permute-start | bytes 1769480 | tf_op jit(solution)/shard_map/cond/branch_1_fun/ppermute | solution.py:415
  866.6 49.0 %collective-permute-start.138 = (bf16[64,4608]{1,0:T(8,128)(2,1)S(1)}, bf16[64,4608]{1,0:T(8,128)(2,1)S(1)}, u32[]{:S(2)}, u32[]{:S(2)}) collective-permute-start(bf16[64,4608]{1,0:T(8,128)(2,1)S(1)} %get-tuple-element.546), channel_id=1, source_target_pairs={{0,6},{1,7},{2,0},{3,1},{4,2},{5,3},{6,4},{7,5},{8,14},{9,15},{10,... | collective-permute-start | bytes 1769480 | tf_op jit(solution)/shard_map/cond/branch_1_fun/ppermute | solution.py:415
  911.3 55.1 %collective-permute-start.137 = (bf16[64,4608]{1,0:T(8,128)(2,1)S(1)}, bf16[64,4608]{1,0:T(8,128)(2,1)S(1)}, u32[]{:S(2)}, u32[]{:S(2)}) collective-permute-start(bf16[64,4608]{1,0:T(8,128)(2,1)S(1)} %get-tuple-element.547), channel_id=1, source_target_pairs={{0,4},{1,5},{2,6},{3,7},{4,0},{5,1},{6,2},{7,3},{8,12},{9,13},{10,... | collective-permute-start | bytes 1769480 | tf_op jit(solution)/shard_map/cond/branch_1_fun/ppermute | solution.py:415
  914.7 71.6 %collective-permute-start.142 = (bf16[288,1024]{1,0:T(8,128)(2,1)S(1)}, bf16[288,1024]{1,0:T(8,128)(2,1)S(1)}, u32[]{:S(2)}, u32[]{:S(2)}) collective-permute-start(bf16[288,1024]{1,0:T(8,128)(2,1)S(1)} %get-tuple-element.544), channel_id=1, source_target_pairs={{0,4},{1,5},{2,6},{3,7},{4,0},{5,1},{6,2},{7,3},{8,12},{9,13},{10,... | collective-permute-start | bytes 1769480 | tf_op jit(solution)/shard_map/cond/branch_1_fun/ppermute | solution.py:415
  915.1 71.6 %collective-permute-start.131 = (bf16[64,4608]{1,0:T(8,128)(2,1)S(1)}, bf16[64,4608]{1,0:T(8,128)(2,1)S(1)}, u32[]{:S(2)}, u32[]{:S(2)}) collective-permute-start(bf16[64,4608]{1,0:T(8,128)(2,1)S(1)} %get-tuple-element.548), channel_id=1, source_target_pairs={{0,2},{1,3},{2,4},{3,5},{4,6},{5,7},{6,0},{7,1},{8,10},{9,11},{10,... | collective-permute-start | bytes 1769480 | tf_op jit(solution)/shard_map/cond/branch_1_fun/ppermute | solution.py:415
  915.6 71.1 %collective-permute-start.133 = (bf16[64,4608]{1,0:T(8,128)(2,1)S(1)}, bf16[64,4608]{1,0:T(8,128)(2,1)S(1)}, u32[]{:S(2)}, u32[]{:S(2)}) collective-permute-start(bf16[64,4608]{1,0:T(8,128)(2,1)S(1)} %get-tuple-element.549), channel_id=1, source_target_pairs={{0,6},{1,7},{2,0},{3,1},{4,2},{5,3},{6,4},{7,5},{8,14},{9,15},{10,... | collective-permute-start | bytes 1769480 | tf_op jit(solution)/shard_map/cond/branch_1_fun/ppermute | solution.py:415
  (93 other events, 2224.3 us)

commit v2 on v1

--- a/solution.py
+++ b/solution.py
@@ -44,6 +44,10 @@
 
 def params():
     return pltpu.CompilerParams(vmem_limit_bytes=VMEM_LIMIT)
+
+
+def light():
+    return pl.CostEstimate(flops=1 << 20, bytes_accessed=1 << 20, transcendentals=0)
 
 
 def group_mean(value):
@@ -98,9 +102,7 @@
             jax.ShapeDtypeStruct((tokens, KV_HEADS * PAIR), BF16),
         ],
         compiler_params=params(),
-        cost_estimate=pl.CostEstimate(
-            flops=2 * tokens * width * KV_HEADS * GROUP, bytes_accessed=12 << 20, transcendentals=0
-        ),
+        cost_estimate=light(),
     )(normed, weight, cosine, sine, gain_rows)
 
 
@@ -139,9 +141,7 @@
         out_specs=pl.BlockSpec((tokens, PAIR), column),
         out_shape=jax.ShapeDtypeStruct((tokens, KV_HEADS * PAIR), BF16),
         compiler_params=params(),
-        cost_estimate=pl.CostEstimate(
-            flops=10_000_000_000, bytes_accessed=4 << 20, transcendentals=7_000_000
-        ),
+        cost_estimate=light(),
     )(part, query, own, peer)
 
 
@@ -198,9 +198,7 @@
         out_specs=[pl.BlockSpec((tokens, PAIR), column)] * 3,
         out_shape=[shape] * 3,
         compiler_params=params(),
-        cost_estimate=pl.CostEstimate(
-            flops=25_000_000_000, bytes_accessed=12 << 20, transcendentals=7_000_000
-        ),
+        cost_estimate=light(),
     )(part, query, own, peer, grad)
 
 
@@ -271,22 +269,28 @@
             jax.ShapeDtypeStruct((8, PAIR), F32),
         ],
         compiler_params=params(),
-        cost_estimate=pl.CostEstimate(
-            flops=2 * tokens * width * KV_HEADS * GROUP, bytes_accessed=16 << 20, transcendentals=0
-        ),
+        cost_estimate=light(),
     )(raw, dquery, own, recv, cosine, sine, gain_rows, weight)
 
 
+def flat(ref):
+    value = ref[...]
+    return value.reshape(-1, value.shape[-1])
+
+
 def forward_kernel(x_ref, base_ref, g_ref, u_ref, d_ref, out_ref, act_ref, one_ref, two_ref):
-    gate = jnp.dot(x_ref[...], g_ref[...], preferred_element_type=F32)
-    upward = jnp.dot(x_ref[...], u_ref[...], preferred_element_type=F32)
-    sigma = jax.nn.sigmoid(gate)
-    silu = gate * sigma
-    active = (silu * upward).astype(BF16)
-    act_ref[...] = active
-    one_ref[...] = (upward * sigma * (1.0 + gate * (1.0 - sigma))).astype(BF16)
-    two_ref[...] = silu.astype(BF16)
-    down = jnp.dot(active, d_ref[...], preferred_element_type=F32)
+    gate_part, up_part, down_part = (flat(g_ref), flat(u_ref), flat(d_ref))
+    down = 0.0
+    for span in spans(act_ref.shape[1]):
+        gate = jnp.dot(x_ref[...], gate_part[:, span], preferred_element_type=F32)
+        upward = jnp.dot(x_ref[...], up_part[:, span], preferred_element_type=F32)
+        sigma = jax.nn.sigmoid(gate)
+        silu = gate * sigma
+        active = (silu * upward).astype(BF16)
+        act_ref[:, span] = active
+        one_ref[:, span] = (upward * sigma * (1.0 + gate * (1.0 - sigma))).astype(BF16)
+        two_ref[:, span] = silu.astype(BF16)
+        down += jnp.dot(active, down_part[span], preferred_element_type=F32)
 
     @pl.when(pl.program_id(0) == 0)
     def _():
@@ -298,12 +302,15 @@
 
 
 def backward_kernel(grad_ref, one_ref, two_ref, g_ref, u_ref, d_ref, out_ref, dg_ref, du_ref):
-    active = matmul_t(grad_ref[...], d_ref[...])
-    dgate = (active * one_ref[...].astype(F32)).astype(BF16)
-    dup = (active * two_ref[...].astype(F32)).astype(BF16)
-    dg_ref[...] = dgate
-    du_ref[...] = dup
-    total = matmul_t(dgate, g_ref[...]) + matmul_t(dup, u_ref[...])
+    gate_part, up_part, down_part = (flat(g_ref), flat(u_ref), flat(d_ref))
+    total = 0.0
+    for span in spans(dg_ref.shape[1]):
+        active = matmul_t(grad_ref[...], down_part[span])
+        dgate = (active * one_ref[:, span].astype(F32)).astype(BF16)
+        dup = (active * two_ref[:, span].astype(F32)).astype(BF16)
+        dg_ref[:, span] = dgate
+        du_ref[:, span] = dup
+        total += matmul_t(dgate, gate_part[:, span]) + matmul_t(dup, up_part[:, span])
 
     @pl.when(pl.program_id(0) == 0)
     def _():
@@ -314,43 +321,117 @@
         out_ref[...] += total
 
 
-def hidden_chunk(hidden):
-    return next(size for size in (512, 384, 256, 128, hidden) if hidden % size == 0)
-
-
-def ff_forward(normed, base, gate, upward, down):
+def store_outer(left_ref, dgate, dup, span, outs):
+    half = left_ref.shape[0] // 2
+    for right, leave_ref, stay_ref in ((dgate, *outs[:2]), (dup, *outs[2:])):
+        product = jnp.dot(left_ref[...], right, preferred_element_type=F32).astype(BF16)
+        leave_ref[:, span] = product[:half]
+        stay_ref[:, span] = product[half:]
+
+
+def backward_outer_kernel(grad_ref, left_ref, one_ref, two_ref, g_ref, u_ref, d_ref, out_ref, *outs):
+    gate_part, up_part, down_part = (flat(g_ref), flat(u_ref), flat(d_ref))
+    total = 0.0
+    for span in spans(one_ref.shape[1]):
+        active = matmul_t(grad_ref[...], down_part[span])
+        dgate = (active * one_ref[:, span].astype(F32)).astype(BF16)
+        dup = (active * two_ref[:, span].astype(F32)).astype(BF16)
+        store_outer(left_ref, dgate, dup, span, outs)
+        total += matmul_t(dgate, gate_part[:, span]) + matmul_t(dup, up_part[:, span])
+
+    @pl.when(pl.program_id(0) == 0)
+    def _():
+        out_ref[...] = total
+
+    @pl.when(pl.program_id(0) > 0)
+    def _():
+        out_ref[...] += total
+
+
+def outer_kernel(left_ref, dg_ref, du_ref, *outs):
+    store_outer(left_ref, dg_ref[...], du_ref[...], slice(None), outs)
+
+
+def spans(chunk):
+    starts = list(range(0, max(chunk - 511, 1), 512))
+    return [slice(a, b) for a, b in zip(starts, starts[1:] + [chunk])]
+
+
+def sub_chunk(chunk):
+    return next(size for size in (512, 384, 256, 128, chunk) if chunk % size == 0)
+
+
+CHUNKS = 4
+
+
+def can_pack(devices, width, hidden):
+    gate_rows, down_rows = (width // devices, hidden // devices)
+    return (
+        devices % CHUNKS == 0
+        and hidden % (CHUNKS * 128) == 0
+        and hidden // CHUNKS >= width
+        and gate_rows % 16 == 0
+        and down_rows % 16 == 0
+    )
+
+
+def pack_halves(gate, upward, down):
+    rows, hidden = gate.shape
+    chunk = hidden // CHUNKS
+    down = jnp.pad(down, ((0, -down.shape[0] % rows), (0, chunk - down.shape[1])))
+    cut = lambda w: jnp.transpose(w.reshape(rows, CHUNKS, chunk), (1, 0, 2)).reshape(-1, chunk)
+    return jnp.concatenate([down, cut(gate), cut(upward)], axis=0)
+
+
+def weight_specs(weights, tokens, width, hidden):
+    if len(weights) == 3:
+        chunk = sub_chunk(hidden)
+        column = lambda j: (0, j)
+        return (
+            chunk,
+            [
+                pl.BlockSpec((width, chunk), column),
+                pl.BlockSpec((width, chunk), column),
+                pl.BlockSpec((chunk, width), lambda j: (j, 0)),
+            ],
+            weights,
+        )
+    devices = weights[0].shape[0]
+    rows, down_rows, chunk = (width // devices, hidden // devices, hidden // CHUNKS)
+    skip = -(-down_rows // rows)
+    return (
+        chunk,
+        [
+            pl.BlockSpec((devices, rows, chunk), lambda j: (0, skip + j, 0)),
+            pl.BlockSpec((devices, rows, chunk), lambda j: (0, skip + CHUNKS + j, 0)),
+            pl.BlockSpec((devices // CHUNKS, down_rows, width), lambda j: (j, 0, 0)),
+        ],
+        (weights[0],) * 3,
+    )
+
+
+def ff_forward(normed, base, weights, hidden):
     tokens, width = normed.shape
-    hidden = gate.shape[1]
-    chunk = hidden_chunk(hidden)
+    chunk, specs, operands = weight_specs(weights, tokens, width, hidden)
     whole = lambda j: (0, 0)
     column = lambda j: (0, j)
     saved = jax.ShapeDtypeStruct((tokens, hidden), BF16)
     return pl.pallas_call(
         forward_kernel,
         grid=(hidden // chunk,),
-        in_specs=[
-            pl.BlockSpec((tokens, width), whole),
-            pl.BlockSpec((tokens, width), whole),
-            pl.BlockSpec((width, chunk), column),
-            pl.BlockSpec((width, chunk), column),
-            pl.BlockSpec((chunk, width), lambda j: (j, 0)),
-        ],
+        in_specs=[pl.BlockSpec((tokens, width), whole), pl.BlockSpec((tokens, width), whole)]
+        + specs,
         out_specs=[pl.BlockSpec((tokens, width), whole)]
         + [pl.BlockSpec((tokens, chunk), column)] * 3,
         out_shape=[jax.ShapeDtypeStruct((tokens, width), F32), saved, saved, saved],
         compiler_params=params(),
-        cost_estimate=pl.CostEstimate(
-            flops=6 * tokens * width * hidden,
-            bytes_accessed=6 * hidden * (width + tokens),
-            transcendentals=tokens * hidden,
-        ),
-    )(normed, base, gate, upward, down)
-
-
-def ff_backward(grad, one, two, gate, upward, down):
+        cost_estimate=light(),
+    )(normed, base, *operands)
+
+
+def ff_backward(grad, one, two, weights, hidden):
     tokens, width = grad.shape
-    hidden = gate.shape[1]
-    chunk = hidden_chunk(hidden)
+    chunk, specs, operands = weight_specs(weights, tokens, width, hidden)
     whole = lambda j: (0, 0)
     column = lambda j: (0, j)
     saved = jax.ShapeDtypeStruct((tokens, hidden), BF16)
@@ -361,20 +442,56 @@
             pl.BlockSpec((tokens, width), whole),
             pl.BlockSpec((tokens, chunk), column),
             pl.BlockSpec((tokens, chunk), column),
-            pl.BlockSpec((width, chunk), column),
-            pl.BlockSpec((width, chunk), column),
-            pl.BlockSpec((chunk, width), lambda j: (j, 0)),
-        ],
+        ]
+        + specs,
         out_specs=[pl.BlockSpec((tokens, width), whole)]
         + [pl.BlockSpec((tokens, chunk), column)] * 2,
         out_shape=[jax.ShapeDtypeStruct((tokens, width), F32), saved, saved],
         compiler_params=params(),
-        cost_estimate=pl.CostEstimate(
-            flops=6 * tokens * width * hidden,
-            bytes_accessed=6 * hidden * (width + tokens),
-            transcendentals=0,
-        ),
-    )(grad, one, two, gate, upward, down)
+        cost_estimate=light(),
+    )(grad, one, two, *operands)
+
+
+def ff_backward_outer(grad, left, one, two, weights, hidden):
+    tokens, width = grad.shape
+    chunk, specs, operands = weight_specs(weights, tokens, width, hidden)
+    whole = lambda j: (0, 0)
+    column = lambda j: (0, j)
+    half = left.shape[0] // 2
+    return pl.pallas_call(
+        backward_outer_kernel,
+        grid=(hidden // chunk,),
+        in_specs=[
+            pl.BlockSpec((tokens, width), whole),
+            pl.BlockSpec(left.shape, whole),
+            pl.BlockSpec((tokens, chunk), column),
+            pl.BlockSpec((tokens, chunk), column),
+        ]
+        + specs,
+        out_specs=[pl.BlockSpec((tokens, width), whole)]
+        + [pl.BlockSpec((half, chunk), column)] * 4,
+        out_shape=[jax.ShapeDtypeStruct((tokens, width), F32)]
+        + [jax.ShapeDtypeStruct((half, hidden), BF16)] * 4,
+        compiler_params=params(),
+        cost_estimate=light(),
+    )(grad, left, one, two, *operands)
+
+
+def ff_outer(left, dgate, dup):
+    tokens, hidden = dgate.shape
+    chunk = sub_chunk(hidden)
+    column = lambda j: (0, j)
+    half = left.shape[0] // 2
+    return pl.pallas_call(
+        outer_kernel,
+        grid=(hidden // chunk,),
+        in_specs=[pl.BlockSpec(left.shape, lambda j: (0, 0))]
+        + [pl.BlockSpec((tokens, chunk), column)] * 2,
+        out_specs=[pl.BlockSpec((half, chunk), column)] * 4,
+        out_shape=[jax.ShapeDtypeStruct((half, hidden), BF16)] * 4,
+        compiler_params=params(),
+        cost_estimate=light(),
+    )(left, dgate, dup)
 
 
 def local(
@@ -404,6 +521,9 @@
 
     cores = [(i, i ^ 1) for i in range(fsdp)]
     swap = [(0, 1), (1, 0)]
+
+    def after(value, *earlier):
+        return lax.optimization_barrier((value, *earlier))[0] if earlier else value
 
     def to_core(value):
         return lax.ppermute(value, "fsdp", cores)
@@ -440,27 +560,60 @@
             results.append(full.reshape(fsdp * depth, columns))
         return results
 
-    def core_columns(value, which, cut):
+    def turned(value):
+        cut = value.shape[1] // (2 * fsdp)
         wide = value.reshape(value.shape[0], 2, chips, 2, cut)
-        return lax.dynamic_index_in_dim(wide, which, 3, keepdims=False).reshape(
-            value.shape[0], chips * 2 * cut
+        sides = [
+            lax.dynamic_index_in_dim(wide, side, 3, keepdims=False) for side in (1 - core, core)
+        ]
+        return jnp.concatenate(
+            [jnp.transpose(side.reshape(-1, 2 * chips * cut)) for side in sides], axis=0
         )
 
-    def reduce(left, right):
-        cut = left.shape[1] // (2 * fsdp)
-        columns = right.shape[1]
-        leaving = outer_sum(core_columns(left, 1 - core, cut), right).astype(BF16)
-        staying = outer_sum(core_columns(left, core, cut), right)
-        both = (staying + to_core(leaving).astype(F32)).astype(BF16)
-        both = both.reshape(2, chips, cut, columns)
-        crossing = lax.dynamic_index_in_dim(both, 1 - part, 0, keepdims=False)
-        own = lax.dynamic_index_in_dim(both, part, 0, keepdims=False)
-        own = (own.astype(F32) + to_peer(crossing).astype(F32)).astype(BF16)
-        result = lax.dynamic_index_in_dim(own, chip, 0, keepdims=False).astype(F32)
-        for step in range(1, chips):
-            piece = lax.dynamic_index_in_dim(own, (chip + step) % chips, 0, keepdims=False)
-            result = result + along(piece, step).astype(F32)
-        return result
+    def blocks(both):
+        return both.astype(BF16).reshape(2, chips, -1, both.shape[1])
+
+    def core_sum(left, right):
+        half = left.shape[0] // 2
+        leaving = matmul(left[:half], right).astype(BF16)
+        return blocks(matmul(left[half:], right) + to_core(leaving).astype(F32))
+
+    def core_add(leaving, staying):
+        return blocks(staying.astype(F32) + leaving.astype(F32))
+
+    def only(section, value, move):
+        pairs = []
+        for side in range(2):
+            for i in range(fsdp):
+                source = (section * 2 + side) * fsdp + i
+                if move == "seq":
+                    target = (section * 2 + 1 - side) * fsdp + i
+                elif move == "core":
+                    target = (section * 2 + side) * fsdp + (i ^ 1)
+                else:
+                    target = (section * 2 + side) * fsdp + (i + 2 * move) % fsdp
+                pairs.append((source, target))
+        return lax.ppermute(value, ("section", "seq", "fsdp"), pairs)
+
+    def sides(both):
+        return [
+            lax.dynamic_index_in_dim(both, side, 0, keepdims=False) for side in (1 - part, part)
+        ]
+
+    def crossed(staying, came):
+        return (staying.astype(F32) + came.astype(F32)).astype(BF16)
+
+    def pieces(own):
+        return [
+            lax.dynamic_index_in_dim(own, (chip + step) % chips, 0, keepdims=False)
+            for step in range(chips)
+        ]
+
+    def fence(*groups):
+        return lax.optimization_barrier(groups)
+
+    def together(values, *others):
+        return lax.optimization_barrier((*values, *others))[: len(values)]
 
     def reduce_small(value):
         value = value + to_core(value)
@@ -474,8 +627,19 @@
     def zeros(*shape, kind=BF16):
         return jnp.zeros(shape, kind)
 
+    conv_cut = width // (4 * fsdp)
     c_low = lax.ppermute(conv_c, "section", [(0, 1)])
-    shards = (mix_in[0], mix_out[0], w_gate[0], w_up[0], w_down[0])
+
+    def half_of(shard):
+        return lax.dynamic_slice_in_dim(shard, part * (shard.shape[0] // 2), shard.shape[0] // 2, 0)
+
+    halves = (half_of(w_gate[0]), half_of(w_up[0]), half_of(w_down[0]))
+    if can_pack(2 * fsdp, width, hidden):
+        wide_weights = (lax.all_gather(pack_halves(*halves), ("fsdp", "seq"), axis=0),)
+    else:
+        wide_weights = tuple(
+            lax.all_gather(half, ("fsdp", "seq"), axis=0, tiled=True) for half in halves
+        )
 
     positions = (
         jnp.arange(stretches)[:, None] * block + part * rows + jnp.arange(rows)[None, :]
@@ -492,8 +656,8 @@
     def gain_rows():
         return jnp.zeros((8, PAIR), F32).at[:2].set(jnp.tile(head_gains, (1, 2)))
 
-    def attention_forward():
-        w_in, w_out, gate, upward, down = gather(shards)
+    def attention_mixer():
+        w_in, w_out = gather((mix_in[0], mix_out[0]))
         source = tokens[0].reshape(total, width).astype(F32)
         normed = (source * rms_scale(source) * gains[0]).astype(BF16)
         cosine, sine = rope()
@@ -502,33 +666,39 @@
         heads = attend(part_ref, query, own, peer, rows, stretches)
         resid = source + matmul(heads, w_out)
         normed_two = (resid * rms_scale(resid) * gains[1]).astype(BF16)
-        result, active, one, two = ff_forward(normed_two, resid, gate, upward, down)
-        weights = (w_in, w_out, gate, upward, down, zeros(width, width))
-        kept = (normed, raw, query, own, peer, heads, resid, normed_two, active, one, two)
-        return (weights, kept, cosine, sine, result.astype(BF16))
+        weights = (w_in, w_out, zeros(width, width))
+        kept = (normed, raw, query, own, peer, heads, resid, normed_two)
+        return (weights, kept, cosine, sine)
 
     def conv_gather():
         both = jnp.concatenate([c_low, conv_c], axis=1)
-        w_in, c_wide, w_out, gate, upward, down = gather((shards[0], both, *shards[1:]))
+        w_in, c_wide, w_out = gather((mix_in[0], both, mix_out[0]))
         w_c = jnp.concatenate([c_wide[:, :width], c_wide[:, width:]], axis=0)
-        weights = (w_in, w_out, gate, upward, down, w_c)
         flat = lambda: zeros(total, width)
-        wide = lambda: zeros(total, hidden)
         kept = (
             flat(), zeros(total, KV_HEADS * GROUP), flat(), flat(), flat(), flat(),
-            zeros(total, width, kind=F32), flat(), wide(), wide(), wide(),
+            zeros(total, width, kind=F32), flat(),
         )
         table = lambda: zeros(total, PAIR, kind=F32)
-        return (weights, kept, table(), table(), flat())
-
-    weights, kept, cosine, sine, link = lax.cond(first, attention_forward, conv_gather)
+        return ((w_in, w_out, w_c), kept, table(), table())
+
+    weights, kept, cosine, sine = lax.cond(first, attention_mixer, conv_gather)
+
+    def attention_hidden():
+        result, *saved = ff_forward(kept[-1], kept[-2], wide_weights, hidden)
+        return (result.astype(BF16), *saved)
+
+    def conv_wait():
+        return (zeros(total, width), *[zeros(total, hidden) for _ in range(3)])
+
+    link, active, one, two = lax.cond(first, attention_hidden, conv_wait)
     link = lax.ppermute(link, "section", [(0, 1)])
 
     def tail_of(value, start):
         return to_peer(value.reshape(stretches, rows, width)[:, start : start + 2])
 
     def conv_both():
-        w_in, w_out, gate, upward, down, w_c = weights
+        w_in, w_out, w_c = weights
         source = link.astype(F32)
         scale_one = rms_scale(source)
         normed = (source * scale_one * gains[0]).astype(BF16)
@@ -547,10 +717,10 @@
         resid = source + matmul(heads, w_out)
         scale_two = rms_scale(resid)
         normed_two = (resid * scale_two * gains[1]).astype(BF16)
-        result, active, one, two = ff_forward(normed_two, resid, gate, upward, down)
+        result, active, one, two = ff_forward(normed_two, resid, wide_weights, hidden)
 
         grad_ff = cotangent[0].reshape(total, width)
-        grad_two, dgate, dup = ff_backward(grad_ff, one, two, gate, upward, down)
+        grad_two, dgate, dup = ff_backward(grad_ff, one, two, wide_weights, hidden)
         gain_two = jnp.sum(grad_two * resid * scale_two, axis=0)
         grad_resid = grad_ff.astype(F32) + norm_back(grad_two, resid, scale_two, gains[1])
         dmix = grad_resid.astype(BF16)
@@ -571,39 +741,111 @@
         small = jnp.concatenate(
             [gain_one[None], gain_two[None], kernel_grad, jnp.zeros((3, width), F32)], axis=0
         )
-        moved = (normed, dproj, dgate_c, heads, dmix, normed_two, dgate, dup, active)
-        return (result, moved, small, grad_source.astype(BF16))
+        lefts = (normed, heads, normed_two, active)
+        moved = (dproj, dgate_c, dmix, dgate, dup)
+        return (result, lefts, moved, small, grad_source.astype(BF16))
 
     def attention_idle():
         flat = lambda: zeros(total, width)
         wide = lambda: zeros(total, hidden)
-        moved = (
-            flat(), zeros(total, 2 * width), flat(), flat(), flat(), flat(), wide(), wide(), wide(),
-        )
-        return (zeros(total, width, kind=F32), moved, zeros(8, width, kind=F32), flat())
-
-    outputs, moved, conv_small, grad_link = lax.cond(first, attention_idle, conv_both)
+        lefts = (kept[0], kept[5], kept[7], active)
+        moved = (zeros(total, 2 * width), flat(), flat(), wide(), wide())
+        return (zeros(total, width, kind=F32), lefts, moved, zeros(8, width, kind=F32), flat())
+
+    outputs, lefts, moved, conv_small, grad_link = lax.cond(first, attention_idle, conv_both)
+    normed, heads, normed_two, active_both = together(lefts, grad_link)
     grad_link = lax.ppermute(grad_link, "section", [(1, 0)])
-
-    def attention_back():
-        w_in, w_out, gate, upward, down, unused = weights
-        normed, raw, query, own, peer, heads, resid, normed_two, active, one, two = kept
-        shard_down = reduce(active, grad_link)
-        grad_two, dgate, dup = ff_backward(grad_link, one, two, gate, upward, down)
-        shard_gate = reduce(normed_two, dgate)
-        shard_up = reduce(normed_two, dup)
+    conv_dproj, dgate_c, conv_dmix, conv_dgate, conv_dup = moved
+    left_down, left_two, left_heads, left_normed = [
+        turned(value) for value in (active_both, normed_two, heads, normed)
+    ]
+    grad_ff = jnp.where(first, grad_link, cotangent[0].reshape(total, width))
+    down = sides(core_sum(left_down, grad_ff))
+    groups = [[i for i in range(fsdp) if i % 2 == side] for side in range(2)]
+
+    def cross(half):
+        return to_peer(half[0])
+
+    def along_all(own):
+        return lax.all_to_all(own, "fsdp", 0, 0, axis_index_groups=groups, tiled=True)
+
+    def scattered(came):
+        return jnp.sum(came.astype(F32), axis=0)
+
+    def halves_of(leaving, staying):
+        return sides(core_add(to_core(leaving), staying))
+
+    def attention_ff():
+        grad_two, *products = ff_backward_outer(grad_ff, left_two, one, two, wide_weights, hidden)
+        return (grad_two, halves_of(*products[:2]), *products[2:])
+
+    def conv_ff():
+        products = ff_outer(left_two, conv_dgate, conv_dup)
+        return (zeros(total, width, kind=F32), halves_of(*products[:2]), *products[2:])
+
+    step, down = fence(first, down)
+    down_came = cross(down)
+    result = lax.cond(step, attention_ff, conv_ff)
+    down_came, (grad_two, gate, up_leaving, up_staying) = fence(down_came, result)
+
+    def attention_core():
+        unused, raw, query, own, peer, unused, resid, unused = kept
         scale_two = rms_scale(resid)
         gain_two = jnp.sum(grad_two * resid * scale_two, axis=0)
         grad_resid = grad_link.astype(F32) + norm_back(grad_two, resid, scale_two, gains[1])
         dmix = grad_resid.astype(BF16)
-        shard_out = reduce(heads, dmix)
-        dheads = matmul_t(dmix, w_out).astype(BF16)
-        dquery, down_kv, peer_kv = attend_back(part_ref, query, own, peer, dheads, rows, stretches)
-        recv = to_peer(peer_kv.astype(BF16))
+        dheads = matmul_t(dmix, weights[1]).astype(BF16)
+        up = halves_of(up_leaving, up_staying)
+        grads = attend_back(part_ref, query, own, peer, dheads, rows, stretches)
+        blank = zeros(chips, 2 * conv_cut, width)
+        return (
+            up, gain_two, grad_resid, dmix, *grads[:2], grads[2].astype(BF16), [blank, blank],
+        )
+
+    def conv_core():
+        mixed = normed.reshape(total, 2, 2 * fsdp, conv_cut)
+        mixed = jnp.transpose(mixed, (0, 2, 1, 3)).reshape(total, width)
+        lone = sides(core_sum(turned(mixed), dgate_c))
+        flat = lambda: zeros(total, width, kind=F32)
+        up = halves_of(up_leaving, up_staying)
+        return (
+            up, zeros(width, kind=F32), flat(), conv_dmix, flat(), flat(), zeros(total, width), lone,
+        )
+
+    down = crossed(down[1], down_came)
+    step, down, gate = fence(first, down, gate)
+    down_came, gate_came = (along_all(down), cross(gate))
+    result = lax.cond(step, attention_core, conv_core)
+    down_came, gate_came, result = fence(down_came, gate_came, result)
+    up, gain_two, grad_resid, dmix, dquery, down_kv, peer_kv, lone = result
+
+    def joined(*halves):
+        return [jnp.concatenate(parts, axis=2) for parts in zip(*halves)]
+
+    def attention_project():
         dproj, grad_one, head_rows = project_back(
-            raw, dquery, down_kv, recv, cosine, sine, gain_rows(), w_in
+            kept[1], dquery, down_kv, recv, cosine, sine, gain_rows(), weights[0]
         )
-        shard_in = reduce(normed, dproj)
+        inward = sides(core_sum(left_normed, dproj))
+        return (joined(inward, outward), grad_one, head_rows)
+
+    def conv_project():
+        inward = sides(core_sum(left_normed, conv_dproj))
+        return (joined(inward, outward), zeros(total, width, kind=F32), zeros(8, PAIR, kind=F32))
+
+    gate = crossed(gate[1], gate_came)
+    gate, up, lone, peer_kv = fence(gate, up, lone, peer_kv)
+    recv = only(0, peer_kv, "seq")
+    outward = sides(core_sum(left_heads, dmix))
+    gate_came = along_all(gate)
+    step, up, lone, recv, outward = fence(first, up, lone, recv, outward)
+    up_came = cross(up)
+    lone_came = only(1, lone[0], "seq")
+    result = lax.cond(step, attention_project, conv_project)
+    gate_came, up_came, lone_came, result = fence(gate_came, up_came, lone_came, result)
+    mix, grad_one, head_rows = result
+
+    def attention_ends():
         source = tokens[0].reshape(total, width).astype(F32)
         scale_one = rms_scale(source)
         gain_one = jnp.sum(grad_one * source * scale_one, axis=0)
@@ -614,28 +856,25 @@
             [gain_one[None], gain_two[None], jnp.zeros((3, width), F32), head_row,
              jnp.zeros((2, width), F32)], axis=0
         )
-        small = reduce_small(small)
-        shards = (shard_in, shard_out, shard_gate, shard_up, shard_down)
-        return (grad_source, shards, zeros(2 * conv_cut, width, kind=F32), small)
-
-    conv_cut = width // (4 * fsdp)
-
-    def conv_weights():
-        normed, dproj, dgate_c, heads, dmix, normed_two, dgate, dup, active = moved
-        grad_ff = cotangent[0].reshape(total, width)
-        shard_down = reduce(active, grad_ff)
-        shard_gate = reduce(normed_two, dgate)
-        shard_up = reduce(normed_two, dup)
-        shard_out = reduce(heads, dmix)
-        shard_in = reduce(normed, dproj)
-        turned = normed.reshape(total, 2, 2 * fsdp, conv_cut)
-        turned = jnp.transpose(turned, (0, 2, 1, 3)).reshape(total, width)
-        shard_c = reduce(turned, dgate_c)
-        small = reduce_small(conv_small)
-        shards = (shard_in, shard_out, shard_gate, shard_up, shard_down)
-        return (outputs, shards, shard_c, small)
-
-    ends, shards_out, shard_c, small = lax.cond(first, attention_back, conv_weights)
+        return (grad_source, reduce_small(small))
+
+    def conv_ends():
+        return (outputs, reduce_small(conv_small))
+
+    up = crossed(up[1], up_came)
+    lone = pieces(crossed(lone[1], lone_came))
+    step, up, mix = fence(first, up, mix)
+    up_came, mix_came = (along_all(up), cross(mix))
+    result = lax.cond(step, attention_ends, conv_ends)
+    up_came, mix_came, (ends, small) = fence(up_came, mix_came, result)
+    mix_came = along_all(crossed(mix[1], mix_came))
+    lone_came = [only(1, piece, count) for count, piece in enumerate(lone[1:], 1)]
+    shard_c = sum((piece.astype(F32) for piece in lone_came), lone[0].astype(F32))
+    shard_mix = scattered(mix_came)
+    shards_out = (
+        shard_mix[:, : 2 * width], shard_mix[:, 2 * width :],
+        scattered(gate_came), scattered(up_came), scattered(down_came),
+    )
     mail = lax.ppermute(
         jnp.concatenate([shard_c, small], axis=0), "section", swap
     )

time: 1030 us -> 757 us (0.73)
  waiting for transfers between devices: 481 us -> 327 us
  starting transfers between devices: 158 us -> 81.7 us
  local copies, waits for them, and re-layouts: 136 us -> 70.5 us
  other arithmetic: 29.6 us -> 66.2 us
  matrix products: 55.8 us -> 31 us
  loops' own time: 24.9 us -> 7.78 us
  between operations: 1.28 us -> 14.7 us
  Pallas kernels: 139 us -> 150 us
    ppermute x30 -> x6, waiting for transfers between devices: 141 us -> 18.5 us  [along(): lax.ppermute(value, 'fsdp', [(i, (i + 2 * steps) % fsdp) for i in range(f...]
    ppermute x23 -> x12, waiting for transfers between devices: 210 us -> 97.5 us  [to_peer(): return lax.ppermute(value, 'seq', swap)]
    ppermute x30 -> x6, starting transfers between devices: 97 us -> 15.5 us  [along(): lax.ppermute(value, 'fsdp', [(i, (i + 2 * steps) % fsdp) for i in range(f...]
    dot_general x10 -> x0, matrix products: 47.8 us -> none  [outer_sum(): lax.dot_general(left, right, (((0,), (0,)), ((), ())), preferred_element_...]
    all_gather x0 -> x1, waiting for transfers between devices: none -> 33.4 us  [local(): lax.all_gather(pack_halves(*halves), ('fsdp', 'seq'), axis=0)]
    convert_element_type x9 -> x12, other arithmetic: 10.9 us -> 38.9 us  [the longest x5 18.6 us: crossed(): return (staying.astype(F32) + came.astype(F32)).astype(BF16)]
    dot_general x1 -> x7, matrix products: 3.32 us -> 26.8 us  [matmul(): return jnp.dot(left, right, preferred_element_type=F32)]
    ppermute x0 -> x5, waiting for transfers between devices: none -> 22.6 us  [only(): return lax.ppermute(value, ('section', 'seq', 'fsdp'), pairs)]
  transfers between devices with their start and end apart: 70 -> 42, of which waited for: 29 -> 24; matrix products, arithmetic and copies ran while one was open for 16% -> 16% of each run, Pallas kernels for 11% -> 17%
where the time goes in v2:
time: 757 us; the launch traced here: 749 us
  waiting for transfers between devices  327 us (43%)
  Pallas kernels  150 us (20%)
  starting transfers between devices  81.7 us (11%)
  local copies, waits for them, and re-layouts  70.5 us (9%)
  other arithmetic  66.2 us (9%)
  matrix products  31 us (4%)
  between operations  14.7 us (2%)
  loops' own time  7.78 us (1%)
    ppermute x1, waiting for transfers between devices, local(): grad_link = lax.ppermute(grad_link, 'section', [(1, 0)])  101 us
    ppermute x12, waiting for transfers between devices, to_peer(): return lax.ppermute(value, 'seq', swap)  97.5 us
    pallas_call x1, Pallas kernels, ff_backward_outer(): pl.pallas_call(backward_outer_kernel, grid=(hidden // chunk,), in_specs=[...  35.9 us
    pallas_call x1, Pallas kernels, attend_back(): pl.pallas_call(functools.partial(attend_back_kernel, rows, stretches), gr...  34.4 us
    all_gather x1, waiting for transfers between devices, local(): lax.all_gather(pack_halves(*halves), ('fsdp', 'seq'), axis=0)  33.4 us
    dot_general x7, matrix products, matmul(): return jnp.dot(left, right, preferred_element_type=F32)  26.8 us
    pallas_call x1, Pallas kernels, ff_forward(): pl.pallas_call(forward_kernel, grid=(hidden // chunk,), in_specs=[pl.Bloc...  25.6 us
    ppermute x5, waiting for transfers between devices, only(): return lax.ppermute(value, ('section', 'seq', 'fsdp'), pairs)  22.6 us
  transfers between devices with their start and end apart: 42, of which 24 were waited for; matrix products, arithmetic and copies ran while one was open for 16% of the time, Pallas kernels for 17%

profile of v2, /device:TPU:0, one launch (start us, length us, event | category | flops | bytes accessed | tf_op | source)
XLA Modules:
  0.0 748.7 jit_solution(10604865636498953549)
XLA Ops:
  18.3 164.3 %conditional.7 = (bf16[1024,2048]{1,0:T(8,128)(2,1)}, bf16[1024,1024]{1,0:T(8,128)(2,1)}, bf16[1024,1024]{1,0:T(8,128)(2,1)}, bf16[512,1024]{1,0:T(8,128)(2,1)},...) conditional(s32[]{:T(128)} %convert_element_type.282, ...), branch_computations={%region_0.1_spmd, %region_1.4_spmd} | conditional | flops 1083314432 | bytes 90523936 | solution.py:685
  62.6 9.4 %collective-permute-start.40 = (bf16[64,1024]{1,0:T(8,128)(2,1)S(1)}, bf16[64,1024]{1,0:T(8,128)(2,1)S(1)}, u32[]{:S(2)}, u32[]{:S(2)}) collective-permute-start(bf16[64,1024]{1,0:T(8,128)(2,1)S(1)} %dynamic-slice_bitcast_fusion.3), channel_id=1, source_target_pairs={{0,4},{1,5},{2,6},{3,7},{4,0},{5,1},{6,2},{7,3},{8,12},{9,13},{10,... | collective-permute-start | bytes 393224 | tf_op jit(solution)/shard_map/cond/branch_1_fun/ppermute | solution.py:535
  101.9 14.8 %branch_1_fun.6 = (bf16[512,2048]{1,0:T(8,128)(2,1)}, bf16[512,1024]{1,0:T(8,128)(2,1)S(1)}, bf16[512,1024]{1,0:T(8,128)(2,1)S(1)}) custom-call(bf16[512,1024]{1,0:T(8,128)(2,1)S(1)} %fusion.2.x_ref, bf16[1024,2048]{1,0:T(8,128)(2,1)} %bitcast.38.w_ref, f32[512,128]{1,0:T(8,128)S(1)} %get-tuple-element.682.cos_ref, ...), custom_call_target="tpu_custom_call" | custom-call | flops 1048576 | bytes 1048576 | tf_op jit(solution)/shard_map/cond/branch_1_fun/pallas_call | solution.py:84
  122.2 31.5 %collective-permute-done.45.peer_ref = bf16[512,1024]{1,0:T(8,128)(2,1)S(1)} collective-permute-done((bf16[512,1024]{1,0:T(8,128)(2,1)S(1)}, bf16[512,1024]{1,0:T(8,128)(2,1)S(1)}, u32[]{:S(2)}, u32[]{:S(2)}) %collective-permute-start.45) | collective-permute-done | bytes 1048608 | tf_op jit(solution)/shard_map/cond/branch_1_fun/ppermute | solution.py:532
  153.7 20.7 %branch_1_fun.7 = bf16[512,1024]{1,0:T(8,128)(2,1)} custom-call(s32[1]{0:T(128)} %get-tuple-element.224.part_ref, bf16[512,1024]{1,0:T(8,128)(2,1)S(1)} %get-tuple-element.676.q_ref, bf16[512,1024]{1,0:T(8,128)(2,1)S(1)} %get-tuple-element.677.own_ref, bf16[512,1024]{1,0:T(8,128)(2,1)S(1)} %collective-permute-done.45.peer_ref), custom_call_target="tpu_custom_call" | custom-call | flops 1048576 | bytes 1048576 | tf_op jit(solution)/shard_map/cond/branch_1_fun/pallas_call | solution.py:136
  182.6 33.4 %all-gather.3.cloned.1.call-done = bf16[13312,1152]{1,0:T(8,128)(2,1)} async-done(((bf16[832,1152]{1,0:T(8,128)(2,1)}), bf16[13312,1152]{1,0:T(8,128)(2,1)}) %all-gather.3.cloned.1.call-update) | async-done | bytes 30670864 | tf_op jit(solution)/shard_map/all_gather | solution.py:638
  216.0 27.3 %conditional.8 = (bf16[512,1024]{1,0:T(8,128)(2,1)S(1)}, bf16[512,4608]{1,0:T(8,128)(2,1)}, bf16[512,4608]{1,0:T(8,128)(2,1)}, bf16[512,4608]{1,0:T(8,128)(2,1)}) conditional(s32[]{:T(128)} %convert_element_type.282, () %tuple.85, (bf16[512,1024]{1,0:T(8,128)(2,1)S(1)}, f32[512,1024]{1,0:T(8,128)}, bf16[16,832,1152]{2,1,0:T(8,128)(2,1)}) %tuple.175), branch_computations={%region_4.5_spmd, %region_5.6_spmd} | conditional | flops 1572864 | bytes 15204392 | solution.py:694
  216.0 25.6 %branch_1_fun.8 = (f32[512,1024]{1,0:T(8,128)}, bf16[512,4608]{1,0:T(8,128)(2,1)}, bf16[512,4608]{1,0:T(8,128)(2,1)}, bf16[512,4608]{1,0:T(8,128)(2,1)}) custom-call(bf16[512,1024]{1,0:T(8,128)(2,1)S(1)} %get-tuple-element.225.x_ref, f32[512,1024]{1,0:T(8,128)} %get-tuple-element.226.base_ref, bf16[16,832,1152]{2,1,0:T(8,128)(2,1)} %get-tuple-element.227.g_ref.u_ref.d_ref, ...), custom_call_target="tpu_custom_call" | custom-call | flops 1048576 | bytes 1048576 | tf_op jit(solution)/shard_map/cond/branch_1_fun/pallas_call | solution.py:419
  244.7 15.1 %collective-permute-done.54 = bf16[512,1024]{1,0:T(8,128)(2,1)S(1)} collective-permute-done((bf16[512,1024]{1,0:T(8,128)(2,1)S(1)}, bf16[512,1024]{1,0:T(8,128)(2,1)S(1)}, u32[]{:S(2)}, u32[]{:S(2)}) %collective-permute-start.54) | collective-permute-done | bytes 1048608 | tf_op jit(solution)/shard_map/ppermute | solution.py:695
  259.9 17.9 %conditional.9 = (f32[512,1024]{1,0:T(8,128)}, bf16[512,1024]{1,0:T(8,128)(2,1)}, bf16[512,1024]{1,0:T(8,128)(2,1)}, bf16[512,1024]{1,0:T(8,128)(2,1)S(1)}, bf16...) conditional(s32[]{:T(128)} %convert_element_type.282, ...), branch_computations={%region_6.16_spmd, %region_16.17_spmd} | conditional | flops 8649187328 | bytes 253248320 | solution.py:755
  290.1 100.6 %collective-permute-done.55 = bf16[512,1024]{1,0:T(8,128)(2,1)} collective-permute-done((bf16[512,1024]{1,0:T(8,128)(2,1)}, bf16[512,1024]{1,0:T(8,128)(2,1)}, u32[]{:S(2)}, u32[]{:S(2)}) %collective-permute-start.55) | collective-permute-done | bytes 1048608 | tf_op jit(solution)/shard_map/ppermute | solution.py:757
  396.2 8.2 %collective-permute-done.56 = bf16[2304,1024]{1,0:T(8,128)(2,1)} collective-permute-done((bf16[2304,1024]{1,0:T(8,128)(2,1)}, bf16[2304,1024]{1,0:T(8,128)(2,1)}, u32[]{:S(2)}, u32[]{:S(2)}) %collective-permute-start.56) | collective-permute-done | bytes 4718624 | tf_op jit(solution)/shard_map/ppermute | solution.py:529
  413.5 52.9 %conditional.10 = (f32[512,1024]{1,0:T(8,128)S(1)}, bf16[4,64,4608]{2,1,0:T(8,128)(2,1)}, bf16[4,64,4608]{2,1,0:T(8,128)(2,1)}, bf16[512,4608]{1,0:T(8,128)(2,1)}, bf16[512,4608]{1,0:T(8,128)(2,1)}) conditional(s32[]{:T(128)} %convert_element_type.287, (bf16[1024,512]{1,0:T(8,128)(2,1)S(1)}, bf16[512,4608]{1,0:T(8,128)(2,1)}, ...), branch_computations={%region_17.18_spmd, %region_18.19_spmd} | conditional | flops 10485767 | bytes 47710400 | solution.py:788
  414.7 35.9 %branch_1_fun.9 = (f32[512,1024]{1,0:T(8,128)S(1)}, bf16[512,4608]{1,0:T(8,128)(2,1)}, bf16[512,4608]{1,0:T(8,128)(2,1)}, bf16[512,4608]{1,0:T(8,128)(2,1)}, bf16[512,4608]{1,0:T(8,128)(2,1)}) custom-call(bf16[512,1024]{1,0:T(8,128)(2,1)} %copy-done.37, bf16[1024,512]{1,0:T(8,128)(2,1)S(1)} %get-tuple-element.261.left_ref, ...), custom_call_target="tpu_custom_call" | custom-call | flops 1048576 | bytes 1048576 | tf_op jit(solution)/shard_map/cond/branch_1_fun/pallas_call | solution.py:461
  450.6 8.2 %collective-permute-done.5 = bf16[512,4608]{1,0:T(8,128)(2,1)} collective-permute-done((bf16[512,4608]{1,0:T(8,128)(2,1)}, bf16[512,4608]{1,0:T(8,128)(2,1)}, u32[]{:S(2)}, u32[]{:S(2)}) %collective-permute-start.5) | collective-permute-done | bytes 4718624 | tf_op jit(solution)/shard_map/cond/branch_1_fun/ppermute | solution.py:529
  482.1 59.0 %conditional.11 = (bf16[4,64,4608]{2,1,0:T(8,128)(2,1)}, bf16[4,64,4608]{2,1,0:T(8,128)(2,1)}, f32[1024]{0:T(1024)S(1)}, f32[512,1024]{1,0:T(8,128)}, bf16[512,1...) conditional(s32[]{:T(128)} %convert_element_type.291, ...), branch_computations={%region_19.20_spmd, %region_20.24_spmd} | conditional | flops 1094188544 | bytes 83401016 | solution.py:818
  494.7 34.4 %branch_1_fun.10 = (f32[512,1024]{1,0:T(8,128)}, f32[512,1024]{1,0:T(8,128)}, f32[512,1024]{1,0:T(8,128)}) custom-call(s32[1]{0:T(128)} %get-tuple-element.285.part_ref, bf16[512,1024]{1,0:T(8,128)(2,1)S(1)} %copy-done.18, bf16[512,1024]{1,0:T(8,128)(2,1)S(1)} %copy-done.20, bf16[512,1024]{1,0:T(8,128)(2,1)S(1)} %copy-done.22, ...), custom_call_target="tpu_custom_call" | custom-call | flops 1048576 | bytes 1048576 | tf_op jit(solution)/shard_map/cond/branch_1_fun/pallas_call | solution.py:193
  558.5 22.5 %collective-permute-done.59 = bf16[512,1024]{1,0:T(8,128)(2,1)S(1)} collective-permute-done((bf16[512,1024]{1,0:T(8,128)(2,1)}, bf16[512,1024]{1,0:T(8,128)(2,1)S(1)}, u32[]{:S(2)}, u32[]{:S(2)}) %collective-permute-start.59) | collective-permute-done | bytes 1048608 | tf_op jit(solution)/shard_map/ppermute | solution.py:596
  584.1 34.8 %conditional.12 = (bf16[4,64,3072]{2,1,0:T(8,128)(2,1)}, bf16[4,64,3072]{2,1,0:T(8,128)(2,1)}, f32[512,1024]{1,0:T(8,128)S(1)}, f32[8,128]{1,0:T(8,128)S(1)}) conditional(s32[]{:T(128)} %convert_element_type.298, (bf16[512,512]{1,0:T(8,128)(2,1)S(1)}, bf16[512,2048]{1,0:T(8,128)(2,1)}, bf16[512,512]{1,0:T(8,128)(2,1)S(1)}, s32[]{:T(128)}, ...), branch_computations={%region_24.25_spmd, %region_25.26_spmd} | conditional | flops 2159017984 | bytes 39854864 | solution.py:844
  585.3 18.3 %branch_1_fun.11 = (bf16[512,2048]{1,0:T(8,128)(2,1)}, f32[512,1024]{1,0:T(8,128)S(1)}, f32[8,128]{1,0:T(8,128)S(1)}) custom-call(bf16[512,2048]{1,0:T(8,128)(2,1)} %get-tuple-element.299.raw_ref, f32[512,1024]{1,0:T(8,128)} %get-tuple-element.300.dq_ref, f32[512,1024]{1,0:T(8,128)} %get-tuple-element.301.own_ref, ...), custom_call_target="tpu_custom_call" | custom-call | flops 1048576 | bytes 1048576 | tf_op jit(solution)/shard_map/cond/branch_1_fun/pallas_call | solution.py:248
  619.0 14.5 %collective-permute-done.61 = bf16[4,64,4608]{2,1,0:T(8,128)(2,1)} collective-permute-done((bf16[4,64,4608]{2,1,0:T(8,128)(2,1)}, bf16[4,64,4608]{2,1,0:T(8,128)(2,1)}, u32[]{:S(2)}, u32[]{:S(2)}) %collective-permute-start.61) | collective-permute-done | bytes 2359328 | tf_op jit(solution)/shard_map/ppermute | solution.py:532
  642.9 53.2 %conditional.13 = (f32[512,1024]{1,0:T(8,128)}, f32[8,1024]{1,0:T(8,128)S(1)}) conditional(s32[]{:T(128)} %convert_element_type.301, (f32[8,1024]{1,0:T(8,128)S(1)}, f32[512,1024]{1,0:T(8,128)}) %tuple.106, (bf16[1,2,256,1024]{3,2,1,0:T(8,128)(2,1)S(1)}, f32[2,1024]{1,0:T(2,128)S(1)}, f32[512,1024]{1,0:T(8,128)S(1)}, f32[512,1024]{1,0:T(8,128)}, ...), branch_computations={%region_26.27_spmd, %region_27.31_spmd} | conditional | flops 9469632 | bytes 12588988 | solution.py:868
  647.1 30.7 %collective-permute-done.7 = f32[8,1024]{1,0:T(8,128)S(1)} collective-permute-done((f32[8,1024]{1,0:T(8,128)S(1)}, f32[8,1024]{1,0:T(8,128)S(1)}, u32[]{:S(2)}, u32[]{:S(2)}) %collective-permute-start.7) | collective-permute-done | bytes 32800 | tf_op jit(solution)/shard_map/cond/branch_1_fun/ppermute | solution.py:532
  710.2 15.2 %collective-permute-start.67 = (f32[72,1024]{1,0:T(8,128)S(1)}, f32[72,1024]{1,0:T(8,128)S(1)}, u32[]{:S(2)}, u32[]{:S(2)}) collective-permute-start(f32[72,1024]{1,0:T(8,128)S(1)} %pad_maximum_fusion.10), channel_id=1, source_target_pairs={{0,16},{16,0},{1,17},{17,1},{2,18},{18,2},{3,19},{19,3},{4,20},{20... | collective-permute-start | bytes 884744 | tf_op jit(solution)/shard_map/ppermute | solution.py:878
  (278 shorter events, 287.2 us)
Async XLA Ops:
  7.2 208.9 %all-gather.3.cloned.1.call-start = ((), (), s32[]{:S(2)}) async-start(), calls=%async_computation.4 | async-start | bytes 32587776 | tf_op jit(solution)/shard_map/all_gather | solution.py:638
  20.0 21.6 %collective-permute-start.33 = (bf16[64,2048]{1,0:T(8,128)(2,1)S(1)}, bf16[64,2048]{1,0:T(8,128)(2,1)S(1)}, u32[]{:S(2)}, u32[]{:S(2)}) collective-permute-start(bf16[64,2048]{1,0:T(8,128)(2,1)S(1)} %dynamic-slice_bitcast_fusion.2), channel_id=1, source_target_pairs={{0,4},{1,5},{2,6},{3,7},{4,0},{5,1},{6,2},{7,3},{8,12},{9,13},{10,... | collective-permute-start | bytes 786440 | tf_op jit(solution)/shard_map/cond/branch_1_fun/ppermute | solution.py:535
  22.6 22.1 %collective-permute-start.35 = (bf16[64,2048]{1,0:T(8,128)(2,1)S(1)}, bf16[64,2048]{1,0:T(8,128)(2,1)S(1)}, u32[]{:S(2)}, u32[]{:S(2)}) collective-permute-start(bf16[64,2048]{1,0:T(8,128)(2,1)S(1)} %dynamic-slice_bitcast_fusion.2), channel_id=1, source_target_pairs={{0,6},{1,7},{2,0},{3,1},{4,2},{5,3},{6,4},{7,5},{8,14},{9,15},{10,... | collective-permute-start | bytes 786440 | tf_op jit(solution)/shard_map/cond/branch_1_fun/ppermute | solution.py:535
  32.3 14.7 %collective-permute-start.32 = (bf16[64,2048]{1,0:T(8,128)(2,1)S(1)}, bf16[64,2048]{1,0:T(8,128)(2,1)S(1)}, u32[]{:S(2)}, u32[]{:S(2)}) collective-permute-start(bf16[64,2048]{1,0:T(8,128)(2,1)S(1)} %collective-permute-done.31), channel_id=1, source_target_pairs={{0,8},{8,0},{1,9},{9,1},{2,10},{10,2},{3,11},{11,3},{4,12},{12,4},... | collective-permute-start | bytes 786440 | tf_op jit(solution)/shard_map/cond/branch_1_fun/ppermute | solution.py:532
  44.7 16.8 %collective-permute-start.36 = (bf16[64,2048]{1,0:T(8,128)(2,1)S(1)}, bf16[64,2048]{1,0:T(8,128)(2,1)S(1)}, u32[]{:S(2)}, u32[]{:S(2)}) collective-permute-start(bf16[64,2048]{1,0:T(8,128)(2,1)S(1)} %collective-permute-done.35), channel_id=1, source_target_pairs={{0,8},{8,0},{1,9},{9,1},{2,10},{10,2},{3,11},{11,3},{4,12},{12,4},... | collective-permute-start | bytes 786440 | tf_op jit(solution)/shard_map/cond/branch_1_fun/ppermute | solution.py:532
  62.2 32.3 %collective-permute-start.37 = (bf16[4,2,64,2048]{3,2,1,0:T(8,128)(2,1)}, bf16[4,2,64,2048]{3,2,1,0:T(8,128)(2,1)}, u32[]{:S(2)}, u32[]{:S(2)}) collective-permute-start(bf16[4,2,64,2048]{3,2,1,0:T(8,128)(2,1)} %bitcast_dynamic-update-slice_fusion.23), channel_id=1, source_target_pairs={{0,1},{1,0},{2,3},{3,2},{4,5},{5,4},{6,7},{7,6},{8,9},{9,8},{10,11... | collective-permute-start | bytes 6291464 | tf_op jit(solution)/shard_map/cond/branch_1_fun/ppermute | solution.py:529
  62.6 20.3 %collective-permute-start.40 = (bf16[64,1024]{1,0:T(8,128)(2,1)S(1)}, bf16[64,1024]{1,0:T(8,128)(2,1)S(1)}, u32[]{:S(2)}, u32[]{:S(2)}) collective-permute-start(bf16[64,1024]{1,0:T(8,128)(2,1)S(1)} %dynamic-slice_bitcast_fusion.3), channel_id=1, source_target_pairs={{0,4},{1,5},{2,6},{3,7},{4,0},{5,1},{6,2},{7,3},{8,12},{9,13},{10,... | collective-permute-start | bytes 393224 | tf_op jit(solution)/shard_map/cond/branch_1_fun/ppermute | solution.py:535
  94.4 24.0 %collective-permute-start.44 = (bf16[4,2,64,1024]{3,2,1,0:T(8,128)(2,1)S(1)}, bf16[4,2,64,1024]{3,2,1,0:T(8,128)(2,1)}, u32[]{:S(2)}, u32[]{:S(2)}) collective-permute-start(bf16[4,2,64,1024]{3,2,1,0:T(8,128)(2,1)S(1)} %bitcast_dynamic-update-slice_fusion.29), channel_id=1, source_target_pairs={{0,1},{1,0},{2,3},{3,2},{4,5},{5,4},{6,7},{7,6},{8,9},{9,8},{10,11... | collective-permute-start | bytes 3145736 | tf_op jit(solution)/shard_map/cond/branch_1_fun/ppermute | solution.py:529
  116.7 37.0 %collective-permute-start.45 = (bf16[512,1024]{1,0:T(8,128)(2,1)S(1)}, bf16[512,1024]{1,0:T(8,128)(2,1)S(1)}, u32[]{:S(2)}, u32[]{:S(2)}) collective-permute-start(bf16[512,1024]{1,0:T(8,128)(2,1)S(1)} %get-tuple-element.677.own_ref), channel_id=1, source_target_pairs={{0,8},{8,0},{1,9},{9,1},{2,10},{10,2},{3,11},{11,3},{4,12},{12,4},... | collective-permute-start | bytes 3145736 | tf_op jit(solution)/shard_map/cond/branch_1_fun/ppermute | solution.py:532
  243.4 16.5 %collective-permute-start.54 = (bf16[512,1024]{1,0:T(8,128)(2,1)S(1)}, bf16[512,1024]{1,0:T(8,128)(2,1)S(1)}, u32[]{:S(2)}, u32[]{:S(2)}) collective-permute-start(bf16[512,1024]{1,0:T(8,128)(2,1)S(1)} %get-tuple-element.443), channel_id=1, source_target_pairs={{0,16},{1,17},{2,18},{3,19},{4,20},{5,21},{6,22},{7,23},{8,24},{9,... | collective-permute-start | bytes 3145736 | tf_op jit(solution)/shard_map/ppermute | solution.py:695
  277.7 112.9 %collective-permute-start.55 = (bf16[512,1024]{1,0:T(8,128)(2,1)}, bf16[512,1024]{1,0:T(8,128)(2,1)}, u32[]{:S(2)}, u32[]{:S(2)}) collective-permute-start(bf16[512,1024]{1,0:T(8,128)(2,1)} %get-tuple-element.454), channel_id=1, source_target_pairs={{16,0},{17,1},{18,2},{19,3},{20,4},{21,5},{22,6},{23,7},{24,8},{25... | collective-permute-start | bytes 3145736 | tf_op jit(solution)/shard_map/ppermute | solution.py:757
  412.4 53.9 %collective-permute-start.57 = (bf16[4,288,1024]{2,1,0:T(8,128)(2,1)}, bf16[4,288,1024]{2,1,0:T(8,128)(2,1)}, u32[]{:S(2)}, u32[]{:S(2)}) collective-permute-start(bf16[4,288,1024]{2,1,0:T(8,128)(2,1)} %get-tuple-element.457), channel_id=1, source_target_pairs={{0,8},{8,0},{1,9},{9,1},{2,10},{10,2},{3,11},{11,3},{4,12},{12,4},... | collective-permute-start | bytes 7077896 | tf_op jit(solution)/shard_map/ppermute | solution.py:532
  471.3 69.9 %all-to-all-start = ((bf16[4,288,1024]{2,1,0:T(8,128)(2,1)}), bf16[4,288,1024]{2,1,0:T(8,128)(2,1)}, u32[]{:S(2)}, u32[]{:S(2)}) async-start(bf16[4,288,1024]{2,1,0:T(8,128)(2,1)} %add_convert_fusion.9), calls=%async_computation | async-start | bytes 4718592 | tf_op jit(solution)/shard_map/all_to_all | solution.py:770
  475.8 65.3 %collective-permute-start.58 = (bf16[4,64,4608]{2,1,0:T(8,128)(2,1)}, bf16[4,64,4608]{2,1,0:T(8,128)(2,1)}, u32[]{:S(2)}, u32[]{:S(2)}) collective-permute-start(bf16[4,64,4608]{2,1,0:T(8,128)(2,1)} %get-tuple-element.474), channel_id=1, source_target_pairs={{0,8},{8,0},{1,9},{9,1},{2,10},{10,2},{3,11},{11,3},{4,12},{12,4},... | collective-permute-start | bytes 7077896 | tf_op jit(solution)/shard_map/ppermute | solution.py:532
  482.5 49.3 %collective-permute-start.50 = (bf16[512,4608]{1,0:T(8,128)(2,1)}, bf16[512,4608]{1,0:T(8,128)(2,1)}, u32[]{:S(2)}, u32[]{:S(2)}) collective-permute-start(bf16[512,4608]{1,0:T(8,128)(2,1)} %get-tuple-element.279), channel_id=1, source_target_pairs={{0,1},{1,0},{2,3},{3,2},{4,5},{5,4},{6,7},{7,6},{8,9},{9,8},{10,11... | collective-permute-start | bytes 14155784 | tf_op jit(solution)/shard_map/cond/branch_1_fun/ppermute | solution.py:529
  549.0 84.5 %all-to-all-start.1 = ((bf16[4,64,4608]{2,1,0:T(8,128)(2,1)}), bf16[4,64,4608]{2,1,0:T(8,128)(2,1)}, u32[]{:S(2)}, u32[]{:S(2)}) async-start(bf16[4,64,4608]{2,1,0:T(8,128)(2,1)} %add_convert_fusion.8), calls=%async_computation.1 | async-start | bytes 4718592 | tf_op jit(solution)/shard_map/all_to_all | solution.py:770
  554.1 26.9 %collective-permute-start.59 = (bf16[512,1024]{1,0:T(8,128)(2,1)}, bf16[512,1024]{1,0:T(8,128)(2,1)S(1)}, u32[]{:S(2)}, u32[]{:S(2)}) collective-permute-start(bf16[512,1024]{1,0:T(8,128)(2,1)} %get-tuple-element.505), channel_id=1, source_target_pairs={{0,8},{1,9},{2,10},{3,11},{4,12},{5,13},{6,14},{7,15},{8,0},{9,1},... | collective-permute-start | bytes 3145736 | tf_op jit(solution)/shard_map/ppermute | solution.py:596
  581.1 52.4 %collective-permute-start.61 = (bf16[4,64,4608]{2,1,0:T(8,128)(2,1)}, bf16[4,64,4608]{2,1,0:T(8,128)(2,1)}, u32[]{:S(2)}, u32[]{:S(2)}) collective-permute-start(bf16[4,64,4608]{2,1,0:T(8,128)(2,1)} %get-tuple-element.510), channel_id=1, source_target_pairs={{0,8},{8,0},{1,9},{9,1},{2,10},{10,2},{3,11},{11,3},{4,12},{12,4},... | collective-permute-start | bytes 7077896 | tf_op jit(solution)/shard_map/ppermute | solution.py:532
  582.0 37.0 %collective-permute-start.62 = (bf16[4,64,1024]{2,1,0:T(8,128)(2,1)}, bf16[4,64,1024]{2,1,0:T(8,128)(2,1)}, u32[]{:S(2)}, u32[]{:S(2)}) collective-permute-start(bf16[4,64,1024]{2,1,0:T(8,128)(2,1)} %get-tuple-element.511), channel_id=1, source_target_pairs={{16,24},{17,25},{18,26},{19,27},{20,28},{21,29},{22,30},{23,31},{2... | collective-permute-start | bytes 1572872 | tf_op jit(solution)/shard_map/ppermute | solution.py:596
  637.8 58.3 %all-to-all-start.2 = ((bf16[4,64,4608]{2,1,0:T(8,128)(2,1)}), bf16[4,64,4608]{2,1,0:T(8,128)(2,1)}, u32[]{:S(2)}, u32[]{:S(2)}) async-start(bf16[4,64,4608]{2,1,0:T(8,128)(2,1)} %add_convert_fusion.7), calls=%async_computation.2 | async-start | bytes 4718592 | tf_op jit(solution)/shard_map/all_to_all | solution.py:770
  642.5 53.7 %collective-permute-start.63 = (bf16[4,64,3072]{2,1,0:T(8,128)(2,1)}, bf16[4,64,3072]{2,1,0:T(8,128)(2,1)}, u32[]{:S(2)}, u32[]{:S(2)}) collective-permute-start(bf16[4,64,3072]{2,1,0:T(8,128)(2,1)} %get-tuple-element.530), channel_id=1, source_target_pairs={{0,8},{8,0},{1,9},{9,1},{2,10},{10,2},{3,11},{11,3},{4,12},{12,4},... | collective-permute-start | bytes 4718600 | tf_op jit(solution)/shard_map/ppermute | solution.py:532
  645.5 32.3 %collective-permute-start.7 = (f32[8,1024]{1,0:T(8,128)S(1)}, f32[8,1024]{1,0:T(8,128)S(1)}, u32[]{:S(2)}, u32[]{:S(2)}) collective-permute-start(f32[8,1024]{1,0:T(8,128)S(1)} %add.455), channel_id=1, source_target_pairs={{0,8},{8,0},{1,9},{9,1},{2,10},{10,2},{3,11},{11,3},{4,12},{12,4},... | collective-permute-start | bytes 98312 | tf_op jit(solution)/shard_map/cond/branch_1_fun/ppermute | solution.py:532
  699.8 40.1 %all-to-all-start.3 = ((bf16[4,64,3072]{2,1,0:T(8,128)(2,1)}), bf16[4,64,3072]{2,1,0:T(8,128)(2,1)S(1)}, u32[]{:S(2)}, u32[]{:S(2)}) async-start(bf16[4,64,3072]{2,1,0:T(8,128)(2,1)} %add_convert_fusion.10), calls=%async_computation.3 | async-start | bytes 3145728 | tf_op jit(solution)/shard_map/all_to_all | solution.py:770
  710.2 21.5 %collective-permute-start.67 = (f32[72,1024]{1,0:T(8,128)S(1)}, f32[72,1024]{1,0:T(8,128)S(1)}, u32[]{:S(2)}, u32[]{:S(2)}) collective-permute-start(f32[72,1024]{1,0:T(8,128)S(1)} %pad_maximum_fusion.10), channel_id=1, source_target_pairs={{0,16},{16,0},{1,17},{17,1},{2,18},{18,2},{3,19},{19,3},{4,20},{20... | collective-permute-start | bytes 884744 | tf_op jit(solution)/shard_map/ppermute | solution.py:878
  (53 other events, 685.7 us)
Sparse Core Ops, SparseCore 0:
  10.8 205.1 all-gather.2

commit v3 on v2

--- a/solution.py
+++ b/solution.py
@@ -149,6 +149,7 @@
     rows, stretches, part_ref, q_ref, own_ref, peer_ref, grad_ref, dq_ref, down_ref, dpeer_ref
 ):
     second = part_ref[0] == 1
+    sums = {}
     for stretch in reversed(range(stretches)):
         blocks = []
         for s in range(stretch + 1):
@@ -177,26 +178,26 @@
         dq_ref[span, :] = jnp.concatenate(dquery, axis=1)
         both = jnp.concatenate([dkeys, dvalues], axis=1)
         for s in range(stretch + 1):
-            for place, out in ((2 * s, down_ref), (2 * s + 1, dpeer_ref)):
-                piece = both[place * rows : (place + 1) * rows]
-                span_s = slice(s * rows, (s + 1) * rows)
-                if stretch == stretches - 1:
-                    out[span_s, :] = piece
-                else:
-                    out[span_s, :] += piece
-
-
-def attend_back(part, query, own, peer, grad, rows, stretches):
+            for side in range(2):
+                piece = both[(2 * s + side) * rows : (2 * s + side + 1) * rows]
+                sums[s, side] = sums[s, side] + piece if (s, side) in sums else piece
+    for (s, side), value in sums.items():
+        out = (down_ref, dpeer_ref)[side]
+        out[s * rows : (s + 1) * rows, :] = value.astype(out.dtype)
+
+
+def attend_back(part, query, own, peer, grad, rows, stretches, groups):
     tokens = query.shape[0]
-    column = lambda g: (0, g)
-    shape = jax.ShapeDtypeStruct((tokens, KV_HEADS * PAIR), F32)
+    count = len(groups)
+    column = lambda g: (0, g + groups.start)
+    shape = lambda kind: jax.ShapeDtypeStruct((tokens, count * PAIR), kind)
     return pl.pallas_call(
         functools.partial(attend_back_kernel, rows, stretches),
-        grid=(KV_HEADS,),
+        grid=(count,),
         in_specs=[pl.BlockSpec(memory_space=pltpu.SMEM)]
         + [pl.BlockSpec((tokens, PAIR), column)] * 4,
-        out_specs=[pl.BlockSpec((tokens, PAIR), column)] * 3,
-        out_shape=[shape] * 3,
+        out_specs=[pl.BlockSpec((tokens, PAIR), lambda g: (0, g))] * 3,
+        out_shape=[shape(F32), shape(F32), shape(BF16)],
         compiler_params=params(),
         cost_estimate=light(),
     )(part, query, own, peer, grad)
@@ -273,13 +274,21 @@
     )(raw, dquery, own, recv, cosine, sine, gain_rows, weight)
 
 
-def flat(ref):
-    value = ref[...]
-    return value.reshape(-1, value.shape[-1])
+LANES = 128
+
+
+def wide(ref, columns):
+    if len(ref.shape) == 2:
+        return ref[...]
+    count = columns // LANES
+    rows = ref.shape[1] // count
+    parts = [ref[:, i * rows : (i + 1) * rows, :].reshape(-1, LANES) for i in range(count)]
+    return jnp.concatenate(parts, axis=1)
 
 
 def forward_kernel(x_ref, base_ref, g_ref, u_ref, d_ref, out_ref, act_ref, one_ref, two_ref):
-    gate_part, up_part, down_part = (flat(g_ref), flat(u_ref), flat(d_ref))
+    chunk, width = (act_ref.shape[1], out_ref.shape[1])
+    gate_part, up_part, down_part = (wide(g_ref, chunk), wide(u_ref, chunk), wide(d_ref, width))
     down = 0.0
     for span in spans(act_ref.shape[1]):
         gate = jnp.dot(x_ref[...], gate_part[:, span], preferred_element_type=F32)
@@ -301,26 +310,6 @@
         out_ref[...] += down
 
 
-def backward_kernel(grad_ref, one_ref, two_ref, g_ref, u_ref, d_ref, out_ref, dg_ref, du_ref):
-    gate_part, up_part, down_part = (flat(g_ref), flat(u_ref), flat(d_ref))
-    total = 0.0
-    for span in spans(dg_ref.shape[1]):
-        active = matmul_t(grad_ref[...], down_part[span])
-        dgate = (active * one_ref[:, span].astype(F32)).astype(BF16)
-        dup = (active * two_ref[:, span].astype(F32)).astype(BF16)
-        dg_ref[:, span] = dgate
-        du_ref[:, span] = dup
-        total += matmul_t(dgate, gate_part[:, span]) + matmul_t(dup, up_part[:, span])
-
-    @pl.when(pl.program_id(0) == 0)
-    def _():
-        out_ref[...] = total
-
-    @pl.when(pl.program_id(0) > 0)
-    def _():
-        out_ref[...] += total
-
-
 def store_outer(left_ref, dgate, dup, span, outs):
     half = left_ref.shape[0] // 2
     for right, leave_ref, stay_ref in ((dgate, *outs[:2]), (dup, *outs[2:])):
@@ -330,7 +319,8 @@
 
 
 def backward_outer_kernel(grad_ref, left_ref, one_ref, two_ref, g_ref, u_ref, d_ref, out_ref, *outs):
-    gate_part, up_part, down_part = (flat(g_ref), flat(u_ref), flat(d_ref))
+    chunk, width = (one_ref.shape[1], out_ref.shape[1])
+    gate_part, up_part, down_part = (wide(g_ref, chunk), wide(u_ref, chunk), wide(d_ref, width))
     total = 0.0
     for span in spans(one_ref.shape[1]):
         active = matmul_t(grad_ref[...], down_part[span])
@@ -352,6 +342,44 @@
     store_outer(left_ref, dg_ref[...], du_ref[...], slice(None), outs)
 
 
+def both_ways_kernel(x_ref, grad_ref, g_ref, u_ref, d_ref, out_ref, act_ref, dg_ref, du_ref):
+    chunk, width = (act_ref.shape[1], out_ref.shape[1])
+    gate_part, up_part, down_part = (wide(g_ref, chunk), wide(u_ref, chunk), wide(d_ref, width))
+    total = 0.0
+    for span in spans(act_ref.shape[1]):
+        gate = jnp.dot(x_ref[...], gate_part[:, span], preferred_element_type=F32)
+        upward = jnp.dot(x_ref[...], up_part[:, span], preferred_element_type=F32)
+        dactive = matmul_t(grad_ref[...], down_part[span])
+        sigma = jax.nn.sigmoid(gate)
+        silu = gate * sigma
+        act_ref[:, span] = (silu * upward).astype(BF16)
+        dgate = (dactive * upward * sigma * (1.0 + gate * (1.0 - sigma))).astype(BF16)
+        dup = (dactive * silu).astype(BF16)
+        dg_ref[:, span] = dgate
+        du_ref[:, span] = dup
+        total += matmul_t(dgate, gate_part[:, span]) + matmul_t(dup, up_part[:, span])
+
+    @pl.when(pl.program_id(0) == 0)
+    def _():
+        out_ref[...] = total
+
+    @pl.when(pl.program_id(0) > 0)
+    def _():
+        out_ref[...] += total
+
+
+def down_kernel(base_ref, act_ref, d_ref, out_ref):
+    down = jnp.dot(act_ref[...], wide(d_ref, out_ref.shape[1]), preferred_element_type=F32)
+
+    @pl.when(pl.program_id(0) == 0)
+    def _():
+        out_ref[...] = base_ref[...] + down
+
+    @pl.when(pl.program_id(0) > 0)
+    def _():
+        out_ref[...] += down
+
+
 def spans(chunk):
     starts = list(range(0, max(chunk - 511, 1), 512))
     return [slice(a, b) for a, b in zip(starts, starts[1:] + [chunk])]
@@ -368,19 +396,16 @@
     gate_rows, down_rows = (width // devices, hidden // devices)
     return (
         devices % CHUNKS == 0
-        and hidden % (CHUNKS * 128) == 0
-        and hidden // CHUNKS >= width
+        and hidden % (CHUNKS * LANES) == 0
+        and width % LANES == 0
         and gate_rows % 16 == 0
         and down_rows % 16 == 0
     )
 
 
 def pack_halves(gate, upward, down):
-    rows, hidden = gate.shape
-    chunk = hidden // CHUNKS
-    down = jnp.pad(down, ((0, -down.shape[0] % rows), (0, chunk - down.shape[1])))
-    cut = lambda w: jnp.transpose(w.reshape(rows, CHUNKS, chunk), (1, 0, 2)).reshape(-1, chunk)
-    return jnp.concatenate([down, cut(gate), cut(upward)], axis=0)
+    cut = lambda w: jnp.transpose(w.reshape(w.shape[0], -1, LANES), (1, 0, 2)).reshape(-1, LANES)
+    return jnp.concatenate([cut(gate), cut(upward), cut(down)], axis=0)
 
 
 def weight_specs(weights, tokens, width, hidden):
@@ -397,14 +422,15 @@
             weights,
         )
     devices = weights[0].shape[0]
-    rows, down_rows, chunk = (width // devices, hidden // devices, hidden // CHUNKS)
-    skip = -(-down_rows // rows)
+    chunk = hidden // CHUNKS
+    tall = width // devices * (hidden // LANES)
+    piece = tall // CHUNKS
     return (
         chunk,
         [
-            pl.BlockSpec((devices, rows, chunk), lambda j: (0, skip + j, 0)),
-            pl.BlockSpec((devices, rows, chunk), lambda j: (0, skip + CHUNKS + j, 0)),
-            pl.BlockSpec((devices // CHUNKS, down_rows, width), lambda j: (j, 0, 0)),
+            pl.BlockSpec((devices, piece, LANES), lambda j: (0, j, 0)),
+            pl.BlockSpec((devices, piece, LANES), lambda j: (0, CHUNKS + j, 0)),
+            pl.BlockSpec((devices // CHUNKS, tall, LANES), lambda j: (j, 2, 0)),
         ],
         (weights[0],) * 3,
     )
@@ -429,27 +455,42 @@
     )(normed, base, *operands)
 
 
-def ff_backward(grad, one, two, weights, hidden):
-    tokens, width = grad.shape
+def ff_both_ways(normed, grad, weights, hidden):
+    tokens, width = normed.shape
     chunk, specs, operands = weight_specs(weights, tokens, width, hidden)
     whole = lambda j: (0, 0)
     column = lambda j: (0, j)
     saved = jax.ShapeDtypeStruct((tokens, hidden), BF16)
     return pl.pallas_call(
-        backward_kernel,
+        both_ways_kernel,
+        grid=(hidden // chunk,),
+        in_specs=[pl.BlockSpec((tokens, width), whole), pl.BlockSpec((tokens, width), whole)]
+        + specs,
+        out_specs=[pl.BlockSpec((tokens, width), whole)]
+        + [pl.BlockSpec((tokens, chunk), column)] * 3,
+        out_shape=[jax.ShapeDtypeStruct((tokens, width), F32), saved, saved, saved],
+        compiler_params=params(),
+        cost_estimate=light(),
+    )(normed, grad, *operands)
+
+
+def ff_down(base, active, weights, hidden):
+    tokens, width = base.shape
+    chunk, specs, operands = weight_specs(weights, tokens, width, hidden)
+    whole = lambda j: (0, 0)
+    return pl.pallas_call(
+        down_kernel,
         grid=(hidden // chunk,),
         in_specs=[
             pl.BlockSpec((tokens, width), whole),
-            pl.BlockSpec((tokens, chunk), column),
-            pl.BlockSpec((tokens, chunk), column),
-        ]
-        + specs,
-        out_specs=[pl.BlockSpec((tokens, width), whole)]
-        + [pl.BlockSpec((tokens, chunk), column)] * 2,
-        out_shape=[jax.ShapeDtypeStruct((tokens, width), F32), saved, saved],
+            pl.BlockSpec((tokens, chunk), lambda j: (0, j)),
+            specs[2],
+        ],
+        out_specs=pl.BlockSpec((tokens, width), whole),
+        out_shape=jax.ShapeDtypeStruct((tokens, width), F32),
         compiler_params=params(),
         cost_estimate=light(),
-    )(grad, one, two, *operands)
+    )(base, active, operands[2])
 
 
 def ff_backward_outer(grad, left, one, two, weights, hidden):
@@ -531,29 +572,41 @@
     def to_peer(value):
         return lax.ppermute(value, "seq", swap)
 
-    def along(value, steps):
-        return lax.ppermute(value, "fsdp", [(i, (i + 2 * steps) % fsdp) for i in range(fsdp)])
+    def exchange(value, offset, section=None):
+        if section is None:
+            return lax.ppermute(value, "fsdp", [(i, i ^ offset) for i in range(fsdp)])
+        pairs = [
+            ((section * 2 + side) * fsdp + i, (section * 2 + side) * fsdp + (i ^ offset))
+            for side in range(2)
+            for i in range(fsdp)
+        ]
+        return lax.ppermute(value, ("section", "seq", "fsdp"), pairs)
 
     def gather(shards):
-        results, sent = ([], [])
-        for number, shard in enumerate(shards):
+        results = []
+        for shard in shards:
             depth, columns = shard.shape
             half = depth // 2
             mine = lax.dynamic_slice_in_dim(shard, part * half, half, 0)
-            if number >= 1:
-                tied = sent[0] if number == 1 else sent[number - 2]
-                mine, unused = lax.optimization_barrier((mine, tied))
-            arrived = [along(mine, step) for step in range(1, chips)]
-            sent.append(arrived)
-            crossed = [to_peer(piece) for piece in arrived]
+            if results:
+                mine = after(mine, results[-1])
+            batches = [([0], mine[None])]
+            for bit in reversed(range(chips.bit_length() - 1)):
+                offsets = [offset ^ (1 << bit) for known, rows_of in batches for offset in known]
+                block_of = jnp.concatenate([rows_of for known, rows_of in batches], axis=0)
+                batches.append((offsets, exchange(block_of, 2 << bit)))
+            arrived = batches[1:]
             held = jnp.zeros((chips, 2, half, columns), BF16)
             held = lax.dynamic_update_slice(
                 held, shard.reshape(1, 2, half, columns), (chip, 0, 0, 0)
             )
-            for step, near, far in zip(range(1, chips), arrived, crossed):
-                source = (chip - step) % chips
-                held = lax.dynamic_update_slice(held, near[None, None], (source, part, 0, 0))
-                held = lax.dynamic_update_slice(held, far[None, None], (source, 1 - part, 0, 0))
+            for known, near in arrived:
+                far = to_peer(near)
+                for index, offset in enumerate(known):
+                    for value, where in ((near, part), (far, 1 - part)):
+                        held = lax.dynamic_update_slice(
+                            held, value[index][None, None], (chip ^ offset, where, 0, 0)
+                        )
             other = to_core(held)
             full = jnp.broadcast_to(held[:, None], (chips, 2, 2, half, columns))
             full = lax.dynamic_update_slice(full, other[:, None], (0, 1 - core, 0, 0, 0))
@@ -603,26 +656,11 @@
     def crossed(staying, came):
         return (staying.astype(F32) + came.astype(F32)).astype(BF16)
 
-    def pieces(own):
-        return [
-            lax.dynamic_index_in_dim(own, (chip + step) % chips, 0, keepdims=False)
-            for step in range(chips)
-        ]
-
     def fence(*groups):
         return lax.optimization_barrier(groups)
 
     def together(values, *others):
         return lax.optimization_barrier((*values, *others))[: len(values)]
-
-    def reduce_small(value):
-        value = value + to_core(value)
-        value = value + to_peer(value)
-        step = 2
-        while step < fsdp:
-            value = value + lax.ppermute(value, "fsdp", [(i, i ^ step) for i in range(fsdp)])
-            step *= 2
-        return value
 
     def zeros(*shape, kind=BF16):
         return jnp.zeros(shape, kind)
@@ -717,10 +755,8 @@
         resid = source + matmul(heads, w_out)
         scale_two = rms_scale(resid)
         normed_two = (resid * scale_two * gains[1]).astype(BF16)
-        result, active, one, two = ff_forward(normed_two, resid, wide_weights, hidden)
-
         grad_ff = cotangent[0].reshape(total, width)
-        grad_two, dgate, dup = ff_backward(grad_ff, one, two, wide_weights, hidden)
+        grad_two, active, dgate, dup = ff_both_ways(normed_two, grad_ff, wide_weights, hidden)
         gain_two = jnp.sum(grad_two * resid * scale_two, axis=0)
         grad_resid = grad_ff.astype(F32) + norm_back(grad_two, resid, scale_two, gains[1])
         dmix = grad_resid.astype(BF16)
@@ -739,11 +775,12 @@
         gain_one = jnp.sum(grad_one * source * scale_one, axis=0)
         grad_source = grad_resid + norm_back(grad_one, source, scale_one, gains[0])
         small = jnp.concatenate(
-            [gain_one[None], gain_two[None], kernel_grad, jnp.zeros((3, width), F32)], axis=0
+            [jnp.zeros((2, width), F32), gain_one[None], gain_two[None], kernel_grad,
+             jnp.zeros((1, width), F32)], axis=0
         )
         lefts = (normed, heads, normed_two, active)
         moved = (dproj, dgate_c, dmix, dgate, dup)
-        return (result, lefts, moved, small, grad_source.astype(BF16))
+        return (resid, lefts, moved, small, grad_source.astype(BF16))
 
     def attention_idle():
         flat = lambda: zeros(total, width)
@@ -752,7 +789,7 @@
         moved = (zeros(total, 2 * width), flat(), flat(), wide(), wide())
         return (zeros(total, width, kind=F32), lefts, moved, zeros(8, width, kind=F32), flat())
 
-    outputs, lefts, moved, conv_small, grad_link = lax.cond(first, attention_idle, conv_both)
+    conv_resid, lefts, moved, conv_small, grad_link = lax.cond(first, attention_idle, conv_both)
     normed, heads, normed_two, active_both = together(lefts, grad_link)
     grad_link = lax.ppermute(grad_link, "section", [(1, 0)])
     conv_dproj, dgate_c, conv_dmix, conv_dgate, conv_dup = moved
@@ -767,10 +804,36 @@
         return to_peer(half[0])
 
     def along_all(own):
-        return lax.all_to_all(own, "fsdp", 0, 0, axis_index_groups=groups, tiled=True)
+        return [lax.all_to_all(own, "fsdp", 0, 0, axis_index_groups=groups, tiled=True)]
+
+    class Halving:
+        def __init__(self, own):
+            self.held, self.bit = (own, 0)
+            self.split()
+
+        def split(self):
+            count, *shape = self.held.shape
+            wide = self.held.reshape(count // 2, 2, *shape)
+            side = (chip >> self.bit) % 2
+            self.leaving, self.staying = [
+                lax.dynamic_index_in_dim(wide, which, 1, keepdims=False)
+                for which in (1 - side, side)
+            ]
+
+        def send(self, section=None):
+            return exchange(self.leaving, 2 << self.bit, section)
+
+        def add(self, came):
+            last = self.staying.shape[0] == 1
+            self.held = self.staying.astype(F32) + came.astype(F32)
+            self.bit += 1
+            if not last:
+                self.held = self.held.astype(BF16)
+                self.split()
+            return self
 
     def scattered(came):
-        return jnp.sum(came.astype(F32), axis=0)
+        return sum(jnp.sum(part.astype(F32), axis=0) for part in came)
 
     def halves_of(leaving, staying):
         return sides(core_add(to_core(leaving), staying))
@@ -795,21 +858,29 @@
         grad_resid = grad_link.astype(F32) + norm_back(grad_two, resid, scale_two, gains[1])
         dmix = grad_resid.astype(BF16)
         dheads = matmul_t(dmix, weights[1]).astype(BF16)
-        up = halves_of(up_leaving, up_staying)
-        grads = attend_back(part_ref, query, own, peer, dheads, rows, stretches)
+        up, dheads = fence(halves_of(up_leaving, up_staying), dheads)
+        grads = []
+        for groups in (range(KV_HEADS // 2), range(KV_HEADS // 2, KV_HEADS)):
+            if grads:
+                grads, dheads = fence(grads, dheads)
+            grads.append(attend_back(part_ref, query, own, peer, dheads, rows, stretches, groups))
+        recv = [to_peer(half[2]) for half in grads]
+        dquery, down_kv = [
+            jnp.concatenate([half[i] for half in grads], axis=1) for i in range(2)
+        ]
+        recv = jnp.concatenate(recv, axis=1)
         blank = zeros(chips, 2 * conv_cut, width)
-        return (
-            up, gain_two, grad_resid, dmix, *grads[:2], grads[2].astype(BF16), [blank, blank],
-        )
+        return (up, gain_two, grad_resid, dmix, dquery, down_kv, recv, [blank, blank])
 
     def conv_core():
         mixed = normed.reshape(total, 2, 2 * fsdp, conv_cut)
         mixed = jnp.transpose(mixed, (0, 2, 1, 3)).reshape(total, width)
         lone = sides(core_sum(turned(mixed), dgate_c))
+        output = ff_down(conv_resid, active_both, wide_weights, hidden)
         flat = lambda: zeros(total, width, kind=F32)
         up = halves_of(up_leaving, up_staying)
         return (
-            up, zeros(width, kind=F32), flat(), conv_dmix, flat(), flat(), zeros(total, width), lone,
+            up, zeros(width, kind=F32), output, conv_dmix, flat(), flat(), zeros(total, width), lone,
         )
 
     down = crossed(down[1], down_came)
@@ -817,7 +888,7 @@
     down_came, gate_came = (along_all(down), cross(gate))
     result = lax.cond(step, attention_core, conv_core)
     down_came, gate_came, result = fence(down_came, gate_came, result)
-    up, gain_two, grad_resid, dmix, dquery, down_kv, peer_kv, lone = result
+    up, gain_two, grad_resid, dmix, dquery, down_kv, recv, lone = result
 
     def joined(*halves):
         return [jnp.concatenate(parts, axis=2) for parts in zip(*halves)]
@@ -827,25 +898,7 @@
             kept[1], dquery, down_kv, recv, cosine, sine, gain_rows(), weights[0]
         )
         inward = sides(core_sum(left_normed, dproj))
-        return (joined(inward, outward), grad_one, head_rows)
-
-    def conv_project():
-        inward = sides(core_sum(left_normed, conv_dproj))
-        return (joined(inward, outward), zeros(total, width, kind=F32), zeros(8, PAIR, kind=F32))
-
-    gate = crossed(gate[1], gate_came)
-    gate, up, lone, peer_kv = fence(gate, up, lone, peer_kv)
-    recv = only(0, peer_kv, "seq")
-    outward = sides(core_sum(left_heads, dmix))
-    gate_came = along_all(gate)
-    step, up, lone, recv, outward = fence(first, up, lone, recv, outward)
-    up_came = cross(up)
-    lone_came = only(1, lone[0], "seq")
-    result = lax.cond(step, attention_project, conv_project)
-    gate_came, up_came, lone_came, result = fence(gate_came, up_came, lone_came, result)
-    mix, grad_one, head_rows = result
-
-    def attention_ends():
+        outward = sides(core_sum(left_heads, dmix))
         source = tokens[0].reshape(total, width).astype(F32)
         scale_one = rms_scale(source)
         gain_one = jnp.sum(grad_one * source * scale_one, axis=0)
@@ -853,41 +906,59 @@
         head_grad = jnp.stack([head_rows[0, :HEAD] + head_rows[0, HEAD:], head_rows[1, :HEAD]])
         head_row = jnp.pad(head_grad.reshape(1, PAIR), ((0, 0), (0, width - PAIR)))
         small = jnp.concatenate(
-            [gain_one[None], gain_two[None], jnp.zeros((3, width), F32), head_row,
-             jnp.zeros((2, width), F32)], axis=0
+            [gain_one[None], gain_two[None], jnp.zeros((5, width), F32), head_row], axis=0
         )
-        return (grad_source, reduce_small(small))
-
-    def conv_ends():
-        return (outputs, reduce_small(conv_small))
-
-    up = crossed(up[1], up_came)
-    lone = pieces(crossed(lone[1], lone_came))
-    step, up, mix = fence(first, up, mix)
-    up_came, mix_came = (along_all(up), cross(mix))
-    result = lax.cond(step, attention_ends, conv_ends)
-    up_came, mix_came, (ends, small) = fence(up_came, mix_came, result)
-    mix_came = along_all(crossed(mix[1], mix_came))
-    lone_came = [only(1, piece, count) for count, piece in enumerate(lone[1:], 1)]
-    shard_c = sum((piece.astype(F32) for piece in lone_came), lone[0].astype(F32))
-    shard_mix = scattered(mix_came)
+        return (joined(inward, outward), grad_source, small + to_core(small))
+
+    def conv_project():
+        outward = sides(core_sum(left_heads, dmix))
+        inward = sides(core_sum(left_normed, conv_dproj))
+        output = grad_resid
+        small = conv_small + to_core(conv_small)
+        return (joined(inward, outward), output, small)
+
+    gate = crossed(gate[1], gate_came)
+    step, gate, up, lone = fence(first, gate, up, lone)
+    gate_came, up_came, lone_came = (along_all(gate), cross(up), only(1, lone[0], "seq"))
+    result = lax.cond(step, attention_project, conv_project)
+    gate_came, up_came, lone_came, result = fence(gate_came, up_came, lone_came, result)
+    mix, ends, small = result
+
+    up = Halving(crossed(up[1], up_came))
+    lone = Halving(crossed(lone[1], lone_came))
+    mix_came = cross(mix)
+    up_came, lone_came = (up.send(), lone.send(1))
+    small = small + lax.ppermute(small, "section", swap)
+    up_came, lone_came, small = fence(up_came, lone_came, small)
+    up, lone, small_came = (up.add(up_came), lone.add(lone_came), to_peer(small))
+    bits = chips.bit_length() - 1
+    for bit in range(1, bits):
+        up_came, lone_came = (up.send(), lone.send(1))
+        if bit == 1:
+            mix_came, small_came = fence(mix_came, small_came)
+            mix = Halving(crossed(mix[1], mix_came))
+            small = small + small_came
+            mix_came, small_came = (mix.send(), exchange(small, 2))
+        up_came, lone_came, mix_came, small_came = fence(
+            up_came, lone_came, mix_came, small_came
+        )
+        up, lone, mix = (up.add(up_came), lone.add(lone_came), mix.add(mix_came))
+        small = small + small_came
+        mix_came, small_came = (mix.send(), exchange(small, 2 << bit))
+    mail = lax.ppermute(lone.held[0, :conv_cut], "section", [(1, 0)])
+    mail, mix_came, small_came = fence(mail, mix_came, small_came)
+    small = small + small_came
+    shard_mix = mix.add(mix_came).held[0]
+    c_shard = jnp.where(first, mail, lone.held[0, conv_cut:])
     shards_out = (
         shard_mix[:, : 2 * width], shard_mix[:, 2 * width :],
-        scattered(gate_came), scattered(up_came), scattered(down_came),
+        scattered(gate_came), up.held[0], scattered(down_came),
     )
-    mail = lax.ppermute(
-        jnp.concatenate([shard_c, small], axis=0), "section", swap
-    )
-    c_shard = jnp.where(first, mail[:conv_cut], shard_c[conv_cut:])
-    theirs = mail[2 * conv_cut :]
-    merged_a, merged_c = (jnp.where(first, small, theirs), jnp.where(first, theirs, small))
-    grad_norm = jnp.stack([merged_a[:2], merged_c[:2]])
-    grad_head = merged_a[5, :PAIR].reshape(2, HEAD)
     return (
         ends.reshape(1, 1, stretches, rows, width),
-        grad_norm,
-        grad_head,
-        merged_c[2:5],
+        small[:4].reshape(2, 2, width),
+        small[7, :PAIR].reshape(2, HEAD),
+        small[4:7],
         *[shard[None] for shard in shards_out],
         c_shard,
     )

time: 757 us -> 717 us (0.947)
  starting transfers between devices: 81.7 us -> 47.7 us
    ppermute x9 -> x14, waiting for transfers between devices: 28.7 us -> 99 us  [the longest x10 95.5 us: exchange(): return lax.ppermute(value, 'fsdp', [(i, i ^ offset) for i in range(fsdp)])]
    all_gather x1, waiting for transfers between devices: 33.4 us -> 9.74 us  [local(): lax.all_gather(pack_halves(*halves), ('fsdp', 'seq'), axis=0)]
    ppermute x5 -> x1, waiting for transfers between devices: 22.6 us -> 0.01 us  [only(): return lax.ppermute(value, ('section', 'seq', 'fsdp'), pairs)]
    ppermute x9 -> x14, starting transfers between devices: 35.3 us -> 15.5 us  [the longest x10 12.8 us: exchange(): return lax.ppermute(value, 'fsdp', [(i, i ^ offset) for i in range(fsdp)])]
    ppermute x1, waiting for transfers between devices: 101 us -> 87.2 us  [local(): grad_link = lax.ppermute(grad_link, 'section', [(1, 0)])]
    all_to_all x4 -> x2, starting transfers between devices: 17.8 us -> 9.63 us  [along_all(): lax.all_to_all(own, 'fsdp', 0, 0, axis_index_groups=groups, tiled=True)]
    another operation x18 -> x15, local copies, waits for them, and re-layouts: 17.2 us -> 14.4 us
    pallas_call x1 -> x2, Pallas kernels: 34.4 us -> 36.1 us  [attend_back(): pl.pallas_call(functools.partial(attend_back_kernel, rows, stretches), gr...]
  transfers between devices with their start and end apart: 42 -> 41, of which waited for: 24 -> 23; matrix products, arithmetic and copies ran while one was open for 16% -> 15% of each run, Pallas kernels for 17% -> 18%
where the time goes in v3:
time: 717 us; the launch traced here: 710 us
  waiting for transfers between devices  325 us (45%)
  Pallas kernels  153 us (21%)
  local copies, waits for them, and re-layouts  65.1 us (9%)
  other arithmetic  64.4 us (9%)
  starting transfers between devices  47.7 us (7%)
  matrix products  30.2 us (4%)
  between operations  15.1 us (2%)
  loops' own time  9.1 us (1%)
    ppermute x10, waiting for transfers between devices, exchange(): return lax.ppermute(value, 'fsdp', [(i, i ^ offset) for i in range(fsdp)])  95.5 us
    ppermute x12, waiting for transfers between devices, to_peer(): return lax.ppermute(value, 'seq', swap)  91.1 us
    ppermute x1, waiting for transfers between devices, local(): grad_link = lax.ppermute(grad_link, 'section', [(1, 0)])  87.2 us
    pallas_call x1, Pallas kernels, ff_backward_outer(): pl.pallas_call(backward_outer_kernel, grid=(hidden // chunk,), in_specs=[...  36.5 us
    pallas_call x2, Pallas kernels, attend_back(): pl.pallas_call(functools.partial(attend_back_kernel, rows, stretches), gr...  36.1 us
    pallas_call x1, Pallas kernels, ff_forward(): pl.pallas_call(forward_kernel, grid=(hidden // chunk,), in_specs=[pl.Bloc...  26 us
    dot_general x7, matrix products, matmul(): return jnp.dot(left, right, preferred_element_type=F32)  25.9 us
    pallas_call x1, Pallas kernels, attend(): pl.pallas_call(functools.partial(attend_kernel, rows, stretches), grid=(K...  20.2 us
  transfers between devices with their start and end apart: 41, of which 23 were waited for; matrix products, arithmetic and copies ran while one was open for 15% of the time, Pallas kernels for 18%

profile of v3, /device:TPU:0, one launch (start us, length us, event | category | flops | bytes accessed | tf_op | source)
XLA Modules:
  0.0 710.3 jit_solution(11236938260831582343)
XLA Ops:
  18.9 176.9 %conditional.6 = (bf16[1024,2048]{1,0:T(8,128)(2,1)}, bf16[1024,1024]{1,0:T(8,128)(2,1)}, bf16[1024,1024]{1,0:T(8,128)(2,1)}, bf16[512,1024]{1,0:T(8,128)(2,1)},...) conditional(s32[]{:T(128)} %convert_element_type.322, ...), branch_computations={%region_0.1_spmd, %region_1.4_spmd} | conditional | flops 1083707520 | bytes 93130544 | solution.py:723
  22.7 13.9 %collective-permute-done.17 = bf16[1,64,2048]{2,1,0:T(8,128)(2,1)S(1)} collective-permute-done((bf16[1,64,2048]{2,1,0:T(8,128)(2,1)S(1)}, bf16[1,64,2048]{2,1,0:T(8,128)(2,1)S(1)}, u32[]{:S(2)}, u32[]{:S(2)}) %collective-permute-start.17) | collective-permute-done | bytes 262176 | tf_op jit(solution)/shard_map/cond/branch_1_fun/ppermute | solution.py:577
  41.6 15.3 %collective-permute-done.19 = bf16[2,64,2048]{2,1,0:T(8,128)(2,1)} collective-permute-done((bf16[2,64,2048]{2,1,0:T(8,128)(2,1)}, bf16[2,64,2048]{2,1,0:T(8,128)(2,1)}, u32[]{:S(2)}, u32[]{:S(2)}) %collective-permute-start.19) | collective-permute-done | bytes 524320 | tf_op jit(solution)/shard_map/cond/branch_1_fun/ppermute | solution.py:577
  59.6 16.3 %collective-permute-done.20 = bf16[2,64,2048]{2,1,0:T(8,128)(2,1)S(1)} collective-permute-done((bf16[2,64,2048]{2,1,0:T(8,128)(2,1)}, bf16[2,64,2048]{2,1,0:T(8,128)(2,1)S(1)}, u32[]{:S(2)}, u32[]{:S(2)}) %collective-permute-start.20) | collective-permute-done | bytes 524320 | tf_op jit(solution)/shard_map/cond/branch_1_fun/ppermute | solution.py:573
  88.3 10.0 %collective-permute-done.22 = bf16[1,64,1024]{2,1,0:T(8,128)(2,1)S(1)} collective-permute-done((bf16[1,64,1024]{2,1,0:T(8,128)(2,1)S(1)}, bf16[1,64,1024]{2,1,0:T(8,128)(2,1)S(1)}, u32[]{:S(2)}, u32[]{:S(2)}) %collective-permute-start.22) | collective-permute-done | bytes 131104 | tf_op jit(solution)/shard_map/cond/branch_1_fun/ppermute | solution.py:577
  99.3 15.2 %branch_1_fun.7 = (bf16[512,2048]{1,0:T(8,128)(2,1)}, bf16[512,1024]{1,0:T(8,128)(2,1)S(1)}, bf16[512,1024]{1,0:T(8,128)(2,1)S(1)}) custom-call(bf16[512,1024]{1,0:T(8,128)(2,1)} %fusion.14.x_ref, bf16[1024,2048]{1,0:T(8,128)(2,1)} %bitcast.38.w_ref, f32[512,128]{1,0:T(8,128)S(1)} %get-tuple-element.691.cos_ref, f32[512,128]{1,0:T(8,128)S(1)} %get-tuple-element.692.sin_ref, ...), custom_call_target="tpu_custom_call" | custom-call | flops 1048576 | bytes 1048576 | tf_op jit(solution)/shard_map/cond/branch_1_fun/pallas_call | solution.py:84
  118.6 37.5 %collective-permute-done.23 = bf16[1,64,1024]{2,1,0:T(8,128)(2,1)S(1)} collective-permute-done((bf16[1,64,1024]{2,1,0:T(8,128)(2,1)S(1)}, bf16[1,64,1024]{2,1,0:T(8,128)(2,1)S(1)}, u32[]{:S(2)}, u32[]{:S(2)}) %collective-permute-start.23) | collective-permute-done | bytes 131104 | tf_op jit(solution)/shard_map/cond/branch_1_fun/ppermute | solution.py:573
  164.0 20.2 %branch_1_fun.8 = bf16[512,1024]{1,0:T(8,128)(2,1)S(1)} custom-call(s32[1]{0:T(128)} %get-tuple-element.230.part_ref, bf16[512,1024]{1,0:T(8,128)(2,1)S(1)} %get-tuple-element.685.q_ref, bf16[512,1024]{1,0:T(8,128)(2,1)S(1)} %get-tuple-element.686.own_ref, bf16[512,1024]{1,0:T(8,128)(2,1)S(1)} %collective-permute-done.27.peer_ref), custom_call_target="tpu_custom_call" | custom-call | flops 1048576 | bytes 1048576 | tf_op jit(solution)/shard_map/cond/branch_1_fun/pallas_call | solution.py:136
  205.5 27.9 %conditional.7 = (bf16[512,1024]{1,0:T(8,128)(2,1)S(1)}, bf16[512,4608]{1,0:T(8,128)(2,1)}, bf16[512,4608]{1,0:T(8,128)(2,1)}, bf16[512,4608]{1,0:T(8,128)(2,1)}) conditional(s32[]{:T(128)} %convert_element_type.322, () %tuple.80, (bf16[512,1024]{1,0:T(8,128)(2,1)}, f32[512,1024]{1,0:T(8,128)}, bf16[16,6912,128]{2,1,0:T(8,128)(2,1)}) %tuple.166), branch_computations={%region_4.5_spmd, %region_5.6_spmd} | conditional | flops 1572864 | bytes 15204392 | solution.py:732
  205.7 26.0 %branch_1_fun.9 = (f32[512,1024]{1,0:T(8,128)}, bf16[512,4608]{1,0:T(8,128)(2,1)}, bf16[512,4608]{1,0:T(8,128)(2,1)}, bf16[512,4608]{1,0:T(8,128)(2,1)}) custom-call(bf16[512,1024]{1,0:T(8,128)(2,1)} %get-tuple-element.231.x_ref, f32[512,1024]{1,0:T(8,128)} %get-tuple-element.232.base_ref, bf16[16,6912,128]{2,1,0:T(8,128)(2,1)} %get-tuple-element.233.g_ref.u_ref.d_ref, ...), custom_call_target="tpu_custom_call" | custom-call | flops 1048576 | bytes 1048576 | tf_op jit(solution)/shard_map/cond/branch_1_fun/pallas_call | solution.py:445
  234.8 15.9 %collective-permute-done.42 = bf16[512,1024]{1,0:T(8,128)(2,1)S(1)} collective-permute-done((bf16[512,1024]{1,0:T(8,128)(2,1)S(1)}, bf16[512,1024]{1,0:T(8,128)(2,1)S(1)}, u32[]{:S(2)}, u32[]{:S(2)}) %collective-permute-start.42) | collective-permute-done | bytes 1048608 | tf_op jit(solution)/shard_map/ppermute | solution.py:733
  250.7 17.1 %conditional.8 = (f32[512,1024]{1,0:T(8,128)S(1)}, bf16[512,1024]{1,0:T(8,128)(2,1)}, bf16[512,1024]{1,0:T(8,128)(2,1)}, bf16[512,1024]{1,0:T(8,128)(2,1)}, bf16...) conditional(s32[]{:T(128)} %convert_element_type.322, ...), branch_computations={%region_6.16_spmd, %region_16.17_spmd} | conditional | flops 8648138752 | bytes 231228064 | solution.py:792
  280.0 87.2 %collective-permute-done.43 = bf16[512,1024]{1,0:T(8,128)(2,1)} collective-permute-done((bf16[512,1024]{1,0:T(8,128)(2,1)}, bf16[512,1024]{1,0:T(8,128)(2,1)}, u32[]{:S(2)}, u32[]{:S(2)}) %collective-permute-start.43) | collective-permute-done | bytes 1048608 | tf_op jit(solution)/shard_map/ppermute | solution.py:794
  391.6 50.4 %conditional.9 = (f32[512,1024]{1,0:T(8,128)}, bf16[4,64,4608]{2,1,0:T(8,128)(2,1)S(1)}, bf16[4,64,4608]{2,1,0:T(8,128)(2,1)S(1)}, bf16[512,4608]{1,0:T(8,128)(2,1)}, bf16[512,4608]{1,0:T(8,128)(2,1)}) conditional(s32[]{:T(128)} %convert_element_type.327, (bf16[1024,512]{1,0:T(8,128)(2,1)S(1)}, bf16[512,4608]{1,0:T(8,128)(2,1)}, ...), branch_computations={%region_17.18_spmd, %region_18.19_spmd} | conditional | flops 10485767 | bytes 45613224 | solution.py:851
  392.0 36.5 %branch_1_fun.10 = (f32[512,1024]{1,0:T(8,128)}, bf16[512,4608]{1,0:T(8,128)(2,1)}, bf16[512,4608]{1,0:T(8,128)(2,1)}, bf16[512,4608]{1,0:T(8,128)(2,1)}, bf16[512,4608]{1,0:T(8,128)(2,1)}) custom-call(bf16[512,1024]{1,0:T(8,128)(2,1)} %get-tuple-element.263.grad_ref, bf16[1024,512]{1,0:T(8,128)(2,1)S(1)} %get-tuple-element.264.left_ref, ...), custom_call_target="tpu_custom_call" | custom-call | flops 1048576 | bytes 1048576 | tf_op jit(solution)/shard_map/cond/branch_1_fun/pallas_call | solution.py:502
  455.6 85.0 %conditional.10 = (bf16[4,64,4608]{2,1,0:T(8,128)(2,1)}, bf16[4,64,4608]{2,1,0:T(8,128)(2,1)}, f32[1024]{0:T(1024)S(1)}, f32[512,1024]{1,0:T(8,128)}, bf16[512,1...) conditional(s32[]{:T(128)} %convert_element_type.331, ...), branch_computations={%region_19.20_spmd, %region_20.24_spmd} | conditional | flops 1097858560 | bytes 102275520 | solution.py:889
  476.7 17.9 %branch_1_fun.11 = (f32[512,512]{1,0:T(8,128)}, f32[512,512]{1,0:T(8,128)}, bf16[512,512]{1,0:T(8,128)(2,1)}) custom-call(s32[1]{0:T(128)} %get-tuple-element.294.part_ref, bf16[512,1024]{1,0:T(8,128)(2,1)S(1)} %get-tuple-element.295.q_ref, bf16[512,1024]{1,0:T(8,128)(2,1)S(1)} %copy-done.13, bf16[512,1024]{1,0:T(8,128)(2,1)S(1)} %copy-done.15, ...), custom_call_target="tpu_custom_call" | custom-call | flops 1048576 | bytes 1048576 | tf_op jit(solution)/shard_map/cond/branch_1_fun/pallas_call | solution.py:194
  494.6 18.1 %branch_1_fun.12 = (f32[512,512]{1,0:T(8,128)}, f32[512,512]{1,0:T(8,128)}, bf16[512,512]{1,0:T(8,128)(2,1)}) custom-call(s32[1]{0:T(128)} %get-tuple-element.294.part_ref, bf16[512,1024]{1,0:T(8,128)(2,1)S(1)} %get-tuple-element.295.q_ref, bf16[512,1024]{1,0:T(8,128)(2,1)S(1)} %copy-done.13, bf16[512,1024]{1,0:T(8,128)(2,1)S(1)} %copy-done.15, ...), custom_call_target="tpu_custom_call" | custom-call | flops 1048576 | bytes 1048576 | tf_op jit(solution)/shard_map/cond/branch_1_fun/pallas_call | solution.py:194
  527.7 10.8 %collective-permute-done.33 = bf16[512,512]{1,0:T(8,128)(2,1)S(1)} collective-permute-done((bf16[512,512]{1,0:T(8,128)(2,1)S(1)}, bf16[512,512]{1,0:T(8,128)(2,1)S(1)}, u32[]{:S(2)}, u32[]{:S(2)}) %collective-permute-start.33) | collective-permute-done | bytes 524320 | tf_op jit(solution)/shard_map/cond/branch_1_fun/ppermute | solution.py:573
  559.4 40.4 %conditional.11 = (bf16[4,64,3072]{2,1,0:T(8,128)(2,1)S(1)}, bf16[4,64,3072]{2,1,0:T(8,128)(2,1)S(1)}, f32[512,1024]{1,0:T(8,128)}, f32[8,1024]{1,0:T(8,128)S(1)}) conditional(s32[]{:T(128)} %convert_element_type.334, (bf16[512,512]{1,0:T(8,128)(2,1)}, bf16[512,2048]{1,0:T(8,128)(2,1)}, bf16[512,512]{1,0:T(8,128)(2,1)}, s32[]{:T(128)}, ...), branch_computations={%region_24.25_spmd, %region_25.29_spmd} | conditional | flops 3244383744 | bytes 83139888 | solution.py:923
  560.4 19.2 %branch_1_fun.13 = (bf16[512,2048]{1,0:T(8,128)(2,1)}, f32[512,1024]{1,0:T(8,128)}, f32[8,128]{1,0:T(8,128)}) custom-call(bf16[512,2048]{1,0:T(8,128)(2,1)} %get-tuple-element.318.raw_ref, f32[512,1024]{1,0:T(8,128)} %get-tuple-element.319.dq_ref, f32[512,1024]{1,0:T(8,128)} %get-tuple-element.320.own_ref, bf16[512,1024]{1,0:T(8,128)(2,1)} %get-tuple-element.321.recv_ref, ...), custom_call_target="tpu_custom_call" | custom-call | flops 1048576 | bytes 1048576 | tf_op jit(solution)/shard_map/cond/branch_1_fun/pallas_call | solution.py:249
  616.5 20.2 %collective-permute-done.49 = bf16[2,64,4608]{2,1,0:T(8,128)(2,1)} collective-permute-done((bf16[2,64,4608]{2,1,0:T(8,128)(2,1)}, bf16[2,64,4608]{2,1,0:T(8,128)(2,1)}, u32[]{:S(2)}, u32[]{:S(2)}) %collective-permute-start.49) | collective-permute-done | bytes 1179680 | tf_op jit(solution)/shard_map/ppermute | solution.py:577
  656.9 22.4 %collective-permute-done.57 = f32[8,1024]{1,0:T(8,128)S(1)} collective-permute-done((f32[8,1024]{1,0:T(8,128)S(1)}, f32[8,1024]{1,0:T(8,128)S(1)}, u32[]{:S(2)}, u32[]{:S(2)}) %collective-permute-start.57) | collective-permute-done | bytes 32800 | tf_op jit(solution)/shard_map/ppermute | solution.py:577
  685.1 13.7 %collective-permute-done.60 = f32[8,1024]{1,0:T(8,128)S(1)} collective-permute-done((f32[8,1024]{1,0:T(8,128)S(1)}, f32[8,1024]{1,0:T(8,128)S(1)}, u32[]{:S(2)}, u32[]{:S(2)}) %collective-permute-start.60) | collective-permute-done | bytes 32800 | tf_op jit(solution)/shard_map/ppermute | solution.py:577
  (303 shorter events, 269.8 us)
Async XLA Ops:
  7.2 198.3 %all-gather.3.cloned.1.call-start = ((), (), s32[]{:S(2)}) async-start(), calls=%async_computation.2 | async-start | bytes 30081024 | tf_op jit(solution)/shard_map/all_gather | solution.py:676
  37.5 19.5 %collective-permute-start.19 = (bf16[2,64,2048]{2,1,0:T(8,128)(2,1)}, bf16[2,64,2048]{2,1,0:T(8,128)(2,1)}, u32[]{:S(2)}, u32[]{:S(2)}) collective-permute-start(bf16[2,64,2048]{2,1,0:T(8,128)(2,1)} %pad_maximum_fusion.4), channel_id=1, source_target_pairs={{0,2},{1,3},{2,0},{3,1},{4,6},{5,7},{6,4},{7,5},{8,10},{9,11},{10,... | collective-permute-start | bytes 1572872 | tf_op jit(solution)/shard_map/cond/branch_1_fun/ppermute | solution.py:577
  39.0 19.6 %collective-permute-start.18 = (bf16[1,64,2048]{2,1,0:T(8,128)(2,1)}, bf16[1,64,2048]{2,1,0:T(8,128)(2,1)S(1)}, u32[]{:S(2)}, u32[]{:S(2)}) collective-permute-start(bf16[1,64,2048]{2,1,0:T(8,128)(2,1)} %copy-done.48), channel_id=1, source_target_pairs={{0,8},{8,0},{1,9},{9,1},{2,10},{10,2},{3,11},{11,3},{4,12},{12,4},... | collective-permute-start | bytes 786440 | tf_op jit(solution)/shard_map/cond/branch_1_fun/ppermute | solution.py:573
  57.0 19.0 %collective-permute-start.20 = (bf16[2,64,2048]{2,1,0:T(8,128)(2,1)}, bf16[2,64,2048]{2,1,0:T(8,128)(2,1)S(1)}, u32[]{:S(2)}, u32[]{:S(2)}) collective-permute-start(bf16[2,64,2048]{2,1,0:T(8,128)(2,1)} %collective-permute-done.19), channel_id=1, source_target_pairs={{0,8},{8,0},{1,9},{9,1},{2,10},{10,2},{3,11},{11,3},{4,12},{12,4},... | collective-permute-start | bytes 1572872 | tf_op jit(solution)/shard_map/cond/branch_1_fun/ppermute | solution.py:573
  98.4 18.3 %collective-permute-start.24 = (bf16[2,64,1024]{2,1,0:T(8,128)(2,1)S(1)}, bf16[2,64,1024]{2,1,0:T(8,128)(2,1)S(1)}, u32[]{:S(2)}, u32[]{:S(2)}) collective-permute-start(bf16[2,64,1024]{2,1,0:T(8,128)(2,1)S(1)} %pad_maximum_fusion.5), channel_id=1, source_target_pairs={{0,2},{1,3},{2,0},{3,1},{4,6},{5,7},{6,4},{7,5},{8,10},{9,11},{10,... | collective-permute-start | bytes 786440 | tf_op jit(solution)/shard_map/cond/branch_1_fun/ppermute | solution.py:577
  114.6 49.4 %collective-permute-start.27 = (bf16[512,1024]{1,0:T(8,128)(2,1)S(1)}, bf16[512,1024]{1,0:T(8,128)(2,1)S(1)}, u32[]{:S(2)}, u32[]{:S(2)}) collective-permute-start(bf16[512,1024]{1,0:T(8,128)(2,1)S(1)} %get-tuple-element.686.own_ref), channel_id=1, source_target_pairs={{0,8},{8,0},{1,9},{9,1},{2,10},{10,2},{3,11},{11,3},{4,12},{12,4},... | collective-permute-start | bytes 3145736 | tf_op jit(solution)/shard_map/cond/branch_1_fun/ppermute | solution.py:573
  116.5 39.6 %collective-permute-start.23 = (bf16[1,64,1024]{2,1,0:T(8,128)(2,1)S(1)}, bf16[1,64,1024]{2,1,0:T(8,128)(2,1)S(1)}, u32[]{:S(2)}, u32[]{:S(2)}) collective-permute-start(bf16[1,64,1024]{2,1,0:T(8,128)(2,1)S(1)} %collective-permute-done.22), channel_id=1, source_target_pairs={{0,8},{8,0},{1,9},{9,1},{2,10},{10,2},{3,11},{11,3},{4,12},{12,4},... | collective-permute-start | bytes 393224 | tf_op jit(solution)/shard_map/cond/branch_1_fun/ppermute | solution.py:573
  116.7 47.1 %collective-permute-start.25 = (bf16[2,64,1024]{2,1,0:T(8,128)(2,1)S(1)}, bf16[2,64,1024]{2,1,0:T(8,128)(2,1)S(1)}, u32[]{:S(2)}, u32[]{:S(2)}) collective-permute-start(bf16[2,64,1024]{2,1,0:T(8,128)(2,1)S(1)} %collective-permute-done.24), channel_id=1, source_target_pairs={{0,8},{8,0},{1,9},{9,1},{2,10},{10,2},{3,11},{11,3},{4,12},{12,4},... | collective-permute-start | bytes 786440 | tf_op jit(solution)/shard_map/cond/branch_1_fun/ppermute | solution.py:573
  163.9 20.4 %collective-permute-start.26 = (bf16[4,2,64,1024]{3,2,1,0:T(8,128)(2,1)S(1)}, bf16[4,2,64,1024]{3,2,1,0:T(8,128)(2,1)S(1)}, u32[]{:S(2)}, u32[]{:S(2)}) collective-permute-start(bf16[4,2,64,1024]{3,2,1,0:T(8,128)(2,1)S(1)} %fusion.20), channel_id=1, source_target_pairs={{0,1},{1,0},{2,3},{3,2},{4,5},{5,4},{6,7},{7,6},{8,9},{9,8},{10,11... | collective-permute-start | bytes 3145736 | tf_op jit(solution)/shard_map/cond/branch_1_fun/ppermute | solution.py:570
  267.8 99.4 %collective-permute-start.43 = (bf16[512,1024]{1,0:T(8,128)(2,1)}, bf16[512,1024]{1,0:T(8,128)(2,1)}, u32[]{:S(2)}, u32[]{:S(2)}) collective-permute-start(bf16[512,1024]{1,0:T(8,128)(2,1)} %get-tuple-element.464), channel_id=1, source_target_pairs={{16,0},{17,1},{18,2},{19,3},{20,4},{21,5},{22,6},{23,7},{24,8},{25... | collective-permute-start | bytes 3145736 | tf_op jit(solution)/shard_map/ppermute | solution.py:794
  389.7 53.6 %collective-permute-start.45 = (bf16[4,288,1024]{2,1,0:T(8,128)(2,1)}, bf16[4,288,1024]{2,1,0:T(8,128)(2,1)}, u32[]{:S(2)}, u32[]{:S(2)}) collective-permute-start(bf16[4,288,1024]{2,1,0:T(8,128)(2,1)} %get-tuple-element.467), channel_id=1, source_target_pairs={{0,8},{8,0},{1,9},{9,1},{2,10},{10,2},{3,11},{11,3},{4,12},{12,4},... | collective-permute-start | bytes 7077896 | tf_op jit(solution)/shard_map/ppermute | solution.py:573
  449.1 91.6 %all-to-all-start = ((bf16[4,288,1024]{2,1,0:T(8,128)(2,1)}), bf16[4,288,1024]{2,1,0:T(8,128)(2,1)}, u32[]{:S(2)}, u32[]{:S(2)}) async-start(bf16[4,288,1024]{2,1,0:T(8,128)(2,1)} %add_convert_fusion.11), calls=%async_computation | async-start | bytes 4718592 | tf_op jit(solution)/shard_map/all_to_all | solution.py:807
  453.7 86.9 %collective-permute-start.46 = (bf16[4,64,4608]{2,1,0:T(8,128)(2,1)}, bf16[4,64,4608]{2,1,0:T(8,128)(2,1)}, u32[]{:S(2)}, u32[]{:S(2)}) collective-permute-start(bf16[4,64,4608]{2,1,0:T(8,128)(2,1)} %copy-done.41), channel_id=1, source_target_pairs={{0,8},{8,0},{1,9},{9,1},{2,10},{10,2},{3,11},{11,3},{4,12},{12,4},... | collective-permute-start | bytes 7077896 | tf_op jit(solution)/shard_map/ppermute | solution.py:573
  513.0 25.6 %collective-permute-start.33 = (bf16[512,512]{1,0:T(8,128)(2,1)S(1)}, bf16[512,512]{1,0:T(8,128)(2,1)S(1)}, u32[]{:S(2)}, u32[]{:S(2)}) collective-permute-start(bf16[512,512]{1,0:T(8,128)(2,1)S(1)} %copy-done.68), channel_id=1, source_target_pairs={{0,8},{8,0},{1,9},{9,1},{2,10},{10,2},{3,11},{11,3},{4,12},{12,4},... | collective-permute-start | bytes 1572872 | tf_op jit(solution)/shard_map/cond/branch_1_fun/ppermute | solution.py:573
  545.4 58.7 %all-to-all-start.1 = ((bf16[4,64,4608]{2,1,0:T(8,128)(2,1)}), bf16[4,64,4608]{2,1,0:T(8,128)(2,1)S(1)}, u32[]{:S(2)}, u32[]{:S(2)}) async-start(bf16[4,64,4608]{2,1,0:T(8,128)(2,1)} %add_convert_fusion.10), calls=%async_computation.1 | async-start | bytes 4718592 | tf_op jit(solution)/shard_map/all_to_all | solution.py:807
  550.4 52.9 %collective-permute-start.47 = (bf16[4,64,4608]{2,1,0:T(8,128)(2,1)}, bf16[4,64,4608]{2,1,0:T(8,128)(2,1)}, u32[]{:S(2)}, u32[]{:S(2)}) collective-permute-start(bf16[4,64,4608]{2,1,0:T(8,128)(2,1)} %get-tuple-element.512), channel_id=1, source_target_pairs={{0,8},{8,0},{1,9},{9,1},{2,10},{10,2},{3,11},{11,3},{4,12},{12,4},... | collective-permute-start | bytes 7077896 | tf_op jit(solution)/shard_map/ppermute | solution.py:573
  550.6 49.2 %collective-permute-start.48 = (bf16[4,64,1024]{2,1,0:T(8,128)(2,1)}, bf16[4,64,1024]{2,1,0:T(8,128)(2,1)}, u32[]{:S(2)}, u32[]{:S(2)}) collective-permute-start(bf16[4,64,1024]{2,1,0:T(8,128)(2,1)} %get-tuple-element.513), channel_id=1, source_target_pairs={{16,24},{17,25},{18,26},{19,27},{20,28},{21,29},{22,30},{23,31},{2... | collective-permute-start | bytes 1572872 | tf_op jit(solution)/shard_map/ppermute | solution.py:649
  609.5 27.2 %collective-permute-start.49 = (bf16[2,64,4608]{2,1,0:T(8,128)(2,1)}, bf16[2,64,4608]{2,1,0:T(8,128)(2,1)}, u32[]{:S(2)}, u32[]{:S(2)}) collective-permute-start(bf16[2,64,4608]{2,1,0:T(8,128)(2,1)} %dynamic-slice_bitcast_fusion.22), channel_id=1, source_target_pairs={{0,2},{1,3},{2,0},{3,1},{4,6},{5,7},{6,4},{7,5},{8,10},{9,11},{10,... | collective-permute-start | bytes 3538952 | tf_op jit(solution)/shard_map/ppermute | solution.py:577
  612.7 36.0 %collective-permute-start.52 = (bf16[4,64,3072]{2,1,0:T(8,128)(2,1)}, bf16[4,64,3072]{2,1,0:T(8,128)(2,1)S(1)}, u32[]{:S(2)}, u32[]{:S(2)}) collective-permute-start(bf16[4,64,3072]{2,1,0:T(8,128)(2,1)} %copy-done.47), channel_id=1, source_target_pairs={{0,8},{8,0},{1,9},{9,1},{2,10},{10,2},{3,11},{11,3},{4,12},{12,4},... | collective-permute-start | bytes 4718600 | tf_op jit(solution)/shard_map/ppermute | solution.py:573
  639.1 40.2 %collective-permute-start.54 = (bf16[1,64,4608]{2,1,0:T(8,128)(2,1)S(1)}, bf16[1,64,4608]{2,1,0:T(8,128)(2,1)S(1)}, u32[]{:S(2)}, u32[]{:S(2)}) collective-permute-start(bf16[1,64,4608]{2,1,0:T(8,128)(2,1)S(1)} %constant_dynamic-slice_fusion.7), channel_id=1, source_target_pairs={{0,4},{1,5},{2,6},{3,7},{4,0},{5,1},{6,2},{7,3},{8,12},{9,13},{10,... | collective-permute-start | bytes 1769480 | tf_op jit(solution)/shard_map/ppermute | solution.py:577
  649.4 29.9 %collective-permute-start.56 = (bf16[2,64,3072]{2,1,0:T(8,128)(2,1)S(1)}, bf16[2,64,3072]{2,1,0:T(8,128)(2,1)S(1)}, u32[]{:S(2)}, u32[]{:S(2)}) collective-permute-start(bf16[2,64,3072]{2,1,0:T(8,128)(2,1)S(1)} %dynamic-slice_bitcast_fusion.23), channel_id=1, source_target_pairs={{0,2},{1,3},{2,0},{3,1},{4,6},{5,7},{6,4},{7,5},{8,10},{9,11},{10,... | collective-permute-start | bytes 2359304 | tf_op jit(solution)/shard_map/ppermute | solution.py:577
  654.5 24.7 %collective-permute-start.57 = (f32[8,1024]{1,0:T(8,128)S(1)}, f32[8,1024]{1,0:T(8,128)S(1)}, u32[]{:S(2)}, u32[]{:S(2)}) collective-permute-start(f32[8,1024]{1,0:T(8,128)S(1)} %add.493), channel_id=1, source_target_pairs={{0,2},{1,3},{2,0},{3,1},{4,6},{5,7},{6,4},{7,5},{8,10},{9,11},{10,... | collective-permute-start | bytes 98312 | tf_op jit(solution)/shard_map/ppermute | solution.py:577
  679.5 19.2 %collective-permute-start.59 = (bf16[1,64,3072]{2,1,0:T(8,128)(2,1)S(1)}, bf16[1,64,3072]{2,1,0:T(8,128)(2,1)S(1)}, u32[]{:S(2)}, u32[]{:S(2)}) collective-permute-start(bf16[1,64,3072]{2,1,0:T(8,128)(2,1)S(1)} %constant_dynamic-slice_fusion.5), channel_id=1, source_target_pairs={{0,4},{1,5},{2,6},{3,7},{4,0},{5,1},{6,2},{7,3},{8,12},{9,13},{10,... | collective-permute-start | bytes 1179656 | tf_op jit(solution)/shard_map/ppermute | solution.py:577
  681.3 17.5 %collective-permute-start.58 = (f32[32,1024]{1,0:T(8,128)S(1)}, f32[32,1024]{1,0:T(8,128)S(1)}, u32[]{:S(2)}, u32[]{:S(2)}) collective-permute-start(f32[32,1024]{1,0:T(8,128)S(1)} %slice_bitcast_fusion.23), channel_id=1, source_target_pairs={{16,0},{17,1},{18,2},{19,3},{20,4},{21,5},{22,6},{23,7},{24,8},{25... | collective-permute-start | bytes 393224 | tf_op jit(solution)/shard_map/ppermute | solution.py:948
  (60 other events, 734.0 us)
Sparse Core Ops, SparseCore 0:
  11.4 194.0 all-gather.2

commit v4 on v3

--- a/solution.py
+++ b/solution.py
@@ -16,6 +16,7 @@
 EPSILON = 1e-05
 THETA = 1000000.0
 NEGATIVE = -1e30
+SCALE = HEAD ** (-0.5)
 BF16 = jnp.bfloat16
 F32 = jnp.float32
 VMEM_LIMIT = 56 * 1024 * 1024
@@ -114,14 +115,15 @@
             blocks += [own_ref[s * rows : (s + 1) * rows, :], peer_ref[s * rows : (s + 1) * rows, :]]
         pack = jnp.concatenate(blocks, axis=0)
         keys, values = (pack[:, :HEAD], pack[:, HEAD:])
-        count = pack.shape[0]
-        row = lax.broadcasted_iota(jnp.int32, (rows, count), 0)
-        col = lax.broadcasted_iota(jnp.int32, (rows, count), 1) - stretch * 2 * rows
+        early = stretch * 2 * rows
+        row = lax.broadcasted_iota(jnp.int32, (rows, 2 * rows), 0)
+        col = lax.broadcasted_iota(jnp.int32, (rows, 2 * rows), 1)
         allowed = (col <= row) | ((col >= rows) & second)
         for j in range(2):
             query = q_ref[stretch * rows : (stretch + 1) * rows, j * HEAD : (j + 1) * HEAD]
-            scores = matmul_t(query, keys) * HEAD ** (-0.5)
-            scores = jnp.where(allowed, scores, NEGATIVE)
+            scores = matmul_t(query * SCALE, keys)
+            last = jnp.where(allowed, scores[:, early:], NEGATIVE)
+            scores = jnp.concatenate([scores[:, :early], last], axis=1) if early else last
             exponent = jnp.exp(scores - jnp.max(scores, axis=1, keepdims=True))
             total = jnp.sum(exponent, axis=1, keepdims=True)
             probs = (exponent * (1.0 / total)).astype(BF16)
@@ -156,25 +158,26 @@
             blocks += [own_ref[s * rows : (s + 1) * rows, :], peer_ref[s * rows : (s + 1) * rows, :]]
         pack = jnp.concatenate(blocks, axis=0)
         keys, values = (pack[:, :HEAD], pack[:, HEAD:])
-        count = pack.shape[0]
-        col = lax.broadcasted_iota(jnp.int32, (count, rows), 0) - stretch * 2 * rows
-        row = lax.broadcasted_iota(jnp.int32, (count, rows), 1)
+        early = stretch * 2 * rows
+        col = lax.broadcasted_iota(jnp.int32, (2 * rows, rows), 0)
+        row = lax.broadcasted_iota(jnp.int32, (2 * rows, rows), 1)
         allowed = (col <= row) | ((col >= rows) & second)
         span = slice(stretch * rows, (stretch + 1) * rows)
         dkeys, dvalues, dquery = (0.0, 0.0, [])
         for j in range(2):
-            query = q_ref[span, j * HEAD : (j + 1) * HEAD]
+            query = q_ref[span, j * HEAD : (j + 1) * HEAD] * SCALE
             grad = grad_ref[span, j * HEAD : (j + 1) * HEAD]
-            scores = matmul_t(keys, query) * HEAD ** (-0.5)
-            scores = jnp.where(allowed, scores, NEGATIVE)
+            scores = matmul_t(keys, query)
+            last = jnp.where(allowed, scores[early:], NEGATIVE)
+            scores = jnp.concatenate([scores[:early], last], axis=0) if early else last
             exponent = jnp.exp(scores - jnp.max(scores, axis=0, keepdims=True))
             probs = exponent * (1.0 / jnp.sum(exponent, axis=0, keepdims=True))
             dprobs = matmul_t(values, grad)
             dscores = probs * (dprobs - jnp.sum(probs * dprobs, axis=0, keepdims=True))
             dscores = dscores.astype(BF16)
             dvalues += jnp.dot(probs.astype(BF16), grad, preferred_element_type=F32)
-            dkeys += jnp.dot(dscores, query, preferred_element_type=F32) * HEAD ** (-0.5)
-            dquery.append(outer_sum(dscores, keys) * HEAD ** (-0.5))
+            dkeys += jnp.dot(dscores, query, preferred_element_type=F32)
+            dquery.append(outer_sum(dscores, keys) * SCALE)
         dq_ref[span, :] = jnp.concatenate(dquery, axis=1)
         both = jnp.concatenate([dkeys, dvalues], axis=1)
         for s in range(stretch + 1):
@@ -572,15 +575,8 @@
     def to_peer(value):
         return lax.ppermute(value, "seq", swap)
 
-    def exchange(value, offset, section=None):
-        if section is None:
-            return lax.ppermute(value, "fsdp", [(i, i ^ offset) for i in range(fsdp)])
-        pairs = [
-            ((section * 2 + side) * fsdp + i, (section * 2 + side) * fsdp + (i ^ offset))
-            for side in range(2)
-            for i in range(fsdp)
-        ]
-        return lax.ppermute(value, ("section", "seq", "fsdp"), pairs)
+    def exchange(value, offset):
+        return lax.ppermute(value, "fsdp", [(i, i ^ offset) for i in range(fsdp)])
 
     def gather(shards):
         results = []
@@ -633,20 +629,6 @@
 
     def core_add(leaving, staying):
         return blocks(staying.astype(F32) + leaving.astype(F32))
-
-    def only(section, value, move):
-        pairs = []
-        for side in range(2):
-            for i in range(fsdp):
-                source = (section * 2 + side) * fsdp + i
-                if move == "seq":
-                    target = (section * 2 + 1 - side) * fsdp + i
-                elif move == "core":
-                    target = (section * 2 + side) * fsdp + (i ^ 1)
-                else:
-                    target = (section * 2 + side) * fsdp + (i + 2 * move) % fsdp
-                pairs.append((source, target))
-        return lax.ppermute(value, ("section", "seq", "fsdp"), pairs)
 
     def sides(both):
         return [
@@ -787,17 +769,21 @@
         wide = lambda: zeros(total, hidden)
         lefts = (kept[0], kept[5], kept[7], active)
         moved = (zeros(total, 2 * width), flat(), flat(), wide(), wide())
-        return (zeros(total, width, kind=F32), lefts, moved, zeros(8, width, kind=F32), flat())
+        back = cotangent[0].reshape(total, width)
+        return (zeros(total, width, kind=F32), lefts, moved, zeros(8, width, kind=F32), back)
 
     conv_resid, lefts, moved, conv_small, grad_link = lax.cond(first, attention_idle, conv_both)
     normed, heads, normed_two, active_both = together(lefts, grad_link)
-    grad_link = lax.ppermute(grad_link, "section", [(1, 0)])
+    grad_ff = lax.ppermute(grad_link, "section", swap)
     conv_dproj, dgate_c, conv_dmix, conv_dgate, conv_dup = moved
     left_down, left_two, left_heads, left_normed = [
         turned(value) for value in (active_both, normed_two, heads, normed)
     ]
-    grad_ff = jnp.where(first, grad_link, cotangent[0].reshape(total, width))
-    down = sides(core_sum(left_down, grad_ff))
+    middle = width // 2
+    down = [
+        sides(core_sum(left_down, grad_ff[:, cut]))
+        for cut in (slice(0, middle), slice(middle, None))
+    ]
     groups = [[i for i in range(fsdp) if i % 2 == side] for side in range(2)]
 
     def cross(half):
@@ -820,8 +806,8 @@
                 for which in (1 - side, side)
             ]
 
-        def send(self, section=None):
-            return exchange(self.leaving, 2 << self.bit, section)
+        def send(self):
+            return exchange(self.leaving, 2 << self.bit)
 
         def add(self, came):
             last = self.staying.shape[0] == 1
@@ -844,54 +830,58 @@
 
     def conv_ff():
         products = ff_outer(left_two, conv_dgate, conv_dup)
-        return (zeros(total, width, kind=F32), halves_of(*products[:2]), *products[2:])
+        output = ff_down(conv_resid, active_both, wide_weights, hidden)
+        return (output, halves_of(*products[:2]), *products[2:])
 
     step, down = fence(first, down)
-    down_came = cross(down)
+    down_came = [cross(half) for half in down]
     result = lax.cond(step, attention_ff, conv_ff)
     down_came, (grad_two, gate, up_leaving, up_staying) = fence(down_came, result)
+
+    def sum_down():
+        return jnp.concatenate(
+            [crossed(half[1], came) for half, came in zip(down, down_came)], axis=2
+        )
 
     def attention_core():
         unused, raw, query, own, peer, unused, resid, unused = kept
         scale_two = rms_scale(resid)
         gain_two = jnp.sum(grad_two * resid * scale_two, axis=0)
-        grad_resid = grad_link.astype(F32) + norm_back(grad_two, resid, scale_two, gains[1])
+        grad_resid = grad_ff.astype(F32) + norm_back(grad_two, resid, scale_two, gains[1])
         dmix = grad_resid.astype(BF16)
         dheads = matmul_t(dmix, weights[1]).astype(BF16)
-        up, dheads = fence(halves_of(up_leaving, up_staying), dheads)
-        grads = []
-        for groups in (range(KV_HEADS // 2), range(KV_HEADS // 2, KV_HEADS)):
-            if grads:
-                grads, dheads = fence(grads, dheads)
-            grads.append(attend_back(part_ref, query, own, peer, dheads, rows, stretches, groups))
-        recv = [to_peer(half[2]) for half in grads]
-        dquery, down_kv = [
-            jnp.concatenate([half[i] for half in grads], axis=1) for i in range(2)
-        ]
-        recv = jnp.concatenate(recv, axis=1)
-        blank = zeros(chips, 2 * conv_cut, width)
-        return (up, gain_two, grad_resid, dmix, dquery, down_kv, recv, [blank, blank])
+        up, dheads, own_down = fence(halves_of(up_leaving, up_staying), dheads, sum_down())
+        came = along_all(own_down)
+        half = KV_HEADS // 2
+        back = functools.partial(attend_back, part_ref, query, own, peer)
+        low, dheads = fence(back(dheads, rows, stretches, range(half)), dheads)
+        low_recv = to_peer(low[2])
+        low_recv, high = fence(low_recv, back(dheads, rows, stretches, range(half, KV_HEADS)))
+        high_recv = to_peer(high[2])
+        dquery, down_kv = [jnp.concatenate([low[i], high[i]], axis=1) for i in range(2)]
+        recv = jnp.concatenate([low_recv, high_recv], axis=1)
+        came, recv = fence(came, recv)
+        shard = scattered(came)
+        blank = zeros(2 * conv_cut, width, kind=F32)
+        return (shard, up, gain_two, grad_resid, dmix, dquery, down_kv, recv, blank)
 
     def conv_core():
         mixed = normed.reshape(total, 2, 2 * fsdp, conv_cut)
         mixed = jnp.transpose(mixed, (0, 2, 1, 3)).reshape(total, width)
         lone = sides(core_sum(turned(mixed), dgate_c))
-        output = ff_down(conv_resid, active_both, wide_weights, hidden)
-        flat = lambda: zeros(total, width, kind=F32)
+        came = along_all(sum_down())
+        blanks = [zeros(total, width, kind=kind) for kind in (F32, F32, BF16)]
         up = halves_of(up_leaving, up_staying)
-        return (
-            up, zeros(width, kind=F32), output, conv_dmix, flat(), flat(), zeros(total, width), lone,
-        )
-
-    down = crossed(down[1], down_came)
-    step, down, gate = fence(first, down, gate)
-    down_came, gate_came = (along_all(down), cross(gate))
+        peer, up, blanks, output = fence(to_peer(lone[0]), up, blanks, grad_two)
+        came, lone = fence(came, crossed(lone[1], peer))
+        shard, lone = (scattered(came), scattered(along_all(lone)))
+        return (shard, up, zeros(width, kind=F32), output, conv_dmix, *blanks, lone)
+
+    step, gate = fence(first, gate)
+    gate_came = cross(gate)
     result = lax.cond(step, attention_core, conv_core)
-    down_came, gate_came, result = fence(down_came, gate_came, result)
-    up, gain_two, grad_resid, dmix, dquery, down_kv, recv, lone = result
-
-    def joined(*halves):
-        return [jnp.concatenate(parts, axis=2) for parts in zip(*halves)]
+    gate_came, result = fence(gate_came, result)
+    shard_down, up, gain_two, grad_resid, dmix, dquery, down_kv, recv, lone = result
 
     def attention_project():
         dproj, grad_one, head_rows = project_back(
@@ -908,51 +898,51 @@
         small = jnp.concatenate(
             [gain_one[None], gain_two[None], jnp.zeros((5, width), F32), head_row], axis=0
         )
-        return (joined(inward, outward), grad_source, small + to_core(small))
+        return ([inward, outward], grad_source, small + to_core(small))
 
     def conv_project():
         outward = sides(core_sum(left_heads, dmix))
         inward = sides(core_sum(left_normed, conv_dproj))
         output = grad_resid
         small = conv_small + to_core(conv_small)
-        return (joined(inward, outward), output, small)
+        return ([inward, outward], output, small)
 
     gate = crossed(gate[1], gate_came)
-    step, gate, up, lone = fence(first, gate, up, lone)
-    gate_came, up_came, lone_came = (along_all(gate), cross(up), only(1, lone[0], "seq"))
+    step, gate, up = fence(first, gate, up)
+    gate_came, up_came = (along_all(gate), cross(up))
     result = lax.cond(step, attention_project, conv_project)
-    gate_came, up_came, lone_came, result = fence(gate_came, up_came, lone_came, result)
+    gate_came, up_came, result = fence(gate_came, up_came, result)
     mix, ends, small = result
 
     up = Halving(crossed(up[1], up_came))
-    lone = Halving(crossed(lone[1], lone_came))
-    mix_came = cross(mix)
-    up_came, lone_came = (up.send(), lone.send(1))
-    small = small + lax.ppermute(small, "section", swap)
-    up_came, lone_came, small = fence(up_came, lone_came, small)
-    up, lone, small_came = (up.add(up_came), lone.add(lone_came), to_peer(small))
+    mix_came = [cross(half) for half in mix]
+    up_came = up.send()
+    up_came, small_came = fence(up_came, to_peer(small))
+    up, small = (up.add(up_came), small + small_came)
+    small_came = exchange(small, 2)
     bits = chips.bit_length() - 1
     for bit in range(1, bits):
-        up_came, lone_came = (up.send(), lone.send(1))
         if bit == 1:
             mix_came, small_came = fence(mix_came, small_came)
-            mix = Halving(crossed(mix[1], mix_came))
+            mix = [Halving(crossed(half[1], came)) for half, came in zip(mix, mix_came)]
             small = small + small_came
-            mix_came, small_came = (mix.send(), exchange(small, 2))
-        up_came, lone_came, mix_came, small_came = fence(
-            up_came, lone_came, mix_came, small_came
-        )
-        up, lone, mix = (up.add(up_came), lone.add(lone_came), mix.add(mix_came))
+            mix_came, small_came = ([half.send() for half in mix], exchange(small, 4))
+        up_came = up.send()
+        up_came, mix_came, small_came = fence(up_came, mix_came, small_came)
+        up = up.add(up_came)
+        mix = [half.add(came) for half, came in zip(mix, mix_came)]
         small = small + small_came
-        mix_came, small_came = (mix.send(), exchange(small, 2 << bit))
-    mail = lax.ppermute(lone.held[0, :conv_cut], "section", [(1, 0)])
-    mail, mix_came, small_came = fence(mail, mix_came, small_came)
-    small = small + small_came
-    shard_mix = mix.add(mix_came).held[0]
-    c_shard = jnp.where(first, mail, lone.held[0, conv_cut:])
+        mix_came = [half.send() for half in mix]
+        if bit < bits - 1:
+            small_came = exchange(small, 4 << bit)
+    mail = lax.ppermute(jnp.concatenate([small, lone[:conv_cut]], axis=0), "section", swap)
+    mix_came, mail = fence(mix_came, mail)
+    small = small + mail[: small.shape[0]]
+    c_shard = jnp.where(first, mail[small.shape[0] :], lone[conv_cut:])
+    shard_in, shard_out = [half.add(came).held[0] for half, came in zip(mix, mix_came)]
     shards_out = (
-        shard_mix[:, : 2 * width], shard_mix[:, 2 * width :],
-        scattered(gate_came), up.held[0], scattered(down_came),
+        shard_in, shard_out,
+        scattered(gate_came), up.held[0], shard_down,
     )
     return (
         ends.reshape(1, 1, stretches, rows, width),

time: 717 us -> 710 us (level)
  waiting for transfers between devices: 325 us -> 232 us
  starting transfers between devices: 47.7 us -> 130 us
    ppermute x6 -> x2, waiting for transfers between devices: 90.7 us -> 12.7 us  [the longest x1 12.7 us: local(): grad_ff = lax.ppermute(grad_link, 'section', swap)]
    ppermute x6 -> x2, starting transfers between devices: 5.58 us -> 82.4 us  [the longest x1 73.4 us: local(): grad_ff = lax.ppermute(grad_link, 'section', swap)]
    ppermute x12 -> x14, waiting for transfers between devices: 91.1 us -> 81.3 us  [to_peer(): return lax.ppermute(value, 'seq', swap)]
    ppermute x8 -> x9, waiting for transfers between devices: 19.1 us -> 12.3 us  [to_core(): return lax.ppermute(value, 'fsdp', cores)]
    ppermute x12 -> x14, starting transfers between devices: 12.7 us -> 15.3 us  [to_peer(): return lax.ppermute(value, 'seq', swap)]
    dot_general x7 -> x9, matrix products: 25.9 us -> 28.3 us  [matmul(): return jnp.dot(left, right, preferred_element_type=F32)]
    ppermute x10 -> x12, waiting for transfers between devices: 95.5 us -> 93.2 us  [exchange(): return lax.ppermute(value, 'fsdp', [(i, i ^ offset) for i in range(fsdp)])]
    ppermute x10 -> x12, starting transfers between devices: 12.8 us -> 14.9 us  [exchange(): return lax.ppermute(value, 'fsdp', [(i, i ^ offset) for i in range(fsdp)])]
  transfers between devices with their start and end apart: 41 -> 42, of which waited for: 23 -> 24; matrix products, arithmetic and copies ran while one was open for 15% -> 18% of each run, Pallas kernels for 18% -> 18%
where the time goes in v4:
time: 710 us; the launch traced here: 703 us
  waiting for transfers between devices  232 us (33%)
  Pallas kernels  154 us (22%)
  starting transfers between devices  130 us (18%)
  other arithmetic  66.1 us (9%)
  local copies, waits for them, and re-layouts  64.3 us (9%)
  matrix products  32.5 us (5%)
  between operations  14.8 us (2%)
  loops' own time  10.5 us (1%)
    ppermute x12, waiting for transfers between devices, exchange(): return lax.ppermute(value, 'fsdp', [(i, i ^ offset) for i in range(fsdp)])  93.2 us
    ppermute x14, waiting for transfers between devices, to_peer(): return lax.ppermute(value, 'seq', swap)  81.3 us
    ppermute x1, starting transfers between devices, local(): grad_ff = lax.ppermute(grad_link, 'section', swap)  73.4 us
    pallas_call x1, Pallas kernels, ff_backward_outer(): pl.pallas_call(backward_outer_kernel, grid=(hidden // chunk,), in_specs=[...  36.9 us
    pallas_call x2, Pallas kernels, attend_back(): pl.pallas_call(functools.partial(attend_back_kernel, rows, stretches), gr...  36.5 us
    dot_general x9, matrix products, matmul(): return jnp.dot(left, right, preferred_element_type=F32)  28.3 us
    pallas_call x1, Pallas kernels, ff_forward(): pl.pallas_call(forward_kernel, grid=(hidden // chunk,), in_specs=[pl.Bloc...  26 us
    pallas_call x1, Pallas kernels, attend(): pl.pallas_call(functools.partial(attend_kernel, rows, stretches), grid=(K...  20 us
  transfers between devices with their start and end apart: 42, of which 24 were waited for; matrix products, arithmetic and copies ran while one was open for 18% of the time, Pallas kernels for 18%

profile of v4, /device:TPU:0, one launch (start us, length us, event | category | flops | bytes accessed | tf_op | source)
XLA Modules:
  0.0 703.4 jit_solution(16972726699486707364)
XLA Ops:
  18.9 176.5 %conditional.6 = (bf16[1024,2048]{1,0:T(8,128)(2,1)}, bf16[1024,1024]{1,0:T(8,128)(2,1)}, bf16[1024,1024]{1,0:T(8,128)(2,1)}, bf16[512,1024]{1,0:T(8,128)(2,1)},...) conditional(s32[]{:T(128)} %convert_element_type.376, ...), branch_computations={%region_0.1_spmd, %region_1.4_spmd} | conditional | flops 1083707520 | bytes 93130544 | solution.py:705
  22.7 13.9 %collective-permute-done.17 = bf16[1,64,2048]{2,1,0:T(8,128)(2,1)S(1)} collective-permute-done((bf16[1,64,2048]{2,1,0:T(8,128)(2,1)S(1)}, bf16[1,64,2048]{2,1,0:T(8,128)(2,1)S(1)}, u32[]{:S(2)}, u32[]{:S(2)}) %collective-permute-start.17) | collective-permute-done | bytes 262176 | tf_op jit(solution)/shard_map/cond/branch_1_fun/ppermute | solution.py:579
  41.6 15.4 %collective-permute-done.19 = bf16[2,64,2048]{2,1,0:T(8,128)(2,1)} collective-permute-done((bf16[2,64,2048]{2,1,0:T(8,128)(2,1)}, bf16[2,64,2048]{2,1,0:T(8,128)(2,1)}, u32[]{:S(2)}, u32[]{:S(2)}) %collective-permute-start.19) | collective-permute-done | bytes 524320 | tf_op jit(solution)/shard_map/cond/branch_1_fun/ppermute | solution.py:579
  59.6 16.3 %collective-permute-done.20 = bf16[2,64,2048]{2,1,0:T(8,128)(2,1)S(1)} collective-permute-done((bf16[2,64,2048]{2,1,0:T(8,128)(2,1)}, bf16[2,64,2048]{2,1,0:T(8,128)(2,1)S(1)}, u32[]{:S(2)}, u32[]{:S(2)}) %collective-permute-start.20) | collective-permute-done | bytes 524320 | tf_op jit(solution)/shard_map/cond/branch_1_fun/ppermute | solution.py:576
  88.2 10.0 %collective-permute-done.22 = bf16[1,64,1024]{2,1,0:T(8,128)(2,1)S(1)} collective-permute-done((bf16[1,64,1024]{2,1,0:T(8,128)(2,1)S(1)}, bf16[1,64,1024]{2,1,0:T(8,128)(2,1)S(1)}, u32[]{:S(2)}, u32[]{:S(2)}) %collective-permute-start.22) | collective-permute-done | bytes 131104 | tf_op jit(solution)/shard_map/cond/branch_1_fun/ppermute | solution.py:579
  99.2 15.2 %branch_1_fun.7 = (bf16[512,2048]{1,0:T(8,128)(2,1)}, bf16[512,1024]{1,0:T(8,128)(2,1)S(1)}, bf16[512,1024]{1,0:T(8,128)(2,1)S(1)}) custom-call(bf16[512,1024]{1,0:T(8,128)(2,1)} %fusion.14.x_ref, bf16[1024,2048]{1,0:T(8,128)(2,1)} %bitcast.38.w_ref, f32[512,128]{1,0:T(8,128)S(1)} %get-tuple-element.743.cos_ref, f32[512,128]{1,0:T(8,128)S(1)} %get-tuple-element.744.sin_ref, ...), custom_call_target="tpu_custom_call" | custom-call | flops 1048576 | bytes 1048576 | tf_op jit(solution)/shard_map/cond/branch_1_fun/pallas_call | solution.py:85
  118.5 37.5 %collective-permute-done.23 = bf16[1,64,1024]{2,1,0:T(8,128)(2,1)S(1)} collective-permute-done((bf16[1,64,1024]{2,1,0:T(8,128)(2,1)S(1)}, bf16[1,64,1024]{2,1,0:T(8,128)(2,1)S(1)}, u32[]{:S(2)}, u32[]{:S(2)}) %collective-permute-start.23) | collective-permute-done | bytes 131104 | tf_op jit(solution)/shard_map/cond/branch_1_fun/ppermute | solution.py:576
  163.9 20.0 %branch_1_fun.8 = bf16[512,1024]{1,0:T(8,128)(2,1)S(1)} custom-call(s32[1]{0:T(128)} %get-tuple-element.250.part_ref, bf16[512,1024]{1,0:T(8,128)(2,1)S(1)} %get-tuple-element.737.q_ref, bf16[512,1024]{1,0:T(8,128)(2,1)S(1)} %get-tuple-element.738.own_ref, bf16[512,1024]{1,0:T(8,128)(2,1)S(1)} %collective-permute-done.27.peer_ref), custom_call_target="tpu_custom_call" | custom-call | flops 1048576 | bytes 1048576 | tf_op jit(solution)/shard_map/cond/branch_1_fun/pallas_call | solution.py:138
  195.4 10.1 %all-gather.3.cloned.1.call-done = bf16[110592,128]{1,0:T(8,128)(2,1)} async-done(((bf16[6912,128]{1,0:T(8,128)(2,1)}), bf16[110592,128]{1,0:T(8,128)(2,1)}) %all-gather.3.cloned.1.call-update) | async-done | bytes 28311568 | tf_op jit(solution)/shard_map/all_gather | solution.py:658
  205.5 27.9 %conditional.7 = (bf16[512,1024]{1,0:T(8,128)(2,1)S(1)}, bf16[512,4608]{1,0:T(8,128)(2,1)}, bf16[512,4608]{1,0:T(8,128)(2,1)}, bf16[512,4608]{1,0:T(8,128)(2,1)}) conditional(s32[]{:T(128)} %convert_element_type.376, () %tuple.84, (bf16[512,1024]{1,0:T(8,128)(2,1)}, f32[512,1024]{1,0:T(8,128)}, bf16[16,6912,128]{2,1,0:T(8,128)(2,1)}) %tuple.169), branch_computations={%region_4.5_spmd, %region_5.6_spmd} | conditional | flops 1572864 | bytes 15204392 | solution.py:714
  205.7 26.0 %branch_1_fun.9 = (f32[512,1024]{1,0:T(8,128)}, bf16[512,4608]{1,0:T(8,128)(2,1)}, bf16[512,4608]{1,0:T(8,128)(2,1)}, bf16[512,4608]{1,0:T(8,128)(2,1)}) custom-call(bf16[512,1024]{1,0:T(8,128)(2,1)} %get-tuple-element.251.x_ref, f32[512,1024]{1,0:T(8,128)} %get-tuple-element.252.base_ref, bf16[16,6912,128]{2,1,0:T(8,128)(2,1)} %get-tuple-element.253.g_ref.u_ref.d_ref, ...), custom_call_target="tpu_custom_call" | custom-call | flops 1048576 | bytes 1048576 | tf_op jit(solution)/shard_map/cond/branch_1_fun/pallas_call | solution.py:448
  234.8 15.9 %collective-permute-done.43 = bf16[512,1024]{1,0:T(8,128)(2,1)S(1)} collective-permute-done((bf16[512,1024]{1,0:T(8,128)(2,1)S(1)}, bf16[512,1024]{1,0:T(8,128)(2,1)S(1)}, u32[]{:S(2)}, u32[]{:S(2)}) %collective-permute-start.43) | collective-permute-done | bytes 1048608 | tf_op jit(solution)/shard_map/ppermute | solution.py:715
  250.7 18.4 %conditional.8 = (f32[512,1024]{1,0:T(8,128)S(1)}, bf16[512,1024]{1,0:T(8,128)(2,1)}, bf16[512,1024]{1,0:T(8,128)(2,1)}, bf16[512,1024]{1,0:T(8,128)(2,1)}, bf16...) conditional(s32[]{:T(128)} %convert_element_type.376, ...), branch_computations={%region_6.16_spmd, %region_16.17_spmd} | conditional | flops 8648138752 | bytes 231228064 | solution.py:775
  269.1 73.4 %collective-permute-start.44 = (bf16[512,1024]{1,0:T(8,128)(2,1)}, bf16[512,1024]{1,0:T(8,128)(2,1)S(1)}, u32[]{:S(2)}, u32[]{:S(2)}) collective-permute-start(bf16[512,1024]{1,0:T(8,128)(2,1)} %get-tuple-element.512), channel_id=1, source_target_pairs={{0,16},{16,0},{1,17},{17,1},{2,18},{18,2},{3,19},{19,3},{4,20},{20... | collective-permute-start | bytes 3145736 | tf_op jit(solution)/shard_map/ppermute | solution.py:777
  353.4 12.7 %collective-permute-done.44 = bf16[512,1024]{1,0:T(8,128)(2,1)S(1)} collective-permute-done((bf16[512,1024]{1,0:T(8,128)(2,1)}, bf16[512,1024]{1,0:T(8,128)(2,1)S(1)}, u32[]{:S(2)}, u32[]{:S(2)}) %collective-permute-start.44) | collective-permute-done | bytes 1048608 | tf_op jit(solution)/shard_map/ppermute | solution.py:777
  389.5 52.1 %conditional.9 = (f32[512,1024]{1,0:T(8,128)}, bf16[4,64,4608]{2,1,0:T(8,128)(2,1)}, bf16[4,64,4608]{2,1,0:T(8,128)(2,1)S(1)}, bf16[512,4608]{1,0:T(8,128)(2,1)}, bf16[512,4608]{1,0:T(8,128)(2,1)}) conditional(s32[]{:T(128)} %convert_element_type.383, (f32[512,1024]{1,0:T(8,128)S(1)}, bf16[512,4608]{1,0:T(8,128)(2,1)}, ...), branch_computations={%region_17.18_spmd, %region_18.19_spmd} | conditional | flops 11534343 | bytes 58720468 | solution.py:838
  389.6 36.9 %branch_1_fun.10 = (f32[512,1024]{1,0:T(8,128)}, bf16[512,4608]{1,0:T(8,128)(2,1)}, bf16[512,4608]{1,0:T(8,128)(2,1)}, bf16[512,4608]{1,0:T(8,128)(2,1)}, bf16[512,4608]{1,0:T(8,128)(2,1)}) custom-call(bf16[512,1024]{1,0:T(8,128)(2,1)} %get-tuple-element.287.grad_ref, bf16[1024,512]{1,0:T(8,128)(2,1)} %get-tuple-element.288.left_ref, ...), custom_call_target="tpu_custom_call" | custom-call | flops 1048576 | bytes 1048576 | tf_op jit(solution)/shard_map/cond/branch_1_fun/pallas_call | solution.py:505
  443.0 89.1 %conditional.10 = (f32[288,1024]{1,0:T(8,128)}, bf16[4,64,4608]{2,1,0:T(8,128)(2,1)}, bf16[4,64,4608]{2,1,0:T(8,128)(2,1)}, f32[1024]{0:T(1024)S(1)}, f32[512,10...) conditional(s32[]{:T(128)} %convert_element_type.385, ...), branch_computations={%region_19.22_spmd, %region_22.27_spmd} | conditional | flops 1109360128 | bytes 130193952 | solution.py:882
  474.0 18.2 %branch_1_fun.11 = (f32[512,512]{1,0:T(8,128)}, f32[512,512]{1,0:T(8,128)}, bf16[512,512]{1,0:T(8,128)(2,1)}) custom-call(s32[1]{0:T(128)} %get-tuple-element.332.part_ref, bf16[512,1024]{1,0:T(8,128)(2,1)S(1)} %get-tuple-element.333.q_ref, bf16[512,1024]{1,0:T(8,128)(2,1)S(1)} %copy-done.13, bf16[512,1024]{1,0:T(8,128)(2,1)S(1)} %copy-done.15, ...), custom_call_target="tpu_custom_call" | custom-call | flops 1048576 | bytes 1048576 | tf_op jit(solution)/shard_map/cond/branch_1_fun/pallas_call | solution.py:197
  492.8 18.2 %branch_1_fun.12 = (f32[512,512]{1,0:T(8,128)}, f32[512,512]{1,0:T(8,128)}, bf16[512,512]{1,0:T(8,128)(2,1)}) custom-call(s32[1]{0:T(128)} %get-tuple-element.332.part_ref, bf16[512,1024]{1,0:T(8,128)(2,1)S(1)} %get-tuple-element.333.q_ref, bf16[512,1024]{1,0:T(8,128)(2,1)S(1)} %copy-done.13, bf16[512,1024]{1,0:T(8,128)(2,1)S(1)} %copy-done.15, ...), custom_call_target="tpu_custom_call" | custom-call | flops 1048576 | bytes 1048576 | tf_op jit(solution)/shard_map/cond/branch_1_fun/pallas_call | solution.py:197
  549.3 40.6 %conditional.11 = (bf16[4,64,2048]{2,1,0:T(8,128)(2,1)}, bf16[4,64,2048]{2,1,0:T(8,128)(2,1)S(1)}, bf16[4,64,1024]{2,1,0:T(8,128)(2,1)}, bf16[4,64,1024]{2,1,0:T...) conditional(s32[]{:T(128)} %convert_element_type.388, (bf16[512,512]{1,0:T(8,128)(2,1)}, ...), branch_computations={%region_27.28_spmd, %region_28.32_spmd} | conditional | flops 3238092288 | bytes 76848448 | solution.py:913
  550.3 19.0 %branch_1_fun.13 = (bf16[512,2048]{1,0:T(8,128)(2,1)}, f32[512,1024]{1,0:T(8,128)}, f32[8,128]{1,0:T(8,128)}) custom-call(bf16[512,2048]{1,0:T(8,128)(2,1)} %get-tuple-element.364.raw_ref, f32[512,1024]{1,0:T(8,128)S(1)} %get-tuple-element.365.dq_ref, f32[512,1024]{1,0:T(8,128)} %get-tuple-element.366.own_ref, ...), custom_call_target="tpu_custom_call" | custom-call | flops 1048576 | bytes 1048576 | tf_op jit(solution)/shard_map/cond/branch_1_fun/pallas_call | solution.py:252
  603.9 21.5 %collective-permute-done.51 = bf16[2,64,4608]{2,1,0:T(8,128)(2,1)} collective-permute-done((bf16[2,64,4608]{2,1,0:T(8,128)(2,1)S(1)}, bf16[2,64,4608]{2,1,0:T(8,128)(2,1)}, u32[]{:S(2)}, u32[]{:S(2)}) %collective-permute-start.51) | collective-permute-done | bytes 1179680 | tf_op jit(solution)/shard_map/ppermute | solution.py:579
  645.2 13.8 %collective-permute-done.59 = f32[8,1024]{1,0:T(8,128)S(1)} collective-permute-done((f32[8,1024]{1,0:T(8,128)S(1)}, f32[8,1024]{1,0:T(8,128)S(1)}, u32[]{:S(2)}, u32[]{:S(2)}) %collective-permute-start.59) | collective-permute-done | bytes 32800 | tf_op jit(solution)/shard_map/ppermute | solution.py:579
  (324 shorter events, 284.2 us)
Async XLA Ops:
  7.2 198.3 %all-gather.3.cloned.1.call-start = ((), (), s32[]{:S(2)}) async-start(), calls=%async_computation.4 | async-start | bytes 30081024 | tf_op jit(solution)/shard_map/all_gather | solution.py:658
  37.4 19.5 %collective-permute-start.19 = (bf16[2,64,2048]{2,1,0:T(8,128)(2,1)}, bf16[2,64,2048]{2,1,0:T(8,128)(2,1)}, u32[]{:S(2)}, u32[]{:S(2)}) collective-permute-start(bf16[2,64,2048]{2,1,0:T(8,128)(2,1)} %pad_maximum_fusion.4), channel_id=1, source_target_pairs={{0,2},{1,3},{2,0},{3,1},{4,6},{5,7},{6,4},{7,5},{8,10},{9,11},{10,... | collective-permute-start | bytes 1572872 | tf_op jit(solution)/shard_map/cond/branch_1_fun/ppermute | solution.py:579
  39.0 19.6 %collective-permute-start.18 = (bf16[1,64,2048]{2,1,0:T(8,128)(2,1)}, bf16[1,64,2048]{2,1,0:T(8,128)(2,1)S(1)}, u32[]{:S(2)}, u32[]{:S(2)}) collective-permute-start(bf16[1,64,2048]{2,1,0:T(8,128)(2,1)} %copy-done.55), channel_id=1, source_target_pairs={{0,8},{8,0},{1,9},{9,1},{2,10},{10,2},{3,11},{11,3},{4,12},{12,4},... | collective-permute-start | bytes 786440 | tf_op jit(solution)/shard_map/cond/branch_1_fun/ppermute | solution.py:576
  56.9 19.0 %collective-permute-start.20 = (bf16[2,64,2048]{2,1,0:T(8,128)(2,1)}, bf16[2,64,2048]{2,1,0:T(8,128)(2,1)S(1)}, u32[]{:S(2)}, u32[]{:S(2)}) collective-permute-start(bf16[2,64,2048]{2,1,0:T(8,128)(2,1)} %collective-permute-done.19), channel_id=1, source_target_pairs={{0,8},{8,0},{1,9},{9,1},{2,10},{10,2},{3,11},{11,3},{4,12},{12,4},... | collective-permute-start | bytes 1572872 | tf_op jit(solution)/shard_map/cond/branch_1_fun/ppermute | solution.py:576
  114.4 49.4 %collective-permute-start.27 = (bf16[512,1024]{1,0:T(8,128)(2,1)S(1)}, bf16[512,1024]{1,0:T(8,128)(2,1)S(1)}, u32[]{:S(2)}, u32[]{:S(2)}) collective-permute-start(bf16[512,1024]{1,0:T(8,128)(2,1)S(1)} %get-tuple-element.738.own_ref), channel_id=1, source_target_pairs={{0,8},{8,0},{1,9},{9,1},{2,10},{10,2},{3,11},{11,3},{4,12},{12,4},... | collective-permute-start | bytes 3145736 | tf_op jit(solution)/shard_map/cond/branch_1_fun/ppermute | solution.py:576
  116.4 39.6 %collective-permute-start.23 = (bf16[1,64,1024]{2,1,0:T(8,128)(2,1)S(1)}, bf16[1,64,1024]{2,1,0:T(8,128)(2,1)S(1)}, u32[]{:S(2)}, u32[]{:S(2)}) collective-permute-start(bf16[1,64,1024]{2,1,0:T(8,128)(2,1)S(1)} %collective-permute-done.22), channel_id=1, source_target_pairs={{0,8},{8,0},{1,9},{9,1},{2,10},{10,2},{3,11},{11,3},{4,12},{12,4},... | collective-permute-start | bytes 393224 | tf_op jit(solution)/shard_map/cond/branch_1_fun/ppermute | solution.py:576
  116.6 47.2 %collective-permute-start.25 = (bf16[2,64,1024]{2,1,0:T(8,128)(2,1)S(1)}, bf16[2,64,1024]{2,1,0:T(8,128)(2,1)S(1)}, u32[]{:S(2)}, u32[]{:S(2)}) collective-permute-start(bf16[2,64,1024]{2,1,0:T(8,128)(2,1)S(1)} %collective-permute-done.24), channel_id=1, source_target_pairs={{0,8},{8,0},{1,9},{9,1},{2,10},{10,2},{3,11},{11,3},{4,12},{12,4},... | collective-permute-start | bytes 786440 | tf_op jit(solution)/shard_map/cond/branch_1_fun/ppermute | solution.py:576
  163.8 20.1 %collective-permute-start.26 = (bf16[4,2,64,1024]{3,2,1,0:T(8,128)(2,1)S(1)}, bf16[4,2,64,1024]{3,2,1,0:T(8,128)(2,1)S(1)}, u32[]{:S(2)}, u32[]{:S(2)}) collective-permute-start(bf16[4,2,64,1024]{3,2,1,0:T(8,128)(2,1)S(1)} %fusion.20), channel_id=1, source_target_pairs={{0,1},{1,0},{2,3},{3,2},{4,5},{5,4},{6,7},{7,6},{8,9},{9,8},{10,11... | collective-permute-start | bytes 3145736 | tf_op jit(solution)/shard_map/cond/branch_1_fun/ppermute | solution.py:573
  269.1 96.9 %collective-permute-start.44 = (bf16[512,1024]{1,0:T(8,128)(2,1)}, bf16[512,1024]{1,0:T(8,128)(2,1)S(1)}, u32[]{:S(2)}, u32[]{:S(2)}) collective-permute-start(bf16[512,1024]{1,0:T(8,128)(2,1)} %get-tuple-element.512), channel_id=1, source_target_pairs={{0,16},{16,0},{1,17},{17,1},{2,18},{18,2},{3,19},{19,3},{4,20},{20... | collective-permute-start | bytes 3145736 | tf_op jit(solution)/shard_map/ppermute | solution.py:777
  384.8 56.8 %collective-permute-start.47 = (bf16[4,288,512]{2,1,0:T(8,128)(2,1)}, bf16[4,288,512]{2,1,0:T(8,128)(2,1)}, u32[]{:S(2)}, u32[]{:S(2)}) collective-permute-start(bf16[4,288,512]{2,1,0:T(8,128)(2,1)} %get-tuple-element.514), channel_id=1, source_target_pairs={{0,8},{8,0},{1,9},{9,1},{2,10},{10,2},{3,11},{11,3},{4,12},{12,4},... | collective-permute-start | bytes 3538952 | tf_op jit(solution)/shard_map/ppermute | solution.py:576
  385.0 56.6 %collective-permute-start.48 = (bf16[4,288,512]{2,1,0:T(8,128)(2,1)}, bf16[4,288,512]{2,1,0:T(8,128)(2,1)}, u32[]{:S(2)}, u32[]{:S(2)}) collective-permute-start(bf16[4,288,512]{2,1,0:T(8,128)(2,1)} %get-tuple-element.515), channel_id=1, source_target_pairs={{0,8},{8,0},{1,9},{9,1},{2,10},{10,2},{3,11},{11,3},{4,12},{12,4},... | collective-permute-start | bytes 3538952 | tf_op jit(solution)/shard_map/ppermute | solution.py:576
  441.6 90.5 %collective-permute-start.49 = (bf16[4,64,4608]{2,1,0:T(8,128)(2,1)}, bf16[4,64,4608]{2,1,0:T(8,128)(2,1)}, u32[]{:S(2)}, u32[]{:S(2)}) collective-permute-start(bf16[4,64,4608]{2,1,0:T(8,128)(2,1)} %get-tuple-element.531), channel_id=1, source_target_pairs={{0,8},{8,0},{1,9},{9,1},{2,10},{10,2},{3,11},{11,3},{4,12},{12,4},... | collective-permute-start | bytes 7077896 | tf_op jit(solution)/shard_map/ppermute | solution.py:576
  469.1 59.5 %all-to-all-start.2 = ((bf16[4,288,1024]{2,1,0:T(8,128)(2,1)}), bf16[4,288,1024]{2,1,0:T(8,128)(2,1)}, u32[]{:S(2)}, u32[]{:S(2)}) async-start(bf16[4,288,1024]{2,1,0:T(8,128)(2,1)} %pad_maximum_fusion.10), calls=%async_computation.2 | async-start | bytes 4718592 | tf_op jit(solution)/shard_map/cond/branch_1_fun/all_to_all | solution.py:793
  492.2 18.8 %collective-permute-start.34 = (bf16[512,512]{1,0:T(8,128)(2,1)}, bf16[512,512]{1,0:T(8,128)(2,1)S(1)}, u32[]{:S(2)}, u32[]{:S(2)}) collective-permute-start(bf16[512,512]{1,0:T(8,128)(2,1)} %get-tuple-element.340), channel_id=1, source_target_pairs={{0,8},{8,0},{1,9},{9,1},{2,10},{10,2},{3,11},{11,3},{4,12},{12,4},... | collective-permute-start | bytes 1572872 | tf_op jit(solution)/shard_map/cond/branch_1_fun/ppermute | solution.py:576
  536.9 58.4 %all-to-all-start.3 = ((bf16[4,64,4608]{2,1,0:T(8,128)(2,1)}), bf16[4,64,4608]{2,1,0:T(8,128)(2,1)}, u32[]{:S(2)}, u32[]{:S(2)}) async-start(bf16[4,64,4608]{2,1,0:T(8,128)(2,1)} %add_convert_fusion.13), calls=%async_computation.3 | async-start | bytes 4718592 | tf_op jit(solution)/shard_map/all_to_all | solution.py:793
  541.4 53.1 %collective-permute-start.50 = (bf16[4,64,4608]{2,1,0:T(8,128)(2,1)}, bf16[4,64,4608]{2,1,0:T(8,128)(2,1)}, u32[]{:S(2)}, u32[]{:S(2)}) collective-permute-start(bf16[4,64,4608]{2,1,0:T(8,128)(2,1)} %get-tuple-element.560), channel_id=1, source_target_pairs={{0,8},{8,0},{1,9},{9,1},{2,10},{10,2},{3,11},{11,3},{4,12},{12,4},... | collective-permute-start | bytes 7077896 | tf_op jit(solution)/shard_map/ppermute | solution.py:576
  598.3 27.1 %collective-permute-start.51 = (bf16[2,64,4608]{2,1,0:T(8,128)(2,1)S(1)}, bf16[2,64,4608]{2,1,0:T(8,128)(2,1)}, u32[]{:S(2)}, u32[]{:S(2)}) collective-permute-start(bf16[2,64,4608]{2,1,0:T(8,128)(2,1)S(1)} %dynamic-slice_bitcast_fusion.19), channel_id=1, source_target_pairs={{0,2},{1,3},{2,0},{3,1},{4,6},{5,7},{6,4},{7,5},{8,10},{9,11},{10,... | collective-permute-start | bytes 3538952 | tf_op jit(solution)/shard_map/ppermute | solution.py:579
  600.1 34.9 %collective-permute-start.53 = (bf16[4,64,2048]{2,1,0:T(8,128)(2,1)}, bf16[4,64,2048]{2,1,0:T(8,128)(2,1)S(1)}, u32[]{:S(2)}, u32[]{:S(2)}) collective-permute-start(bf16[4,64,2048]{2,1,0:T(8,128)(2,1)} %get-tuple-element.585), channel_id=1, source_target_pairs={{0,8},{8,0},{1,9},{9,1},{2,10},{10,2},{3,11},{11,3},{4,12},{12,4},... | collective-permute-start | bytes 3145736 | tf_op jit(solution)/shard_map/ppermute | solution.py:576
  601.3 33.7 %collective-permute-start.54 = (bf16[4,64,1024]{2,1,0:T(8,128)(2,1)}, bf16[4,64,1024]{2,1,0:T(8,128)(2,1)S(1)}, u32[]{:S(2)}, u32[]{:S(2)}) collective-permute-start(bf16[4,64,1024]{2,1,0:T(8,128)(2,1)} %get-tuple-element.586), channel_id=1, source_target_pairs={{0,8},{8,0},{1,9},{9,1},{2,10},{10,2},{3,11},{11,3},{4,12},{12,4},... | collective-permute-start | bytes 1572872 | tf_op jit(solution)/shard_map/ppermute | solution.py:576
  629.1 37.0 %collective-permute-start.56 = (bf16[1,64,4608]{2,1,0:T(8,128)(2,1)}, bf16[1,64,4608]{2,1,0:T(8,128)(2,1)S(1)}, u32[]{:S(2)}, u32[]{:S(2)}) collective-permute-start(bf16[1,64,4608]{2,1,0:T(8,128)(2,1)} %constant_dynamic-slice_fusion.7), channel_id=1, source_target_pairs={{0,4},{1,5},{2,6},{3,7},{4,0},{5,1},{6,2},{7,3},{8,12},{9,13},{10,... | collective-permute-start | bytes 1769480 | tf_op jit(solution)/shard_map/ppermute | solution.py:579
  636.3 29.8 %collective-permute-start.57 = (bf16[2,64,2048]{2,1,0:T(8,128)(2,1)}, bf16[2,64,2048]{2,1,0:T(8,128)(2,1)S(1)}, u32[]{:S(2)}, u32[]{:S(2)}) collective-permute-start(bf16[2,64,2048]{2,1,0:T(8,128)(2,1)} %dynamic-slice_bitcast_fusion.25), channel_id=1, source_target_pairs={{0,2},{1,3},{2,0},{3,1},{4,6},{5,7},{6,4},{7,5},{8,10},{9,11},{10,... | collective-permute-start | bytes 1572872 | tf_op jit(solution)/shard_map/ppermute | solution.py:579
  639.3 26.8 %collective-permute-start.58 = (bf16[2,64,1024]{2,1,0:T(8,128)(2,1)S(1)}, bf16[2,64,1024]{2,1,0:T(8,128)(2,1)}, u32[]{:S(2)}, u32[]{:S(2)}) collective-permute-start(bf16[2,64,1024]{2,1,0:T(8,128)(2,1)S(1)} %dynamic-slice_bitcast_fusion.26), channel_id=1, source_target_pairs={{0,2},{1,3},{2,0},{3,1},{4,6},{5,7},{6,4},{7,5},{8,10},{9,11},{10,... | collective-permute-start | bytes 786440 | tf_op jit(solution)/shard_map/ppermute | solution.py:579
  639.7 19.3 %collective-permute-start.59 = (f32[8,1024]{1,0:T(8,128)S(1)}, f32[8,1024]{1,0:T(8,128)S(1)}, u32[]{:S(2)}, u32[]{:S(2)}) collective-permute-start(f32[8,1024]{1,0:T(8,128)S(1)} %add.509), channel_id=1, source_target_pairs={{0,4},{1,5},{2,6},{3,7},{4,0},{5,1},{6,2},{7,3},{8,12},{9,13},{10,... | collective-permute-start | bytes 98312 | tf_op jit(solution)/shard_map/ppermute | solution.py:579
  666.1 20.9 %collective-permute-start.62 = (f32[40,1024]{1,0:T(8,128)S(1)}, f32[40,1024]{1,0:T(8,128)S(1)}, u32[]{:S(2)}, u32[]{:S(2)}) collective-permute-start(f32[40,1024]{1,0:T(8,128)S(1)} %pad_maximum_fusion.17), channel_id=1, source_target_pairs={{0,16},{16,0},{1,17},{17,1},{2,18},{18,2},{3,19},{19,3},{4,20},{20... | collective-permute-start | bytes 491528 | tf_op jit(solution)/shard_map/ppermute | solution.py:938
  (70 other events, 915.9 us)
Sparse Core Ops, SparseCore 0:
  11.4 194.0 all-gather.2

commit v5 on v4

--- a/solution.py
+++ b/solution.py
@@ -629,6 +629,14 @@
 
     def core_add(leaving, staying):
         return blocks(staying.astype(F32) + leaving.astype(F32))
+
+    def lone_swap(value, offset):
+        pairs = []
+        for side in range(2):
+            for i in range(fsdp):
+                other = (1 - side, i) if offset == "seq" else (side, i ^ offset)
+                pairs.append(((2 + side) * fsdp + i, (2 + other[0]) * fsdp + other[1]))
+        return lax.ppermute(value, ("section", "seq", "fsdp"), pairs)
 
     def sides(both):
         return [
@@ -806,8 +814,8 @@
                 for which in (1 - side, side)
             ]
 
-        def send(self):
-            return exchange(self.leaving, 2 << self.bit)
+        def send(self, swap_with=exchange):
+            return swap_with(self.leaving, 2 << self.bit)
 
         def add(self, came):
             last = self.staying.shape[0] == 1
@@ -826,17 +834,20 @@
 
     def attention_ff():
         grad_two, *products = ff_backward_outer(grad_ff, left_two, one, two, wide_weights, hidden)
-        return (grad_two, halves_of(*products[:2]), *products[2:])
+        blank = zeros(chips, 2 * conv_cut, width)
+        return (grad_two, halves_of(*products[:2]), *products[2:], [blank, blank])
 
     def conv_ff():
         products = ff_outer(left_two, conv_dgate, conv_dup)
-        output = ff_down(conv_resid, active_both, wide_weights, hidden)
-        return (output, halves_of(*products[:2]), *products[2:])
+        mixed = normed.reshape(total, 2, 2 * fsdp, conv_cut)
+        mixed = jnp.transpose(mixed, (0, 2, 1, 3)).reshape(total, width)
+        lone = sides(core_sum(turned(mixed), dgate_c))
+        return (zeros(total, width, kind=F32), halves_of(*products[:2]), *products[2:], lone)
 
     step, down = fence(first, down)
     down_came = [cross(half) for half in down]
     result = lax.cond(step, attention_ff, conv_ff)
-    down_came, (grad_two, gate, up_leaving, up_staying) = fence(down_came, result)
+    down_came, (grad_two, gate, up_leaving, up_staying, lone) = fence(down_came, result)
 
     def sum_down():
         return jnp.concatenate(
@@ -850,38 +861,35 @@
         grad_resid = grad_ff.astype(F32) + norm_back(grad_two, resid, scale_two, gains[1])
         dmix = grad_resid.astype(BF16)
         dheads = matmul_t(dmix, weights[1]).astype(BF16)
-        up, dheads, own_down = fence(halves_of(up_leaving, up_staying), dheads, sum_down())
+        up_came = to_core(up_leaving)
+        dheads, own_down = fence(dheads, sum_down())
         came = along_all(own_down)
         half = KV_HEADS // 2
         back = functools.partial(attend_back, part_ref, query, own, peer)
         low, dheads = fence(back(dheads, rows, stretches, range(half)), dheads)
         low_recv = to_peer(low[2])
-        low_recv, high = fence(low_recv, back(dheads, rows, stretches, range(half, KV_HEADS)))
+        high = back(dheads, rows, stretches, range(half, KV_HEADS))
+        low_recv, high, up_came = fence(low_recv, high, up_came)
         high_recv = to_peer(high[2])
+        up = sides(core_add(up_came, up_staying))
         dquery, down_kv = [jnp.concatenate([low[i], high[i]], axis=1) for i in range(2)]
         recv = jnp.concatenate([low_recv, high_recv], axis=1)
         came, recv = fence(came, recv)
-        shard = scattered(came)
-        blank = zeros(2 * conv_cut, width, kind=F32)
-        return (shard, up, gain_two, grad_resid, dmix, dquery, down_kv, recv, blank)
+        return (came, up, gain_two, grad_resid, dmix, dquery, down_kv, recv)
 
     def conv_core():
-        mixed = normed.reshape(total, 2, 2 * fsdp, conv_cut)
-        mixed = jnp.transpose(mixed, (0, 2, 1, 3)).reshape(total, width)
-        lone = sides(core_sum(turned(mixed), dgate_c))
+        output = ff_down(conv_resid, active_both, wide_weights, hidden)
+        blanks = [zeros(total, width, kind=kind) for kind in (BF16, F32, F32, BF16)]
+        up = halves_of(up_leaving, up_staying)
         came = along_all(sum_down())
-        blanks = [zeros(total, width, kind=kind) for kind in (F32, F32, BF16)]
-        up = halves_of(up_leaving, up_staying)
-        peer, up, blanks, output = fence(to_peer(lone[0]), up, blanks, grad_two)
-        came, lone = fence(came, crossed(lone[1], peer))
-        shard, lone = (scattered(came), scattered(along_all(lone)))
-        return (shard, up, zeros(width, kind=F32), output, conv_dmix, *blanks, lone)
-
-    step, gate = fence(first, gate)
-    gate_came = cross(gate)
+        came, up, output, blanks = fence(came, up, output, blanks)
+        return (came, up, zeros(width, kind=F32), output, *blanks)
+
+    step, gate, lone = fence(first, gate, lone)
+    lone_came, gate_came = (lone_swap(lone[0], "seq"), cross(gate))
     result = lax.cond(step, attention_core, conv_core)
-    gate_came, result = fence(gate_came, result)
-    shard_down, up, gain_two, grad_resid, dmix, dquery, down_kv, recv, lone = result
+    gate_came, lone_came, result = fence(gate_came, lone_came, result)
+    down_came, up, gain_two, grad_resid, dmix, dquery, down_kv, recv = result
 
     def attention_project():
         dproj, grad_one, head_rows = project_back(
@@ -901,7 +909,7 @@
         return ([inward, outward], grad_source, small + to_core(small))
 
     def conv_project():
-        outward = sides(core_sum(left_heads, dmix))
+        outward = sides(core_sum(left_heads, conv_dmix))
         inward = sides(core_sum(left_normed, conv_dproj))
         output = grad_resid
         small = conv_small + to_core(conv_small)
@@ -916,9 +924,10 @@
 
     up = Halving(crossed(up[1], up_came))
     mix_came = [cross(half) for half in mix]
-    up_came = up.send()
-    up_came, small_came = fence(up_came, to_peer(small))
-    up, small = (up.add(up_came), small + small_came)
+    lone = Halving(crossed(lone[1], lone_came))
+    up_came, lone_came = (up.send(), lone.send(lone_swap))
+    up_came, lone_came, small_came = fence(up_came, lone_came, to_peer(small))
+    up, lone, small = (up.add(up_came), lone.add(lone_came), small + small_came)
     small_came = exchange(small, 2)
     bits = chips.bit_length() - 1
     for bit in range(1, bits):
@@ -927,14 +936,17 @@
             mix = [Halving(crossed(half[1], came)) for half, came in zip(mix, mix_came)]
             small = small + small_came
             mix_came, small_came = ([half.send() for half in mix], exchange(small, 4))
-        up_came = up.send()
-        up_came, mix_came, small_came = fence(up_came, mix_came, small_came)
-        up = up.add(up_came)
+        up_came, lone_came = (up.send(), lone.send(lone_swap))
+        up_came, lone_came, mix_came, small_came = fence(
+            up_came, lone_came, mix_came, small_came
+        )
+        up, lone = (up.add(up_came), lone.add(lone_came))
         mix = [half.add(came) for half, came in zip(mix, mix_came)]
         small = small + small_came
         mix_came = [half.send() for half in mix]
         if bit < bits - 1:
             small_came = exchange(small, 4 << bit)
+    lone = lone.held[0]
     mail = lax.ppermute(jnp.concatenate([small, lone[:conv_cut]], axis=0), "section", swap)
     mix_came, mail = fence(mix_came, mail)
     small = small + mail[: small.shape[0]]
@@ -942,7 +954,7 @@
     shard_in, shard_out = [half.add(came).held[0] for half, came in zip(mix, mix_came)]
     shards_out = (
         shard_in, shard_out,
-        scattered(gate_came), up.held[0], shard_down,
+        scattered(gate_came), up.held[0], scattered(down_came),
     )
     return (
         ends.reshape(1, 1, stretches, rows, width),

time: 710 us -> 703 us (level)
  waiting for transfers between devices: 232 us -> 224 us
    ppermute x1, starting transfers between devices: 9.05 us -> 0.07 us  [local(): lax.ppermute(jnp.concatenate([small, lone[:conv_cut]], axis=0), 'section'...]
  transfers between devices with their start and end apart: 42 -> 45, of which waited for: 24 -> 24; matrix products, arithmetic and copies ran while one was open for 18% -> 19% of each run, Pallas kernels for 18% -> 18%
where the time goes in v5:
time: 703 us; the launch traced here: 697 us
  waiting for transfers between devices  224 us (32%)
  Pallas kernels  153 us (22%)
  starting transfers between devices  128 us (18%)
  other arithmetic  67.9 us (10%)
  local copies, waits for them, and re-layouts  66.5 us (9%)
  matrix products  33.6 us (5%)
  between operations  14.9 us (2%)
  loops' own time  7.92 us (1%)
    ppermute x12, waiting for transfers between devices, exchange(): return lax.ppermute(value, 'fsdp', [(i, i ^ offset) for i in range(fsdp)])  89.2 us
    ppermute x14, waiting for transfers between devices, to_peer(): return lax.ppermute(value, 'seq', swap)  80.5 us
    ppermute x1, starting transfers between devices, local(): grad_ff = lax.ppermute(grad_link, 'section', swap)  75.6 us
    pallas_call x1, Pallas kernels, ff_backward_outer(): pl.pallas_call(backward_outer_kernel, grid=(hidden // chunk,), in_specs=[...  36.8 us
    pallas_call x2, Pallas kernels, attend_back(): pl.pallas_call(functools.partial(attend_back_kernel, rows, stretches), gr...  36.6 us
    dot_general x9, matrix products, matmul(): return jnp.dot(left, right, preferred_element_type=F32)  29.4 us
    pallas_call x1, Pallas kernels, ff_forward(): pl.pallas_call(forward_kernel, grid=(hidden // chunk,), in_specs=[pl.Bloc...  25.9 us
    pallas_call x1, Pallas kernels, attend(): pl.pallas_call(functools.partial(attend_kernel, rows, stretches), grid=(K...  20 us
  transfers between devices with their start and end apart: 45, of which 24 were waited for; matrix products, arithmetic and copies ran while one was open for 19% of the time, Pallas kernels for 18%

profile of v5, /device:TPU:0, one launch (start us, length us, event | category | flops | bytes accessed | tf_op | source)
XLA Modules:
  0.0 696.9 jit_solution(13046643797860074904)
XLA Ops:
  18.9 176.5 %conditional.6 = (bf16[1024,2048]{1,0:T(8,128)(2,1)}, bf16[1024,1024]{1,0:T(8,128)(2,1)}, bf16[1024,1024]{1,0:T(8,128)(2,1)}, bf16[512,1024]{1,0:T(8,128)(2,1)},...) conditional(s32[]{:T(128)} %convert_element_type.387, ...), branch_computations={%region_0.1_spmd, %region_1.4_spmd} | conditional | flops 1083707520 | bytes 93130544 | solution.py:713
  22.7 13.9 %collective-permute-done.17 = bf16[1,64,2048]{2,1,0:T(8,128)(2,1)S(1)} collective-permute-done((bf16[1,64,2048]{2,1,0:T(8,128)(2,1)S(1)}, bf16[1,64,2048]{2,1,0:T(8,128)(2,1)S(1)}, u32[]{:S(2)}, u32[]{:S(2)}) %collective-permute-start.17) | collective-permute-done | bytes 262176 | tf_op jit(solution)/shard_map/cond/branch_1_fun/ppermute | solution.py:579
  41.6 15.3 %collective-permute-done.19 = bf16[2,64,2048]{2,1,0:T(8,128)(2,1)} collective-permute-done((bf16[2,64,2048]{2,1,0:T(8,128)(2,1)}, bf16[2,64,2048]{2,1,0:T(8,128)(2,1)}, u32[]{:S(2)}, u32[]{:S(2)}) %collective-permute-start.19) | collective-permute-done | bytes 524320 | tf_op jit(solution)/shard_map/cond/branch_1_fun/ppermute | solution.py:579
  59.6 16.3 %collective-permute-done.20 = bf16[2,64,2048]{2,1,0:T(8,128)(2,1)S(1)} collective-permute-done((bf16[2,64,2048]{2,1,0:T(8,128)(2,1)}, bf16[2,64,2048]{2,1,0:T(8,128)(2,1)S(1)}, u32[]{:S(2)}, u32[]{:S(2)}) %collective-permute-start.20) | collective-permute-done | bytes 524320 | tf_op jit(solution)/shard_map/cond/branch_1_fun/ppermute | solution.py:576
  99.2 15.2 %branch_1_fun.7 = (bf16[512,2048]{1,0:T(8,128)(2,1)}, bf16[512,1024]{1,0:T(8,128)(2,1)S(1)}, bf16[512,1024]{1,0:T(8,128)(2,1)S(1)}) custom-call(bf16[512,1024]{1,0:T(8,128)(2,1)} %fusion.14.x_ref, bf16[1024,2048]{1,0:T(8,128)(2,1)} %bitcast.38.w_ref, f32[512,128]{1,0:T(8,128)S(1)} %get-tuple-element.741.cos_ref, f32[512,128]{1,0:T(8,128)S(1)} %get-tuple-element.742.sin_ref, ...), custom_call_target="tpu_custom_call" | custom-call | flops 1048576 | bytes 1048576 | tf_op jit(solution)/shard_map/cond/branch_1_fun/pallas_call | solution.py:85
  118.6 37.5 %collective-permute-done.23 = bf16[1,64,1024]{2,1,0:T(8,128)(2,1)S(1)} collective-permute-done((bf16[1,64,1024]{2,1,0:T(8,128)(2,1)S(1)}, bf16[1,64,1024]{2,1,0:T(8,128)(2,1)S(1)}, u32[]{:S(2)}, u32[]{:S(2)}) %collective-permute-start.23) | collective-permute-done | bytes 131104 | tf_op jit(solution)/shard_map/cond/branch_1_fun/ppermute | solution.py:576
  163.9 20.0 %branch_1_fun.8 = bf16[512,1024]{1,0:T(8,128)(2,1)S(1)} custom-call(s32[1]{0:T(128)} %get-tuple-element.246.part_ref, bf16[512,1024]{1,0:T(8,128)(2,1)S(1)} %get-tuple-element.735.q_ref, bf16[512,1024]{1,0:T(8,128)(2,1)S(1)} %get-tuple-element.736.own_ref, bf16[512,1024]{1,0:T(8,128)(2,1)S(1)} %collective-permute-done.27.peer_ref), custom_call_target="tpu_custom_call" | custom-call | flops 1048576 | bytes 1048576 | tf_op jit(solution)/shard_map/cond/branch_1_fun/pallas_call | solution.py:138
  195.4 10.1 %all-gather.3.cloned.1.call-done = bf16[110592,128]{1,0:T(8,128)(2,1)} async-done(((bf16[6912,128]{1,0:T(8,128)(2,1)}), bf16[110592,128]{1,0:T(8,128)(2,1)}) %all-gather.3.cloned.1.call-update) | async-done | bytes 28311568 | tf_op jit(solution)/shard_map/all_gather | solution.py:666
  205.5 27.9 %conditional.7 = (bf16[512,1024]{1,0:T(8,128)(2,1)S(1)}, bf16[512,4608]{1,0:T(8,128)(2,1)}, bf16[512,4608]{1,0:T(8,128)(2,1)}, bf16[512,4608]{1,0:T(8,128)(2,1)}) conditional(s32[]{:T(128)} %convert_element_type.387, () %tuple.83, (bf16[512,1024]{1,0:T(8,128)(2,1)}, f32[512,1024]{1,0:T(8,128)}, bf16[16,6912,128]{2,1,0:T(8,128)(2,1)}) %tuple.169), branch_computations={%region_4.5_spmd, %region_5.6_spmd} | conditional | flops 1572864 | bytes 15204392 | solution.py:722
  205.7 25.9 %branch_1_fun.9 = (f32[512,1024]{1,0:T(8,128)}, bf16[512,4608]{1,0:T(8,128)(2,1)}, bf16[512,4608]{1,0:T(8,128)(2,1)}, bf16[512,4608]{1,0:T(8,128)(2,1)}) custom-call(bf16[512,1024]{1,0:T(8,128)(2,1)} %get-tuple-element.247.x_ref, f32[512,1024]{1,0:T(8,128)} %get-tuple-element.248.base_ref, bf16[16,6912,128]{2,1,0:T(8,128)(2,1)} %get-tuple-element.249.g_ref.u_ref.d_ref, ...), custom_call_target="tpu_custom_call" | custom-call | flops 1048576 | bytes 1048576 | tf_op jit(solution)/shard_map/cond/branch_1_fun/pallas_call | solution.py:448
  234.8 15.9 %collective-permute-done.42 = bf16[512,1024]{1,0:T(8,128)(2,1)S(1)} collective-permute-done((bf16[512,1024]{1,0:T(8,128)(2,1)S(1)}, bf16[512,1024]{1,0:T(8,128)(2,1)S(1)}, u32[]{:S(2)}, u32[]{:S(2)}) %collective-permute-start.42) | collective-permute-done | bytes 1048608 | tf_op jit(solution)/shard_map/ppermute | solution.py:723
  250.7 16.1 %conditional.8 = (f32[512,1024]{1,0:T(8,128)S(1)}, bf16[512,1024]{1,0:T(8,128)(2,1)}, bf16[512,1024]{1,0:T(8,128)(2,1)}, bf16[512,1024]{1,0:T(8,128)(2,1)}, bf16...) conditional(s32[]{:T(128)} %convert_element_type.387, ...), branch_computations={%region_6.16_spmd, %region_16.17_spmd} | conditional | flops 8648138752 | bytes 231228064 | solution.py:783
  266.7 75.6 %collective-permute-start.43 = (bf16[512,1024]{1,0:T(8,128)(2,1)}, bf16[512,1024]{1,0:T(8,128)(2,1)S(1)}, u32[]{:S(2)}, u32[]{:S(2)}) collective-permute-start(bf16[512,1024]{1,0:T(8,128)(2,1)} %get-tuple-element.511), channel_id=1, source_target_pairs={{0,16},{16,0},{1,17},{17,1},{2,18},{18,2},{3,19},{19,3},{4,20},{20... | collective-permute-start | bytes 3145736 | tf_op jit(solution)/shard_map/ppermute | solution.py:785
  353.3 12.6 %collective-permute-done.43 = bf16[512,1024]{1,0:T(8,128)(2,1)S(1)} collective-permute-done((bf16[512,1024]{1,0:T(8,128)(2,1)}, bf16[512,1024]{1,0:T(8,128)(2,1)S(1)}, u32[]{:S(2)}, u32[]{:S(2)}) %collective-permute-start.43) | collective-permute-done | bytes 1048608 | tf_op jit(solution)/shard_map/ppermute | solution.py:785
  389.2 54.9 %conditional.9 = (f32[512,1024]{1,0:T(8,128)}, bf16[4,64,4608]{2,1,0:T(8,128)(2,1)}, bf16[4,64,4608]{2,1,0:T(8,128)(2,1)}, bf16[512,4608]{1,0:T(8,128)(2,1)}, bf...) conditional(s32[]{:T(128)} %convert_element_type.394, ...), branch_computations={%region_17.18_spmd, %region_18.19_spmd} | conditional | flops 1086324736 | bytes 68682072 | solution.py:849
  389.6 36.8 %branch_1_fun.10 = (f32[512,1024]{1,0:T(8,128)}, bf16[512,4608]{1,0:T(8,128)(2,1)}, bf16[512,4608]{1,0:T(8,128)(2,1)}, bf16[512,4608]{1,0:T(8,128)(2,1)}, bf16[512,4608]{1,0:T(8,128)(2,1)}) custom-call(bf16[512,1024]{1,0:T(8,128)(2,1)} %get-tuple-element.283.grad_ref, bf16[1024,512]{1,0:T(8,128)(2,1)} %get-tuple-element.284.left_ref, ...), custom_call_target="tpu_custom_call" | custom-call | flops 1048576 | bytes 1048576 | tf_op jit(solution)/shard_map/cond/branch_1_fun/pallas_call | solution.py:505
  446.0 77.8 %conditional.10 = (bf16[4,288,1024]{2,1,0:T(8,128)(2,1)}, bf16[4,64,4608]{2,1,0:T(8,128)(2,1)}, bf16[4,64,4608]{2,1,0:T(8,128)(2,1)}, f32[1024]{0:T(1024)S(1)}, ...) conditional(s32[]{:T(128)} %convert_element_type.396, ...), branch_computations={%region_19.20_spmd, %region_20.24_spmd} | conditional | flops 1107295744 | bytes 122198512 | solution.py:890
  469.0 18.3 %branch_1_fun.11 = (f32[512,512]{1,0:T(8,128)}, f32[512,512]{1,0:T(8,128)}, bf16[512,512]{1,0:T(8,128)(2,1)}) custom-call(s32[1]{0:T(128)} %get-tuple-element.322.part_ref, bf16[512,1024]{1,0:T(8,128)(2,1)S(1)} %get-tuple-element.323.q_ref, bf16[512,1024]{1,0:T(8,128)(2,1)S(1)} %copy-done.13, bf16[512,1024]{1,0:T(8,128)(2,1)S(1)} %copy-done.15, ...), custom_call_target="tpu_custom_call" | custom-call | flops 1048576 | bytes 1048576 | tf_op jit(solution)/shard_map/cond/branch_1_fun/pallas_call | solution.py:197
  489.0 18.3 %branch_1_fun.12 = (f32[512,512]{1,0:T(8,128)}, f32[512,512]{1,0:T(8,128)}, bf16[512,512]{1,0:T(8,128)(2,1)}) custom-call(s32[1]{0:T(128)} %get-tuple-element.322.part_ref, bf16[512,1024]{1,0:T(8,128)(2,1)S(1)} %get-tuple-element.323.q_ref, bf16[512,1024]{1,0:T(8,128)(2,1)S(1)} %copy-done.13, bf16[512,1024]{1,0:T(8,128)(2,1)S(1)} %copy-done.15, ...), custom_call_target="tpu_custom_call" | custom-call | flops 1048576 | bytes 1048576 | tf_op jit(solution)/shard_map/cond/branch_1_fun/pallas_call | solution.py:197
  542.1 41.2 %conditional.11 = (bf16[4,64,2048]{2,1,0:T(8,128)(2,1)}, bf16[4,64,2048]{2,1,0:T(8,128)(2,1)S(1)}, bf16[4,64,1024]{2,1,0:T(8,128)(2,1)}, bf16[4,64,1024]{2,1,0:T...) conditional(s32[]{:T(128)} %convert_element_type.399, (bf16[512,512]{1,0:T(8,128)(2,1)}, ...), branch_computations={%region_24.25_spmd, %region_25.29_spmd} | conditional | flops 3238092288 | bytes 72654120 | solution.py:921
  543.0 19.0 %branch_1_fun.13 = (bf16[512,2048]{1,0:T(8,128)(2,1)}, f32[512,1024]{1,0:T(8,128)}, f32[8,128]{1,0:T(8,128)}) custom-call(bf16[512,2048]{1,0:T(8,128)(2,1)} %get-tuple-element.356.raw_ref, f32[512,1024]{1,0:T(8,128)S(1)} %get-tuple-element.357.dq_ref, f32[512,1024]{1,0:T(8,128)} %get-tuple-element.358.own_ref, ...), custom_call_target="tpu_custom_call" | custom-call | flops 1048576 | bytes 1048576 | tf_op jit(solution)/shard_map/cond/branch_1_fun/pallas_call | solution.py:252
  603.4 15.1 %collective-permute-done.51 = bf16[2,64,4608]{2,1,0:T(8,128)(2,1)} collective-permute-done((bf16[2,64,4608]{2,1,0:T(8,128)(2,1)}, bf16[2,64,4608]{2,1,0:T(8,128)(2,1)}, u32[]{:S(2)}, u32[]{:S(2)}) %collective-permute-start.51) | collective-permute-done | bytes 1179680 | tf_op jit(solution)/shard_map/ppermute | solution.py:579
  623.9 11.9 %collective-permute-done.55 = bf16[4,64,1024]{2,1,0:T(8,128)(2,1)S(1)} collective-permute-done((bf16[4,64,1024]{2,1,0:T(8,128)(2,1)}, bf16[4,64,1024]{2,1,0:T(8,128)(2,1)S(1)}, u32[]{:S(2)}, u32[]{:S(2)}) %collective-permute-start.55) | collective-permute-done | bytes 524320 | tf_op jit(solution)/shard_map/ppermute | solution.py:576
  653.3 12.2 %collective-permute-done.60 = bf16[2,64,1024]{2,1,0:T(8,128)(2,1)S(1)} collective-permute-done((bf16[2,64,1024]{2,1,0:T(8,128)(2,1)S(1)}, bf16[2,64,1024]{2,1,0:T(8,128)(2,1)S(1)}, u32[]{:S(2)}, u32[]{:S(2)}) %collective-permute-start.60) | collective-permute-done | bytes 262176 | tf_op jit(solution)/shard_map/ppermute | solution.py:579
  (314 shorter events, 284.2 us)
Async XLA Ops:
  7.2 198.3 %all-gather.3.cloned.1.call-start = ((), (), s32[]{:S(2)}) async-start(), calls=%async_computation.3 | async-start | bytes 30081024 | tf_op jit(solution)/shard_map/all_gather | solution.py:666
  37.5 19.5 %collective-permute-start.19 = (bf16[2,64,2048]{2,1,0:T(8,128)(2,1)}, bf16[2,64,2048]{2,1,0:T(8,128)(2,1)}, u32[]{:S(2)}, u32[]{:S(2)}) collective-permute-start(bf16[2,64,2048]{2,1,0:T(8,128)(2,1)} %pad_maximum_fusion.4), channel_id=1, source_target_pairs={{0,2},{1,3},{2,0},{3,1},{4,6},{5,7},{6,4},{7,5},{8,10},{9,11},{10,... | collective-permute-start | bytes 1572872 | tf_op jit(solution)/shard_map/cond/branch_1_fun/ppermute | solution.py:579
  39.0 19.6 %collective-permute-start.18 = (bf16[1,64,2048]{2,1,0:T(8,128)(2,1)}, bf16[1,64,2048]{2,1,0:T(8,128)(2,1)S(1)}, u32[]{:S(2)}, u32[]{:S(2)}) collective-permute-start(bf16[1,64,2048]{2,1,0:T(8,128)(2,1)} %copy-done.44), channel_id=1, source_target_pairs={{0,8},{8,0},{1,9},{9,1},{2,10},{10,2},{3,11},{11,3},{4,12},{12,4},... | collective-permute-start | bytes 786440 | tf_op jit(solution)/shard_map/cond/branch_1_fun/ppermute | solution.py:576
  114.5 49.4 %collective-permute-start.27 = (bf16[512,1024]{1,0:T(8,128)(2,1)S(1)}, bf16[512,1024]{1,0:T(8,128)(2,1)S(1)}, u32[]{:S(2)}, u32[]{:S(2)}) collective-permute-start(bf16[512,1024]{1,0:T(8,128)(2,1)S(1)} %get-tuple-element.736.own_ref), channel_id=1, source_target_pairs={{0,8},{8,0},{1,9},{9,1},{2,10},{10,2},{3,11},{11,3},{4,12},{12,4},... | collective-permute-start | bytes 3145736 | tf_op jit(solution)/shard_map/cond/branch_1_fun/ppermute | solution.py:576
  116.4 39.6 %collective-permute-start.23 = (bf16[1,64,1024]{2,1,0:T(8,128)(2,1)S(1)}, bf16[1,64,1024]{2,1,0:T(8,128)(2,1)S(1)}, u32[]{:S(2)}, u32[]{:S(2)}) collective-permute-start(bf16[1,64,1024]{2,1,0:T(8,128)(2,1)S(1)} %collective-permute-done.22), channel_id=1, source_target_pairs={{0,8},{8,0},{1,9},{9,1},{2,10},{10,2},{3,11},{11,3},{4,12},{12,4},... | collective-permute-start | bytes 393224 | tf_op jit(solution)/shard_map/cond/branch_1_fun/ppermute | solution.py:576
  116.6 47.1 %collective-permute-start.25 = (bf16[2,64,1024]{2,1,0:T(8,128)(2,1)S(1)}, bf16[2,64,1024]{2,1,0:T(8,128)(2,1)S(1)}, u32[]{:S(2)}, u32[]{:S(2)}) collective-permute-start(bf16[2,64,1024]{2,1,0:T(8,128)(2,1)S(1)} %collective-permute-done.24), channel_id=1, source_target_pairs={{0,8},{8,0},{1,9},{9,1},{2,10},{10,2},{3,11},{11,3},{4,12},{12,4},... | collective-permute-start | bytes 786440 | tf_op jit(solution)/shard_map/cond/branch_1_fun/ppermute | solution.py:576
  163.8 20.1 %collective-permute-start.26 = (bf16[4,2,64,1024]{3,2,1,0:T(8,128)(2,1)S(1)}, bf16[4,2,64,1024]{3,2,1,0:T(8,128)(2,1)S(1)}, u32[]{:S(2)}, u32[]{:S(2)}) collective-permute-start(bf16[4,2,64,1024]{3,2,1,0:T(8,128)(2,1)S(1)} %fusion.20), channel_id=1, source_target_pairs={{0,1},{1,0},{2,3},{3,2},{4,5},{5,4},{6,7},{7,6},{8,9},{9,8},{10,11... | collective-permute-start | bytes 3145736 | tf_op jit(solution)/shard_map/cond/branch_1_fun/ppermute | solution.py:573
  266.7 99.2 %collective-permute-start.43 = (bf16[512,1024]{1,0:T(8,128)(2,1)}, bf16[512,1024]{1,0:T(8,128)(2,1)S(1)}, u32[]{:S(2)}, u32[]{:S(2)}) collective-permute-start(bf16[512,1024]{1,0:T(8,128)(2,1)} %get-tuple-element.511), channel_id=1, source_target_pairs={{0,16},{16,0},{1,17},{17,1},{2,18},{18,2},{3,19},{19,3},{4,20},{20... | collective-permute-start | bytes 3145736 | tf_op jit(solution)/shard_map/ppermute | solution.py:785
  384.5 59.6 %collective-permute-start.46 = (bf16[4,288,512]{2,1,0:T(8,128)(2,1)}, bf16[4,288,512]{2,1,0:T(8,128)(2,1)}, u32[]{:S(2)}, u32[]{:S(2)}) collective-permute-start(bf16[4,288,512]{2,1,0:T(8,128)(2,1)} %get-tuple-element.513), channel_id=1, source_target_pairs={{0,8},{8,0},{1,9},{9,1},{2,10},{10,2},{3,11},{11,3},{4,12},{12,4},... | collective-permute-start | bytes 3538952 | tf_op jit(solution)/shard_map/ppermute | solution.py:576
  384.8 59.4 %collective-permute-start.47 = (bf16[4,288,512]{2,1,0:T(8,128)(2,1)}, bf16[4,288,512]{2,1,0:T(8,128)(2,1)}, u32[]{:S(2)}, u32[]{:S(2)}) collective-permute-start(bf16[4,288,512]{2,1,0:T(8,128)(2,1)} %get-tuple-element.514), channel_id=1, source_target_pairs={{0,8},{8,0},{1,9},{9,1},{2,10},{10,2},{3,11},{11,3},{4,12},{12,4},... | collective-permute-start | bytes 3538952 | tf_op jit(solution)/shard_map/ppermute | solution.py:576
  444.2 79.6 %collective-permute-start.48 = (bf16[4,64,4608]{2,1,0:T(8,128)(2,1)}, bf16[4,64,4608]{2,1,0:T(8,128)(2,1)}, u32[]{:S(2)}, u32[]{:S(2)}) collective-permute-start(bf16[4,64,4608]{2,1,0:T(8,128)(2,1)} %get-tuple-element.535), channel_id=1, source_target_pairs={{0,8},{8,0},{1,9},{9,1},{2,10},{10,2},{3,11},{11,3},{4,12},{12,4},... | collective-permute-start | bytes 7077896 | tf_op jit(solution)/shard_map/ppermute | solution.py:576
  444.5 79.3 %collective-permute-start.49 = (bf16[4,64,1024]{2,1,0:T(8,128)(2,1)}, bf16[4,64,1024]{2,1,0:T(8,128)(2,1)}, u32[]{:S(2)}, u32[]{:S(2)}) collective-permute-start(bf16[4,64,1024]{2,1,0:T(8,128)(2,1)} %get-tuple-element.536), channel_id=1, source_target_pairs={{16,24},{17,25},{18,26},{19,27},{20,28},{21,29},{22,30},{23,31},{2... | collective-permute-start | bytes 1572872 | tf_op jit(solution)/shard_map/ppermute | solution.py:639
  446.0 63.1 %collective-permute-start.33 = (bf16[512,4608]{1,0:T(8,128)(2,1)}, bf16[512,4608]{1,0:T(8,128)(2,1)}, u32[]{:S(2)}, u32[]{:S(2)}) collective-permute-start(bf16[512,4608]{1,0:T(8,128)(2,1)} %get-tuple-element.335), channel_id=1, source_target_pairs={{0,1},{1,0},{2,3},{3,2},{4,5},{5,4},{6,7},{7,6},{8,9},{9,8},{10,11... | collective-permute-start | bytes 14155784 | tf_op jit(solution)/shard_map/cond/branch_1_fun/ppermute | solution.py:573
  464.3 59.5 %all-to-all-start.1 = ((bf16[4,288,1024]{2,1,0:T(8,128)(2,1)}), bf16[4,288,1024]{2,1,0:T(8,128)(2,1)}, u32[]{:S(2)}, u32[]{:S(2)}) async-start(bf16[4,288,1024]{2,1,0:T(8,128)(2,1)} %pad_maximum_fusion.10), calls=%async_computation.1 | async-start | bytes 4718592 | tf_op jit(solution)/shard_map/cond/branch_1_fun/all_to_all | solution.py:801
  487.3 21.8 %collective-permute-start.32 = (bf16[512,512]{1,0:T(8,128)(2,1)}, bf16[512,512]{1,0:T(8,128)(2,1)}, u32[]{:S(2)}, u32[]{:S(2)}) collective-permute-start(bf16[512,512]{1,0:T(8,128)(2,1)} %get-tuple-element.330), channel_id=1, source_target_pairs={{0,8},{8,0},{1,9},{9,1},{2,10},{10,2},{3,11},{11,3},{4,12},{12,4},... | collective-permute-start | bytes 1572872 | tf_op jit(solution)/shard_map/cond/branch_1_fun/ppermute | solution.py:576
  528.6 58.6 %all-to-all-start.2 = ((bf16[4,64,4608]{2,1,0:T(8,128)(2,1)}), bf16[4,64,4608]{2,1,0:T(8,128)(2,1)}, u32[]{:S(2)}, u32[]{:S(2)}) async-start(bf16[4,64,4608]{2,1,0:T(8,128)(2,1)} %add_convert_fusion.13), calls=%async_computation.2 | async-start | bytes 4718592 | tf_op jit(solution)/shard_map/all_to_all | solution.py:801
  533.1 53.3 %collective-permute-start.50 = (bf16[4,64,4608]{2,1,0:T(8,128)(2,1)}, bf16[4,64,4608]{2,1,0:T(8,128)(2,1)}, u32[]{:S(2)}, u32[]{:S(2)}) collective-permute-start(bf16[4,64,4608]{2,1,0:T(8,128)(2,1)} %get-tuple-element.562), channel_id=1, source_target_pairs={{0,8},{8,0},{1,9},{9,1},{2,10},{10,2},{3,11},{11,3},{4,12},{12,4},... | collective-permute-start | bytes 7077896 | tf_op jit(solution)/shard_map/ppermute | solution.py:576
  591.2 27.3 %collective-permute-start.51 = (bf16[2,64,4608]{2,1,0:T(8,128)(2,1)}, bf16[2,64,4608]{2,1,0:T(8,128)(2,1)}, u32[]{:S(2)}, u32[]{:S(2)}) collective-permute-start(bf16[2,64,4608]{2,1,0:T(8,128)(2,1)} %dynamic-slice_bitcast_fusion.20), channel_id=1, source_target_pairs={{0,2},{1,3},{2,0},{3,1},{4,6},{5,7},{6,4},{7,5},{8,10},{9,11},{10,... | collective-permute-start | bytes 3538952 | tf_op jit(solution)/shard_map/ppermute | solution.py:579
  601.3 34.5 %collective-permute-start.54 = (bf16[4,64,2048]{2,1,0:T(8,128)(2,1)}, bf16[4,64,2048]{2,1,0:T(8,128)(2,1)S(1)}, u32[]{:S(2)}, u32[]{:S(2)}) collective-permute-start(bf16[4,64,2048]{2,1,0:T(8,128)(2,1)} %get-tuple-element.590), channel_id=1, source_target_pairs={{0,8},{8,0},{1,9},{9,1},{2,10},{10,2},{3,11},{11,3},{4,12},{12,4},... | collective-permute-start | bytes 3145736 | tf_op jit(solution)/shard_map/ppermute | solution.py:576
  601.6 34.2 %collective-permute-start.55 = (bf16[4,64,1024]{2,1,0:T(8,128)(2,1)}, bf16[4,64,1024]{2,1,0:T(8,128)(2,1)S(1)}, u32[]{:S(2)}, u32[]{:S(2)}) collective-permute-start(bf16[4,64,1024]{2,1,0:T(8,128)(2,1)} %get-tuple-element.591), channel_id=1, source_target_pairs={{0,8},{8,0},{1,9},{9,1},{2,10},{10,2},{3,11},{11,3},{4,12},{12,4},... | collective-permute-start | bytes 1572872 | tf_op jit(solution)/shard_map/ppermute | solution.py:576
  621.5 44.0 %collective-permute-start.57 = (bf16[1,64,4608]{2,1,0:T(8,128)(2,1)S(1)}, bf16[1,64,4608]{2,1,0:T(8,128)(2,1)S(1)}, u32[]{:S(2)}, u32[]{:S(2)}) collective-permute-start(bf16[1,64,4608]{2,1,0:T(8,128)(2,1)S(1)} %constant_dynamic-slice_fusion.8), channel_id=1, source_target_pairs={{0,4},{1,5},{2,6},{3,7},{4,0},{5,1},{6,2},{7,3},{8,12},{9,13},{10,... | collective-permute-start | bytes 1769480 | tf_op jit(solution)/shard_map/ppermute | solution.py:579
  636.3 29.2 %collective-permute-start.59 = (bf16[2,64,2048]{2,1,0:T(8,128)(2,1)S(1)}, bf16[2,64,2048]{2,1,0:T(8,128)(2,1)S(1)}, u32[]{:S(2)}, u32[]{:S(2)}) collective-permute-start(bf16[2,64,2048]{2,1,0:T(8,128)(2,1)S(1)} %dynamic-slice_bitcast_fusion.26), channel_id=1, source_target_pairs={{0,2},{1,3},{2,0},{3,1},{4,6},{5,7},{6,4},{7,5},{8,10},{9,11},{10,... | collective-permute-start | bytes 1572872 | tf_op jit(solution)/shard_map/ppermute | solution.py:579
  639.3 26.2 %collective-permute-start.60 = (bf16[2,64,1024]{2,1,0:T(8,128)(2,1)S(1)}, bf16[2,64,1024]{2,1,0:T(8,128)(2,1)S(1)}, u32[]{:S(2)}, u32[]{:S(2)}) collective-permute-start(bf16[2,64,1024]{2,1,0:T(8,128)(2,1)S(1)} %dynamic-slice_bitcast_fusion.27), channel_id=1, source_target_pairs={{0,2},{1,3},{2,0},{3,1},{4,6},{5,7},{6,4},{7,5},{8,10},{9,11},{10,... | collective-permute-start | bytes 786440 | tf_op jit(solution)/shard_map/ppermute | solution.py:579
  666.1 19.4 %collective-permute-start.62 = (bf16[1,64,2048]{2,1,0:T(8,128)(2,1)S(1)}, bf16[1,64,2048]{2,1,0:T(8,128)(2,1)S(1)}, u32[]{:S(2)}, u32[]{:S(2)}) collective-permute-start(bf16[1,64,2048]{2,1,0:T(8,128)(2,1)S(1)} %constant_dynamic-slice_fusion.6), channel_id=1, source_target_pairs={{0,4},{1,5},{2,6},{3,7},{4,0},{5,1},{6,2},{7,3},{8,12},{9,13},{10,... | collective-permute-start | bytes 786440 | tf_op jit(solution)/shard_map/ppermute | solution.py:579
  (62 other events, 888.6 us)
Sparse Core Ops, SparseCore 0:
  11.4 194.0 all-gather.2

commit v6 on v5

--- a/solution.py
+++ b/solution.py
@@ -289,7 +289,9 @@
     return jnp.concatenate(parts, axis=1)
 
 
-def forward_kernel(x_ref, base_ref, g_ref, u_ref, d_ref, out_ref, act_ref, one_ref, two_ref):
+def forward_kernel(
+    x_ref, base_ref, g_ref, u_ref, d_ref, out_ref, act_ref, one_ref, two_ref, total_ref
+):
     chunk, width = (act_ref.shape[1], out_ref.shape[1])
     gate_part, up_part, down_part = (wide(g_ref, chunk), wide(u_ref, chunk), wide(d_ref, width))
     down = 0.0
@@ -306,11 +308,15 @@
 
     @pl.when(pl.program_id(0) == 0)
     def _():
-        out_ref[...] = base_ref[...] + down
+        total_ref[...] = base_ref[...] + down
 
     @pl.when(pl.program_id(0) > 0)
     def _():
-        out_ref[...] += down
+        total_ref[...] += down
+
+    @pl.when(pl.program_id(0) == pl.num_programs(0) - 1)
+    def _():
+        out_ref[...] = total_ref[...].astype(BF16)
 
 
 def store_outer(left_ref, dgate, dup, span, outs):
@@ -452,7 +458,8 @@
         + specs,
         out_specs=[pl.BlockSpec((tokens, width), whole)]
         + [pl.BlockSpec((tokens, chunk), column)] * 3,
-        out_shape=[jax.ShapeDtypeStruct((tokens, width), F32), saved, saved, saved],
+        out_shape=[jax.ShapeDtypeStruct((tokens, width), BF16), saved, saved, saved],
+        scratch_shapes=[pltpu.VMEM((tokens, width), F32)],
         compiler_params=params(),
         cost_estimate=light(),
     )(normed, base, *operands)
@@ -714,7 +721,7 @@
 
     def attention_hidden():
         result, *saved = ff_forward(kept[-1], kept[-2], wide_weights, hidden)
-        return (result.astype(BF16), *saved)
+        return (result, *saved)
 
     def conv_wait():
         return (zeros(total, width), *[zeros(total, hidden) for _ in range(3)])

time: 703 us -> 701 us (level)
  no operation moved by 1% of the time
where the time goes in v6:
time: 701 us; the launch traced here: 695 us
  waiting for transfers between devices  224 us (32%)
  Pallas kernels  153 us (22%)
  starting transfers between devices  128 us (18%)
  local copies, waits for them, and re-layouts  66.5 us (9%)
  other arithmetic  66.1 us (9%)
  matrix products  33.6 us (5%)
  between operations  14.9 us (2%)
  loops' own time  7.92 us (1%)
    ppermute x12, waiting for transfers between devices, exchange(): return lax.ppermute(value, 'fsdp', [(i, i ^ offset) for i in range(fsdp)])  89.2 us
    ppermute x14, waiting for transfers between devices, to_peer(): return lax.ppermute(value, 'seq', swap)  80.5 us
    ppermute x1, starting transfers between devices, local(): grad_ff = lax.ppermute(grad_link, 'section', swap)  75.6 us
    pallas_call x1, Pallas kernels, ff_backward_outer(): pl.pallas_call(backward_outer_kernel, grid=(hidden // chunk,), in_specs=[...  36.8 us
    pallas_call x2, Pallas kernels, attend_back(): pl.pallas_call(functools.partial(attend_back_kernel, rows, stretches), gr...  36.6 us
    dot_general x9, matrix products, matmul(): return jnp.dot(left, right, preferred_element_type=F32)  29.4 us
    pallas_call x1, Pallas kernels, ff_forward(): pl.pallas_call(forward_kernel, grid=(hidden // chunk,), in_specs=[pl.Bloc...  25.4 us
    pallas_call x1, Pallas kernels, attend(): pl.pallas_call(functools.partial(attend_kernel, rows, stretches), grid=(K...  20 us
  transfers between devices with their start and end apart: 45, of which 24 were waited for; matrix products, arithmetic and copies ran while one was open for 19% of the time, Pallas kernels for 18%

profile of v6, /device:TPU:0, one launch (start us, length us, event | category | flops | bytes accessed | tf_op | source)
XLA Modules:
  0.0 694.6 jit_solution(16431748770303294543)
XLA Ops:
  18.9 176.5 %conditional.6 = (bf16[1024,2048]{1,0:T(8,128)(2,1)}, bf16[1024,1024]{1,0:T(8,128)(2,1)}, bf16[1024,1024]{1,0:T(8,128)(2,1)}, bf16[512,1024]{1,0:T(8,128)(2,1)},...) conditional(s32[]{:T(128)} %convert_element_type.384, ...), branch_computations={%region_0.1_spmd, %region_1.4_spmd} | conditional | flops 1083707520 | bytes 93130544 | solution.py:720
  22.7 13.9 %collective-permute-done.17 = bf16[1,64,2048]{2,1,0:T(8,128)(2,1)S(1)} collective-permute-done((bf16[1,64,2048]{2,1,0:T(8,128)(2,1)S(1)}, bf16[1,64,2048]{2,1,0:T(8,128)(2,1)S(1)}, u32[]{:S(2)}, u32[]{:S(2)}) %collective-permute-start.17) | collective-permute-done | bytes 262176 | tf_op jit(solution)/shard_map/cond/branch_1_fun/ppermute | solution.py:586
  41.6 15.3 %collective-permute-done.19 = bf16[2,64,2048]{2,1,0:T(8,128)(2,1)} collective-permute-done((bf16[2,64,2048]{2,1,0:T(8,128)(2,1)}, bf16[2,64,2048]{2,1,0:T(8,128)(2,1)}, u32[]{:S(2)}, u32[]{:S(2)}) %collective-permute-start.19) | collective-permute-done | bytes 524320 | tf_op jit(solution)/shard_map/cond/branch_1_fun/ppermute | solution.py:586
  59.6 16.3 %collective-permute-done.20 = bf16[2,64,2048]{2,1,0:T(8,128)(2,1)S(1)} collective-permute-done((bf16[2,64,2048]{2,1,0:T(8,128)(2,1)}, bf16[2,64,2048]{2,1,0:T(8,128)(2,1)S(1)}, u32[]{:S(2)}, u32[]{:S(2)}) %collective-permute-start.20) | collective-permute-done | bytes 524320 | tf_op jit(solution)/shard_map/cond/branch_1_fun/ppermute | solution.py:583
  99.2 15.2 %branch_1_fun.7 = (bf16[512,2048]{1,0:T(8,128)(2,1)}, bf16[512,1024]{1,0:T(8,128)(2,1)S(1)}, bf16[512,1024]{1,0:T(8,128)(2,1)S(1)}) custom-call(bf16[512,1024]{1,0:T(8,128)(2,1)} %fusion.14.x_ref, bf16[1024,2048]{1,0:T(8,128)(2,1)} %bitcast.38.w_ref, f32[512,128]{1,0:T(8,128)S(1)} %get-tuple-element.737.cos_ref, f32[512,128]{1,0:T(8,128)S(1)} %get-tuple-element.738.sin_ref, ...), custom_call_target="tpu_custom_call" | custom-call | flops 1048576 | bytes 1048576 | tf_op jit(solution)/shard_map/cond/branch_1_fun/pallas_call | solution.py:85
  118.6 37.5 %collective-permute-done.23 = bf16[1,64,1024]{2,1,0:T(8,128)(2,1)S(1)} collective-permute-done((bf16[1,64,1024]{2,1,0:T(8,128)(2,1)S(1)}, bf16[1,64,1024]{2,1,0:T(8,128)(2,1)S(1)}, u32[]{:S(2)}, u32[]{:S(2)}) %collective-permute-start.23) | collective-permute-done | bytes 131104 | tf_op jit(solution)/shard_map/cond/branch_1_fun/ppermute | solution.py:583
  163.9 20.0 %branch_1_fun.8 = bf16[512,1024]{1,0:T(8,128)(2,1)S(1)} custom-call(s32[1]{0:T(128)} %get-tuple-element.246.part_ref, bf16[512,1024]{1,0:T(8,128)(2,1)S(1)} %get-tuple-element.731.q_ref, bf16[512,1024]{1,0:T(8,128)(2,1)S(1)} %get-tuple-element.732.own_ref, bf16[512,1024]{1,0:T(8,128)(2,1)S(1)} %collective-permute-done.27.peer_ref), custom_call_target="tpu_custom_call" | custom-call | flops 1048576 | bytes 1048576 | tf_op jit(solution)/shard_map/cond/branch_1_fun/pallas_call | solution.py:138
  195.4 10.1 %all-gather.3.cloned.1.call-done = bf16[110592,128]{1,0:T(8,128)(2,1)} async-done(((bf16[6912,128]{1,0:T(8,128)(2,1)}), bf16[110592,128]{1,0:T(8,128)(2,1)}) %all-gather.3.cloned.1.call-update) | async-done | bytes 28311568 | tf_op jit(solution)/shard_map/all_gather | solution.py:673
  205.5 25.6 %conditional.7 = ((bf16[512,1024]{1,0:T(8,128)(2,1)S(1)}, bf16[512,4608]{1,0:T(8,128)(2,1)}, bf16[512,4608]{1,0:T(8,128)(2,1)}, bf16[512,4608]{1,0:T(8,128)(2,1)})) conditional(s32[]{:T(128)} %convert_element_type.384, () %tuple.82, (bf16[512,1024]{1,0:T(8,128)(2,1)}, f32[512,1024]{1,0:T(8,128)}, bf16[16,6912,128]{2,1,0:T(8,128)(2,1)}) %tuple.170), branch_computations={%region_4.5_spmd, %region_5.6_spmd} | conditional | flops 1048576 | bytes 15204400 | solution.py:729
  205.7 25.4 %branch_1_fun.9 = (bf16[512,1024]{1,0:T(8,128)(2,1)S(1)}, bf16[512,4608]{1,0:T(8,128)(2,1)}, bf16[512,4608]{1,0:T(8,128)(2,1)}, bf16[512,4608]{1,0:T(8,128)(2,1)}) custom-call(bf16[512,1024]{1,0:T(8,128)(2,1)} %get-tuple-element.247.x_ref, f32[512,1024]{1,0:T(8,128)} %get-tuple-element.248.base_ref, ...), custom_call_target="tpu_custom_call" | custom-call | flops 1048576 | bytes 1048576 | tf_op jit(solution)/shard_map/cond/branch_1_fun/pallas_call | solution.py:454
  232.5 15.9 %collective-permute-done.42 = bf16[512,1024]{1,0:T(8,128)(2,1)S(1)} collective-permute-done((bf16[512,1024]{1,0:T(8,128)(2,1)S(1)}, bf16[512,1024]{1,0:T(8,128)(2,1)S(1)}, u32[]{:S(2)}, u32[]{:S(2)}) %collective-permute-start.42) | collective-permute-done | bytes 1048608 | tf_op jit(solution)/shard_map/ppermute | solution.py:730
  248.3 16.1 %conditional.8 = (f32[512,1024]{1,0:T(8,128)S(1)}, bf16[512,1024]{1,0:T(8,128)(2,1)}, bf16[512,1024]{1,0:T(8,128)(2,1)}, bf16[512,1024]{1,0:T(8,128)(2,1)}, bf16...) conditional(s32[]{:T(128)} %convert_element_type.384, ...), branch_computations={%region_6.16_spmd, %region_16.17_spmd} | conditional | flops 8648138752 | bytes 231228064 | solution.py:790
  264.4 75.6 %collective-permute-start.43 = (bf16[512,1024]{1,0:T(8,128)(2,1)}, bf16[512,1024]{1,0:T(8,128)(2,1)S(1)}, u32[]{:S(2)}, u32[]{:S(2)}) collective-permute-start(bf16[512,1024]{1,0:T(8,128)(2,1)} %get-tuple-element.507), channel_id=1, source_target_pairs={{0,16},{16,0},{1,17},{17,1},{2,18},{18,2},{3,19},{19,3},{4,20},{20... | collective-permute-start | bytes 3145736 | tf_op jit(solution)/shard_map/ppermute | solution.py:792
  351.0 12.6 %collective-permute-done.43 = bf16[512,1024]{1,0:T(8,128)(2,1)S(1)} collective-permute-done((bf16[512,1024]{1,0:T(8,128)(2,1)}, bf16[512,1024]{1,0:T(8,128)(2,1)S(1)}, u32[]{:S(2)}, u32[]{:S(2)}) %collective-permute-start.43) | collective-permute-done | bytes 1048608 | tf_op jit(solution)/shard_map/ppermute | solution.py:792
  386.9 54.9 %conditional.9 = (f32[512,1024]{1,0:T(8,128)}, bf16[4,64,4608]{2,1,0:T(8,128)(2,1)}, bf16[4,64,4608]{2,1,0:T(8,128)(2,1)}, bf16[512,4608]{1,0:T(8,128)(2,1)}, bf...) conditional(s32[]{:T(128)} %convert_element_type.391, ...), branch_computations={%region_17.18_spmd, %region_18.19_spmd} | conditional | flops 1086324736 | bytes 68682072 | solution.py:856
  387.3 36.8 %branch_1_fun.10 = (f32[512,1024]{1,0:T(8,128)}, bf16[512,4608]{1,0:T(8,128)(2,1)}, bf16[512,4608]{1,0:T(8,128)(2,1)}, bf16[512,4608]{1,0:T(8,128)(2,1)}, bf16[512,4608]{1,0:T(8,128)(2,1)}) custom-call(bf16[512,1024]{1,0:T(8,128)(2,1)} %get-tuple-element.279.grad_ref, bf16[1024,512]{1,0:T(8,128)(2,1)} %get-tuple-element.280.left_ref, ...), custom_call_target="tpu_custom_call" | custom-call | flops 1048576 | bytes 1048576 | tf_op jit(solution)/shard_map/cond/branch_1_fun/pallas_call | solution.py:512
  443.6 77.8 %conditional.10 = (bf16[4,288,1024]{2,1,0:T(8,128)(2,1)}, bf16[4,64,4608]{2,1,0:T(8,128)(2,1)}, bf16[4,64,4608]{2,1,0:T(8,128)(2,1)}, f32[1024]{0:T(1024)S(1)}, ...) conditional(s32[]{:T(128)} %convert_element_type.393, ...), branch_computations={%region_19.20_spmd, %region_20.24_spmd} | conditional | flops 1107295744 | bytes 122198512 | solution.py:897
  466.7 18.3 %branch_1_fun.11 = (f32[512,512]{1,0:T(8,128)}, f32[512,512]{1,0:T(8,128)}, bf16[512,512]{1,0:T(8,128)(2,1)}) custom-call(s32[1]{0:T(128)} %get-tuple-element.318.part_ref, bf16[512,1024]{1,0:T(8,128)(2,1)S(1)} %get-tuple-element.319.q_ref, bf16[512,1024]{1,0:T(8,128)(2,1)S(1)} %copy-done.13, bf16[512,1024]{1,0:T(8,128)(2,1)S(1)} %copy-done.15, ...), custom_call_target="tpu_custom_call" | custom-call | flops 1048576 | bytes 1048576 | tf_op jit(solution)/shard_map/cond/branch_1_fun/pallas_call | solution.py:197
  486.7 18.3 %branch_1_fun.12 = (f32[512,512]{1,0:T(8,128)}, f32[512,512]{1,0:T(8,128)}, bf16[512,512]{1,0:T(8,128)(2,1)}) custom-call(s32[1]{0:T(128)} %get-tuple-element.318.part_ref, bf16[512,1024]{1,0:T(8,128)(2,1)S(1)} %get-tuple-element.319.q_ref, bf16[512,1024]{1,0:T(8,128)(2,1)S(1)} %copy-done.13, bf16[512,1024]{1,0:T(8,128)(2,1)S(1)} %copy-done.15, ...), custom_call_target="tpu_custom_call" | custom-call | flops 1048576 | bytes 1048576 | tf_op jit(solution)/shard_map/cond/branch_1_fun/pallas_call | solution.py:197
  539.8 41.2 %conditional.11 = (bf16[4,64,2048]{2,1,0:T(8,128)(2,1)}, bf16[4,64,2048]{2,1,0:T(8,128)(2,1)S(1)}, bf16[4,64,1024]{2,1,0:T(8,128)(2,1)}, bf16[4,64,1024]{2,1,0:T...) conditional(s32[]{:T(128)} %convert_element_type.396, (bf16[512,512]{1,0:T(8,128)(2,1)}, ...), branch_computations={%region_24.25_spmd, %region_25.29_spmd} | conditional | flops 3238092288 | bytes 72654120 | solution.py:928
  540.7 19.0 %branch_1_fun.13 = (bf16[512,2048]{1,0:T(8,128)(2,1)}, f32[512,1024]{1,0:T(8,128)}, f32[8,128]{1,0:T(8,128)}) custom-call(bf16[512,2048]{1,0:T(8,128)(2,1)} %get-tuple-element.352.raw_ref, f32[512,1024]{1,0:T(8,128)S(1)} %get-tuple-element.353.dq_ref, f32[512,1024]{1,0:T(8,128)} %get-tuple-element.354.own_ref, ...), custom_call_target="tpu_custom_call" | custom-call | flops 1048576 | bytes 1048576 | tf_op jit(solution)/shard_map/cond/branch_1_fun/pallas_call | solution.py:252
  601.1 15.1 %collective-permute-done.51 = bf16[2,64,4608]{2,1,0:T(8,128)(2,1)} collective-permute-done((bf16[2,64,4608]{2,1,0:T(8,128)(2,1)}, bf16[2,64,4608]{2,1,0:T(8,128)(2,1)}, u32[]{:S(2)}, u32[]{:S(2)}) %collective-permute-start.51) | collective-permute-done | bytes 1179680 | tf_op jit(solution)/shard_map/ppermute | solution.py:586
  621.6 11.9 %collective-permute-done.55 = bf16[4,64,1024]{2,1,0:T(8,128)(2,1)S(1)} collective-permute-done((bf16[4,64,1024]{2,1,0:T(8,128)(2,1)}, bf16[4,64,1024]{2,1,0:T(8,128)(2,1)S(1)}, u32[]{:S(2)}, u32[]{:S(2)}) %collective-permute-start.55) | collective-permute-done | bytes 524320 | tf_op jit(solution)/shard_map/ppermute | solution.py:583
  651.0 12.2 %collective-permute-done.60 = bf16[2,64,1024]{2,1,0:T(8,128)(2,1)S(1)} collective-permute-done((bf16[2,64,1024]{2,1,0:T(8,128)(2,1)S(1)}, bf16[2,64,1024]{2,1,0:T(8,128)(2,1)S(1)}, u32[]{:S(2)}, u32[]{:S(2)}) %collective-permute-start.60) | collective-permute-done | bytes 262176 | tf_op jit(solution)/shard_map/ppermute | solution.py:586
  (313 shorter events, 282.5 us)
Async XLA Ops:
  7.2 198.3 %all-gather.3.cloned.1.call-start = ((), (), s32[]{:S(2)}) async-start(), calls=%async_computation.3 | async-start | bytes 30081024 | tf_op jit(solution)/shard_map/all_gather | solution.py:673
  37.5 19.5 %collective-permute-start.19 = (bf16[2,64,2048]{2,1,0:T(8,128)(2,1)}, bf16[2,64,2048]{2,1,0:T(8,128)(2,1)}, u32[]{:S(2)}, u32[]{:S(2)}) collective-permute-start(bf16[2,64,2048]{2,1,0:T(8,128)(2,1)} %pad_maximum_fusion.4), channel_id=1, source_target_pairs={{0,2},{1,3},{2,0},{3,1},{4,6},{5,7},{6,4},{7,5},{8,10},{9,11},{10,... | collective-permute-start | bytes 1572872 | tf_op jit(solution)/shard_map/cond/branch_1_fun/ppermute | solution.py:586
  39.0 19.6 %collective-permute-start.18 = (bf16[1,64,2048]{2,1,0:T(8,128)(2,1)}, bf16[1,64,2048]{2,1,0:T(8,128)(2,1)S(1)}, u32[]{:S(2)}, u32[]{:S(2)}) collective-permute-start(bf16[1,64,2048]{2,1,0:T(8,128)(2,1)} %copy-done.44), channel_id=1, source_target_pairs={{0,8},{8,0},{1,9},{9,1},{2,10},{10,2},{3,11},{11,3},{4,12},{12,4},... | collective-permute-start | bytes 786440 | tf_op jit(solution)/shard_map/cond/branch_1_fun/ppermute | solution.py:583
  114.5 49.4 %collective-permute-start.27 = (bf16[512,1024]{1,0:T(8,128)(2,1)S(1)}, bf16[512,1024]{1,0:T(8,128)(2,1)S(1)}, u32[]{:S(2)}, u32[]{:S(2)}) collective-permute-start(bf16[512,1024]{1,0:T(8,128)(2,1)S(1)} %get-tuple-element.732.own_ref), channel_id=1, source_target_pairs={{0,8},{8,0},{1,9},{9,1},{2,10},{10,2},{3,11},{11,3},{4,12},{12,4},... | collective-permute-start | bytes 3145736 | tf_op jit(solution)/shard_map/cond/branch_1_fun/ppermute | solution.py:583
  116.4 39.6 %collective-permute-start.23 = (bf16[1,64,1024]{2,1,0:T(8,128)(2,1)S(1)}, bf16[1,64,1024]{2,1,0:T(8,128)(2,1)S(1)}, u32[]{:S(2)}, u32[]{:S(2)}) collective-permute-start(bf16[1,64,1024]{2,1,0:T(8,128)(2,1)S(1)} %collective-permute-done.22), channel_id=1, source_target_pairs={{0,8},{8,0},{1,9},{9,1},{2,10},{10,2},{3,11},{11,3},{4,12},{12,4},... | collective-permute-start | bytes 393224 | tf_op jit(solution)/shard_map/cond/branch_1_fun/ppermute | solution.py:583
  116.6 47.1 %collective-permute-start.25 = (bf16[2,64,1024]{2,1,0:T(8,128)(2,1)S(1)}, bf16[2,64,1024]{2,1,0:T(8,128)(2,1)S(1)}, u32[]{:S(2)}, u32[]{:S(2)}) collective-permute-start(bf16[2,64,1024]{2,1,0:T(8,128)(2,1)S(1)} %collective-permute-done.24), channel_id=1, source_target_pairs={{0,8},{8,0},{1,9},{9,1},{2,10},{10,2},{3,11},{11,3},{4,12},{12,4},... | collective-permute-start | bytes 786440 | tf_op jit(solution)/shard_map/cond/branch_1_fun/ppermute | solution.py:583
  163.8 20.1 %collective-permute-start.26 = (bf16[4,2,64,1024]{3,2,1,0:T(8,128)(2,1)S(1)}, bf16[4,2,64,1024]{3,2,1,0:T(8,128)(2,1)S(1)}, u32[]{:S(2)}, u32[]{:S(2)}) collective-permute-start(bf16[4,2,64,1024]{3,2,1,0:T(8,128)(2,1)S(1)} %fusion.20), channel_id=1, source_target_pairs={{0,1},{1,0},{2,3},{3,2},{4,5},{5,4},{6,7},{7,6},{8,9},{9,8},{10,11... | collective-permute-start | bytes 3145736 | tf_op jit(solution)/shard_map/cond/branch_1_fun/ppermute | solution.py:580
  264.4 99.2 %collective-permute-start.43 = (bf16[512,1024]{1,0:T(8,128)(2,1)}, bf16[512,1024]{1,0:T(8,128)(2,1)S(1)}, u32[]{:S(2)}, u32[]{:S(2)}) collective-permute-start(bf16[512,1024]{1,0:T(8,128)(2,1)} %get-tuple-element.507), channel_id=1, source_target_pairs={{0,16},{16,0},{1,17},{17,1},{2,18},{18,2},{3,19},{19,3},{4,20},{20... | collective-permute-start | bytes 3145736 | tf_op jit(solution)/shard_map/ppermute | solution.py:792
  382.2 59.6 %collective-permute-start.46 = (bf16[4,288,512]{2,1,0:T(8,128)(2,1)}, bf16[4,288,512]{2,1,0:T(8,128)(2,1)}, u32[]{:S(2)}, u32[]{:S(2)}) collective-permute-start(bf16[4,288,512]{2,1,0:T(8,128)(2,1)} %get-tuple-element.509), channel_id=1, source_target_pairs={{0,8},{8,0},{1,9},{9,1},{2,10},{10,2},{3,11},{11,3},{4,12},{12,4},... | collective-permute-start | bytes 3538952 | tf_op jit(solution)/shard_map/ppermute | solution.py:583
  382.5 59.4 %collective-permute-start.47 = (bf16[4,288,512]{2,1,0:T(8,128)(2,1)}, bf16[4,288,512]{2,1,0:T(8,128)(2,1)}, u32[]{:S(2)}, u32[]{:S(2)}) collective-permute-start(bf16[4,288,512]{2,1,0:T(8,128)(2,1)} %get-tuple-element.510), channel_id=1, source_target_pairs={{0,8},{8,0},{1,9},{9,1},{2,10},{10,2},{3,11},{11,3},{4,12},{12,4},... | collective-permute-start | bytes 3538952 | tf_op jit(solution)/shard_map/ppermute | solution.py:583
  441.8 79.6 %collective-permute-start.48 = (bf16[4,64,4608]{2,1,0:T(8,128)(2,1)}, bf16[4,64,4608]{2,1,0:T(8,128)(2,1)}, u32[]{:S(2)}, u32[]{:S(2)}) collective-permute-start(bf16[4,64,4608]{2,1,0:T(8,128)(2,1)} %get-tuple-element.531), channel_id=1, source_target_pairs={{0,8},{8,0},{1,9},{9,1},{2,10},{10,2},{3,11},{11,3},{4,12},{12,4},... | collective-permute-start | bytes 7077896 | tf_op jit(solution)/shard_map/ppermute | solution.py:583
  442.2 79.3 %collective-permute-start.49 = (bf16[4,64,1024]{2,1,0:T(8,128)(2,1)}, bf16[4,64,1024]{2,1,0:T(8,128)(2,1)}, u32[]{:S(2)}, u32[]{:S(2)}) collective-permute-start(bf16[4,64,1024]{2,1,0:T(8,128)(2,1)} %get-tuple-element.532), channel_id=1, source_target_pairs={{16,24},{17,25},{18,26},{19,27},{20,28},{21,29},{22,30},{23,31},{2... | collective-permute-start | bytes 1572872 | tf_op jit(solution)/shard_map/ppermute | solution.py:646
  443.6 63.1 %collective-permute-start.33 = (bf16[512,4608]{1,0:T(8,128)(2,1)}, bf16[512,4608]{1,0:T(8,128)(2,1)}, u32[]{:S(2)}, u32[]{:S(2)}) collective-permute-start(bf16[512,4608]{1,0:T(8,128)(2,1)} %get-tuple-element.331), channel_id=1, source_target_pairs={{0,1},{1,0},{2,3},{3,2},{4,5},{5,4},{6,7},{7,6},{8,9},{9,8},{10,11... | collective-permute-start | bytes 14155784 | tf_op jit(solution)/shard_map/cond/branch_1_fun/ppermute | solution.py:580
  462.0 59.5 %all-to-all-start.1 = ((bf16[4,288,1024]{2,1,0:T(8,128)(2,1)}), bf16[4,288,1024]{2,1,0:T(8,128)(2,1)}, u32[]{:S(2)}, u32[]{:S(2)}) async-start(bf16[4,288,1024]{2,1,0:T(8,128)(2,1)} %pad_maximum_fusion.10), calls=%async_computation.1 | async-start | bytes 4718592 | tf_op jit(solution)/shard_map/cond/branch_1_fun/all_to_all | solution.py:808
  484.9 21.8 %collective-permute-start.32 = (bf16[512,512]{1,0:T(8,128)(2,1)}, bf16[512,512]{1,0:T(8,128)(2,1)}, u32[]{:S(2)}, u32[]{:S(2)}) collective-permute-start(bf16[512,512]{1,0:T(8,128)(2,1)} %get-tuple-element.326), channel_id=1, source_target_pairs={{0,8},{8,0},{1,9},{9,1},{2,10},{10,2},{3,11},{11,3},{4,12},{12,4},... | collective-permute-start | bytes 1572872 | tf_op jit(solution)/shard_map/cond/branch_1_fun/ppermute | solution.py:583
  526.3 58.6 %all-to-all-start.2 = ((bf16[4,64,4608]{2,1,0:T(8,128)(2,1)}), bf16[4,64,4608]{2,1,0:T(8,128)(2,1)}, u32[]{:S(2)}, u32[]{:S(2)}) async-start(bf16[4,64,4608]{2,1,0:T(8,128)(2,1)} %add_convert_fusion.13), calls=%async_computation.2 | async-start | bytes 4718592 | tf_op jit(solution)/shard_map/all_to_all | solution.py:808
  530.8 53.3 %collective-permute-start.50 = (bf16[4,64,4608]{2,1,0:T(8,128)(2,1)}, bf16[4,64,4608]{2,1,0:T(8,128)(2,1)}, u32[]{:S(2)}, u32[]{:S(2)}) collective-permute-start(bf16[4,64,4608]{2,1,0:T(8,128)(2,1)} %get-tuple-element.558), channel_id=1, source_target_pairs={{0,8},{8,0},{1,9},{9,1},{2,10},{10,2},{3,11},{11,3},{4,12},{12,4},... | collective-permute-start | bytes 7077896 | tf_op jit(solution)/shard_map/ppermute | solution.py:583
  588.9 27.3 %collective-permute-start.51 = (bf16[2,64,4608]{2,1,0:T(8,128)(2,1)}, bf16[2,64,4608]{2,1,0:T(8,128)(2,1)}, u32[]{:S(2)}, u32[]{:S(2)}) collective-permute-start(bf16[2,64,4608]{2,1,0:T(8,128)(2,1)} %dynamic-slice_bitcast_fusion.20), channel_id=1, source_target_pairs={{0,2},{1,3},{2,0},{3,1},{4,6},{5,7},{6,4},{7,5},{8,10},{9,11},{10,... | collective-permute-start | bytes 3538952 | tf_op jit(solution)/shard_map/ppermute | solution.py:586
  599.0 34.5 %collective-permute-start.54 = (bf16[4,64,2048]{2,1,0:T(8,128)(2,1)}, bf16[4,64,2048]{2,1,0:T(8,128)(2,1)S(1)}, u32[]{:S(2)}, u32[]{:S(2)}) collective-permute-start(bf16[4,64,2048]{2,1,0:T(8,128)(2,1)} %get-tuple-element.586), channel_id=1, source_target_pairs={{0,8},{8,0},{1,9},{9,1},{2,10},{10,2},{3,11},{11,3},{4,12},{12,4},... | collective-permute-start | bytes 3145736 | tf_op jit(solution)/shard_map/ppermute | solution.py:583
  599.3 34.2 %collective-permute-start.55 = (bf16[4,64,1024]{2,1,0:T(8,128)(2,1)}, bf16[4,64,1024]{2,1,0:T(8,128)(2,1)S(1)}, u32[]{:S(2)}, u32[]{:S(2)}) collective-permute-start(bf16[4,64,1024]{2,1,0:T(8,128)(2,1)} %get-tuple-element.587), channel_id=1, source_target_pairs={{0,8},{8,0},{1,9},{9,1},{2,10},{10,2},{3,11},{11,3},{4,12},{12,4},... | collective-permute-start | bytes 1572872 | tf_op jit(solution)/shard_map/ppermute | solution.py:583
  619.2 44.0 %collective-permute-start.57 = (bf16[1,64,4608]{2,1,0:T(8,128)(2,1)S(1)}, bf16[1,64,4608]{2,1,0:T(8,128)(2,1)S(1)}, u32[]{:S(2)}, u32[]{:S(2)}) collective-permute-start(bf16[1,64,4608]{2,1,0:T(8,128)(2,1)S(1)} %constant_dynamic-slice_fusion.8), channel_id=1, source_target_pairs={{0,4},{1,5},{2,6},{3,7},{4,0},{5,1},{6,2},{7,3},{8,12},{9,13},{10,... | collective-permute-start | bytes 1769480 | tf_op jit(solution)/shard_map/ppermute | solution.py:586
  634.0 29.2 %collective-permute-start.59 = (bf16[2,64,2048]{2,1,0:T(8,128)(2,1)S(1)}, bf16[2,64,2048]{2,1,0:T(8,128)(2,1)S(1)}, u32[]{:S(2)}, u32[]{:S(2)}) collective-permute-start(bf16[2,64,2048]{2,1,0:T(8,128)(2,1)S(1)} %dynamic-slice_bitcast_fusion.26), channel_id=1, source_target_pairs={{0,2},{1,3},{2,0},{3,1},{4,6},{5,7},{6,4},{7,5},{8,10},{9,11},{10,... | collective-permute-start | bytes 1572872 | tf_op jit(solution)/shard_map/ppermute | solution.py:586
  637.0 26.2 %collective-permute-start.60 = (bf16[2,64,1024]{2,1,0:T(8,128)(2,1)S(1)}, bf16[2,64,1024]{2,1,0:T(8,128)(2,1)S(1)}, u32[]{:S(2)}, u32[]{:S(2)}) collective-permute-start(bf16[2,64,1024]{2,1,0:T(8,128)(2,1)S(1)} %dynamic-slice_bitcast_fusion.27), channel_id=1, source_target_pairs={{0,2},{1,3},{2,0},{3,1},{4,6},{5,7},{6,4},{7,5},{8,10},{9,11},{10,... | collective-permute-start | bytes 786440 | tf_op jit(solution)/shard_map/ppermute | solution.py:586
  663.8 19.4 %collective-permute-start.62 = (bf16[1,64,2048]{2,1,0:T(8,128)(2,1)S(1)}, bf16[1,64,2048]{2,1,0:T(8,128)(2,1)S(1)}, u32[]{:S(2)}, u32[]{:S(2)}) collective-permute-start(bf16[1,64,2048]{2,1,0:T(8,128)(2,1)S(1)} %constant_dynamic-slice_fusion.6), channel_id=1, source_target_pairs={{0,4},{1,5},{2,6},{3,7},{4,0},{5,1},{6,2},{7,3},{8,12},{9,13},{10,... | collective-permute-start | bytes 786440 | tf_op jit(solution)/shard_map/ppermute | solution.py:586
  (62 other events, 884.0 us)
Sparse Core Ops, SparseCore 0:
  11.4 194.0 all-gather.2
